TPU v7x, 512 devices: a whole 4x4x16 slice. The times are simulated.
512 devices in a mesh: enc: 32 (over x, y, core), seq: 16 (over z).
Axes of the slice: x: 4, y: 4, z: 16, core: 2. Of those that a mesh axis runs over, the one named last changes fastest.
Arguments:
- tile_maps: bfloat16 [32, 256, 8, 8, 512], P('enc', 'seq'), may hold values from -6 to 6
- conv_weight: bfloat16 [4608, 512], P('enc'), may hold values from -0.15625 to 0.15625
- norm_gain: float32 [512], replicated, may hold values from 0.5 to 1.5
- norm_bias: float32 [512], replicated, may hold values from -3 to 3
- tile_proj: bfloat16 [512, 768], replicated, may hold values from -1 to 1
- positions: int32 [32, 256], P('enc'), may hold values from 0 to 4095, as said below
- slide_cache: bfloat16 [32, 4096, 768], P('enc', 'seq'), may hold values from -16 to 16
- project_in: bfloat16 [768, 2304], P(None, 'seq'), may hold values from -0.4375 to 0.4375
- project_out: bfloat16 [768, 768], replicated, may hold values from -0.21875 to 0.21875
- head_rates: int32 [16], replicated, may hold values from 1 to 8, as said below
Outputs:
- attended: bfloat16 [32, 4096, 768], P('enc', 'seq')
Inputs may be any that keep to these rules, and one draw needn't show every extreme that they name: Positions of one slide are distinct. Of the 16 tiles of one device (entries d * 16 to (d + 1) * 16 - 1), at most 2 lie in one block of 256 positions; in every slide one block receives exactly 2 from every device. `head_rates`: each of 1, 2, 4 and 8 is the rate of 4 heads.
All inputs are finite; a program needn't handle non-finite values.
Results may differ from a plain program's by a relative error of at most 0.017.
Values may be sent and summed in bfloat16 or wider, within the bound.
No kernel may reach another device: no remote copies, remote signals or barrier semaphores. Data moves between devices by JAX's collectives and lax.ppermute only.
A program may use at most 64 MiB of HBM per device.

v0:
```python
from functools import partial

import jax
import jax.numpy as jnp
from jax import lax
from jax.sharding import PartitionSpec as P

E = 768
HEADS = 16


def for_sending(shard):
    return jax.tree.map(lambda a: a.astype(jnp.bfloat16) if a.dtype == jnp.float32 else a, shard)


def dilated_head(query_rows, key_rows, value_rows, offset, dilation):
    length, head_feature_width = query_rows.shape
    block_len = length // 8
    offset = offset.astype(jnp.int32)

    def select(matrix):
        folded = matrix.reshape(length // dilation, dilation, head_feature_width)
        picked = lax.dynamic_slice_in_dim(folded, offset, 1, 1)
        return picked.reshape(length // dilation // block_len, block_len, head_feature_width)

    query_matrix = select(query_rows)
    selected_key_rows = select(key_rows)
    value_matrix = select(value_rows)
    score_matrix = jnp.einsum(
        "fnp,fjp->fnj", query_matrix, selected_key_rows, preferred_element_type=jnp.float32
    ) * head_feature_width ** (-0.5)
    row_max = jnp.max(score_matrix, axis=-1, keepdims=True)
    raised = jnp.exp(score_matrix - row_max)
    attention_weight = (raised / jnp.sum(raised, axis=-1, keepdims=True)).astype(jnp.bfloat16)
    mixed_output = jnp.einsum(
        "tln,tne->tle", attention_weight, value_matrix, preferred_element_type=jnp.float32
    ).astype(jnp.bfloat16)
    placed = jnp.zeros((length // dilation, dilation, head_feature_width), jnp.bfloat16)
    placed = lax.dynamic_update_slice_in_dim(
        placed, mixed_output.reshape(length // dilation, 1, head_feature_width), offset, 1
    )
    return placed.reshape(length, head_feature_width)


def shards(
    tile_maps,
    conv_weight,
    norm_gain,
    norm_bias,
    tile_proj,
    positions,
    slide_cache,
    project_in,
    project_out,
    head_rates,
):
    tile_count = tile_maps.shape[1]
    side_len = tile_maps.shape[2]
    channels = tile_maps.shape[4]
    images = tile_maps[0]
    padded = jnp.pad(images, ((0, 0), (1, 1), (1, 1), (0, 0)))
    columns = jnp.concatenate(
        [
            padded[:, row_shift : row_shift + side_len, col_shift : col_shift + side_len, :]
            for row_shift in range(3)
            for col_shift in range(3)
        ],
        axis=-1,
    )
    columns = columns.reshape(tile_count * side_len * side_len, 9 * channels)
    convolved = jnp.dot(
        columns,
        lax.all_gather(conv_weight, "enc", axis=0, tiled=True),
        preferred_element_type=jnp.float32,
    )
    activated = jnp.maximum(convolved * norm_gain + norm_bias, 0.0) + images.reshape(
        -1, channels
    ).astype(jnp.float32)
    pooled = jnp.mean(activated.reshape(tile_count, side_len * side_len, channels), axis=1).astype(
        jnp.bfloat16
    )
    embedded = jnp.dot(pooled, tile_proj, preferred_element_type=jnp.float32).astype(jnp.bfloat16)
    seq_count = lax.axis_size("seq")
    my_index = lax.axis_index("seq")
    local_len = slide_cache.shape[1]
    capacity = 2 * tile_count // seq_count
    slot_total = seq_count * capacity
    slide_list = positions[0]
    total_tiles = slide_list.shape[0]
    tile_order = jnp.arange(total_tiles)
    owners = slide_list // local_len
    sources = tile_order // tile_count
    same_bucket = (
        (owners[:, None] == owners[None, :])
        & (sources[:, None] == sources[None, :])
        & (tile_order[None, :] < tile_order[:, None])
    )
    bucket_rank = jnp.sum(same_bucket.astype(jnp.int32), axis=1)
    slot_ids = owners * capacity + bucket_rank
    my_slots = lax.dynamic_slice_in_dim(slot_ids, my_index * tile_count, tile_count)
    send_table = (my_slots[None, :] == jnp.arange(slot_total)[:, None]).astype(jnp.bfloat16)
    outgoing = jnp.dot(send_table, embedded, preferred_element_type=jnp.float32).astype(
        jnp.bfloat16
    )
    outgoing = outgoing.reshape(seq_count, capacity, embedded.shape[1])
    incoming = lax.all_to_all(outgoing, "seq", split_axis=0, concat_axis=0, tiled=True)
    arrival = sources * capacity + bucket_rank
    local_offset = slide_list - my_index * local_len
    landing = (
        (owners == my_index)[None, :] & (local_offset[None, :] == jnp.arange(local_len)[:, None])
    ).astype(jnp.bfloat16)
    arrive_table = (arrival[:, None] == jnp.arange(slot_total)[None, :]).astype(jnp.bfloat16)
    placement = jnp.dot(landing, arrive_table, preferred_element_type=jnp.float32).astype(
        jnp.bfloat16
    )
    new_rows = jnp.dot(
        placement, incoming.reshape(slot_total, -1), preferred_element_type=jnp.float32
    ).astype(jnp.bfloat16)
    covered = jnp.sum(landing.astype(jnp.float32), axis=1) > 0.5
    merged = jnp.where(covered[:, None], new_rows, slide_cache[0])
    head_feature_width = E // HEADS
    projections = jnp.dot(
        lax.all_gather(merged, "seq", axis=0, tiled=True),
        project_in,
        preferred_element_type=jnp.float32,
    ).astype(jnp.bfloat16)
    branches = [partial(dilated_head, dilation=factor) for factor in (1, 2, 4, 8)]
    local_heads = projections.shape[1] // (3 * head_feature_width)
    head_index = my_index * local_heads + 0
    dilation = head_rates[head_index]
    branch = (
        (dilation >= 2).astype(jnp.int32)
        + (dilation >= 4).astype(jnp.int32)
        + (dilation >= 8).astype(jnp.int32)
    )
    query_rows = projections[:, 0:head_feature_width]
    key_rows = projections[:, head_feature_width : 2 * head_feature_width]
    value_rows = projections[:, 2 * head_feature_width : 3 * head_feature_width]
    offset = head_index % dilation
    head_outputs = [lax.switch(branch, branches, query_rows, key_rows, value_rows, offset)]
    head_block = jnp.concatenate(head_outputs, axis=1)
    gathered = lax.all_to_all(
        for_sending(head_block), "seq", split_axis=0, concat_axis=1, tiled=True
    ).astype(head_block.dtype)
    output = jnp.dot(gathered, project_out, preferred_element_type=jnp.float32).astype(jnp.bfloat16)
    return output[None]


def solution(mesh):
    in_specs = (
        P("enc", "seq", None, None, None),
        P("enc", None),
        P(),
        P(),
        P(),
        P("enc", None),
        P("enc", "seq", None),
        P(None, "seq"),
        P(),
        P(),
    )
    out_specs = P("enc", "seq", None)
    return jax.shard_map(shards, mesh=mesh, in_specs=in_specs, out_specs=out_specs, check_vma=False)
```

profile of v0, /device:TPU:6, one launch (start us, length us, event | category | flops | bytes accessed | tf_op | source)
XLA Modules:
  0.0 287.9 jit_solution(13201481531376075311)
XLA Ops:
  9.8 5.1 %pad_slice_fusion = (bf16[16,8,8,512]{3,2,1,0:T(8,128)(2,1)S(1)}, bf16[16,8,8,512]{3,2,1,0:T(8,128)(2,1)S(1)}, bf16[16,8,8,512]{3,2,1,0:T(8,128)(2,1)S(1)}, bf16...) fusion(bf16[16,8,8,512]{3,2,1,0:T(8,128)(2,1)} %bitcast.105), kind=kLoop, calls=%fused_computation.72 | loop fusion | bytes 9437184 | tf_op jit(solution)/shard_map/slice | solution.py:64
  20.4 1.2 constant_dynamic-update-slice_fusion.3
  24.8 52.0 %all-gather.3.cloned.1.call-done = bf16[4608,512]{1,0:T(8,128)(2,1)} async-done(((bf16[144,512]{1,0:T(8,128)(2,1)}), bf16[4608,512]{1,0:T(8,128)(2,1)}) %all-gather.3.cloned.1.call-update) | async-done | bytes 4718608 | tf_op jit(solution)/shard_map/all_gather | solution.py:73
  76.7 9.2 %bitcast_reduce_fusion = f32[16,512]{1,0:T(8,128)S(1)} fusion(bf16[1024,512]{1,0:T(8,128)(2,1)S(1)} %bitcast.107, bf16[1024,4608]{1,0:T(8,128)(2,1)} %constant_dynamic-update-slice_fusion, bf16[4608,512]{1,0:T(8,128)(2,1)} %all-gather.3.cloned.1.call-done, f32[512]{0:T(512)S(1)} %copy-done.6, f32[512]{0:T(512)S(1)} %copy-done.7), kind=kOutput, calls=%fused_computation.81 | convolution fusion | flops 4834975744 | bytes 15241216 | tf_op jit(solution)/shard_map/dot_general | solution.py:71
  86.9 12.3 %all-to-all-start = ((bf16[16,2,768]{2,1,0:T(2,128)(2,1)}), bf16[16,2,768]{2,1,0:T(2,128)(2,1)S(1)}, u32[]{:S(2)}, u32[]{:S(2)}) async-start(bf16[16,2,768]{2,1,0:T(2,128)(2,1)} %reshape.294), calls=%async_computation | async-start | bytes 98304 | tf_op jit(solution)/shard_map/all_to_all | solution.py:106
  99.3 12.6 %all-to-all-done = bf16[16,2,768]{2,1,0:T(2,128)(2,1)S(1)} async-done(((bf16[16,2,768]{2,1,0:T(2,128)(2,1)}), bf16[16,2,768]{2,1,0:T(2,128)(2,1)S(1)}, u32[]{:S(2)}, u32[]{:S(2)}) %all-to-all-start) | async-done | bytes 49184 | tf_op jit(solution)/shard_map/all_to_all | solution.py:106
  111.9 2.3 fusion.89
  116.5 74.4 %all-gather.5.cloned.1.call-done = bf16[4096,768]{1,0:T(8,128)(2,1)} async-done(((bf16[256,768]{1,0:T(8,128)(2,1)}), bf16[4096,768]{1,0:T(8,128)(2,1)}) %all-gather.5.cloned.1.call-update) | async-done | bytes 6291472 | tf_op jit(solution)/shard_map/all_gather | solution.py:123
  190.9 4.9 %convolution_convert_fusion.2 = bf16[4096,144]{0,1:T(8,128)(2,1)S(1)} fusion(bf16[4096,768]{1,0:T(8,128)(2,1)} %all-gather.5.cloned.1.call-done, bf16[768,144]{0,1:T(8,128)(2,1)S(1)} %copy-done.5), kind=kOutput, calls=%fused_computation.80 | convolution fusion | flops 906559488 | bytes 7692288 | tf_op jit(solution)/shard_map/dot_general | solution.py:122
  196.0 51.2 %conditional.1 = (bf16[4096,48]{1,0:T(8,128)(2,1)}) conditional(s32[]{:T(128)} %clamp.3, (bf16[4096,48]{0,1:T(8,128)(2,1)S(1)}, bf16[4096,48]{0,1:T(8,128)(2,1)S(1)}, bf16[4096,48]{0,1:T(8,128)(2,1)S(1)}) %tuple.39, (bf16[4096,48]{0,1:T(8,128)(2,1)S(1)}, s32[]{:T(128)}, s32[]{:T(128)}, ...), branch_computations={%region_3.6_spmd, %region_6.9_spmd, %region_9.12_spmd, %region_12.... | conditional | flops 413336064 | bytes 19169288 | solution.py:140
  197.3 1.4 copy.171
  198.7 1.3 copy.172
  200.0 4.2 %constant_dynamic-slice_fusion = (bf16[2048,1,48]{2,1,0:T(2,128)(2,1)S(1)}, bf16[2048,1,48]{2,1,0:T(2,128)(2,1)}) fusion(bf16[2048,2,48]{2,1,0:T(2,128)(2,1)} %bitcast.117, s32[]{:T(128)S(6)} %select_n.91, bf16[2048,2,48]{2,1,0:T(2,128)(2,1)} %bitcast.116), kind=kLoop, calls=%fused_computation.36 | loop fusion | bytes 786436 | tf_op jit(solution)/shard_map/cond/branch_1_fun/dynamic_slice | solution.py:23
  204.2 2.3 copy.194
  206.6 1.3 copy.170
  208.0 3.0 %constant_dynamic-slice_fusion.2 = bf16[2048,1,48]{2,1,0:T(2,128)(2,1)} fusion(bf16[2048,2,48]{2,1,0:T(2,128)(2,1)} %bitcast.118, s32[]{:T(128)S(6)} %select_n.91), kind=kLoop, calls=%fused_computation.38 | loop fusion | bytes 393220 | tf_op jit(solution)/shard_map/cond/branch_1_fun/dynamic_slice | solution.py:23
  210.9 2.3 copy.193
  213.3 3.5 %fusion.116 = (f32[4,512]{1,0:T(4,128)S(1)}, f32[4,512,512]{1,2,0:T(8,128)}) fusion(bf16[4,512,48]{1,0,2:T(4,128)(2,1)S(1)} %reshape.269, bf16[4,512,48]{1,0,2:T(4,128)(2,1)S(1)} %reshape.267), kind=kOutput, calls=%fused_computation.133 | convolution fusion | flops 103809536 | bytes 4595712 | tf_op jit(solution)/shard_map/cond/branch_1_fun/sub | solution.py:33
  217.6 2.6 fusion.37
  220.7 1.4 broadcast.187
  222.1 25.0 %dynamic_update_slice.16 = bf16[2048,2,48]{2,1,0:T(2,128)(2,1)} dynamic-update-slice(bf16[2048,2,48]{2,1,0:T(2,128)(2,1)} %broadcast.187, bf16[2048,1,48]{2,1,0:T(2,128)(2,1)S(1)} %reshape.296, s32[]{:T(128)} %constant.132.clone, s32[]{:T(128)S(6)} %select_n.91, s32[]{:T(128)} %constant.132.clone) | dynamic-update-slice | bytes 393220 | tf_op jit(solution)/shard_map/cond/branch_1_fun/dynamic_update_slice | solution.py:39
  247.2 1.5 copy.180
  248.7 31.1 %all_to_all.24 = bf16[16,256,48]{1,2,0:T(8,128)(2,1)S(1)} all-to-all(bf16[16,256,48]{1,2,0:T(8,128)(2,1)S(1)} %copy.180), channel_id=1, replica_groups=mesh['enc'=32,'seq'=16] {'seq'}, dimensions={0} | all-to-all | bytes 786432 | tf_op jit(solution)/shard_map/all_to_all | solution.py:142
  279.8 1.3 fusion.90
  (45 shorter events, 15.2 us)
Async XLA Ops:
  6.5 273.2 %copy-start = (bf16[768,768]{1,0:T(8,128)(2,1)S(1)}, bf16[768,768]{1,0:T(8,128)(2,1)}, u32[]{:S(2)}) copy-start(bf16[768,768]{1,0:T(8,128)(2,1)} %param.22) | copy-start | bytes 3538948
  6.5 70.2 %all-gather.3.cloned.1.call-start = ((), (), s32[]{:S(2)}) async-start(), calls=%async_computation.2 | async-start | bytes 4866048 | tf_op jit(solution)/shard_map/all_gather | solution.py:73
  14.9 4.4 %copy-start.1 = (bf16[1,16,8,8,512]{4,3,2,1,0:T(8,128)(2,1)S(1)}, bf16[1,16,8,8,512]{4,3,2,1,0:T(8,128)(2,1)}, u32[]{:S(2)}) copy-start(bf16[1,16,8,8,512]{4,3,2,1,0:T(8,128)(2,1)} %param.14) | copy-start | bytes 3145732
  20.4 56.3 %copy-start.6 = (f32[512]{0:T(512)S(1)}, f32[512]{0:T(512)}, u32[]{:S(2)}) copy-start(f32[512]{0:T(512)} %param.17) | copy-start | bytes 6148
  20.4 56.3 %copy-start.7 = (f32[512]{0:T(512)S(1)}, f32[512]{0:T(512)}, u32[]{:S(2)}) copy-start(f32[512]{0:T(512)} %param.16) | copy-start | bytes 6148
  24.8 61.2 %copy-start.4 = (bf16[512,768]{1,0:T(8,128)(2,1)S(1)}, bf16[512,768]{1,0:T(8,128)(2,1)}, u32[]{:S(2)}) copy-start(bf16[512,768]{1,0:T(8,128)(2,1)} %param.18) | copy-start | bytes 2359300
  24.8 89.5 %copy-start.8 = (s32[16]{0:T(128)S(1)}, s32[16]{0:T(128)}, u32[]{:S(2)}) copy-start(s32[16]{0:T(128)} %param.23) | copy-start | bytes 196
  24.8 166.2 %copy-start.5 = (bf16[768,144]{0,1:T(8,128)(2,1)S(1)}, bf16[768,144]{0,1:T(8,128)(2,1)}, u32[]{:S(2)}) copy-start(bf16[768,144]{0,1:T(8,128)(2,1)} %param.21) | copy-start | bytes 663556
  86.9 24.9 %all-to-all-start = ((bf16[16,2,768]{2,1,0:T(2,128)(2,1)}), bf16[16,2,768]{2,1,0:T(2,128)(2,1)S(1)}, u32[]{:S(2)}, u32[]{:S(2)}) async-start(bf16[16,2,768]{2,1,0:T(2,128)(2,1)} %reshape.294), calls=%async_computation | async-start | bytes 98304 | tf_op jit(solution)/shard_map/all_to_all | solution.py:106
  99.2 91.7 %all-gather.5.cloned.1.call-start = ((), (), s32[]{:S(2)}) async-start(), calls=%async_computation.3 | async-start | bytes 6684672 | tf_op jit(solution)/shard_map/all_gather | solution.py:123
Sparse Core Ops, SparseCore 0:
  10.5 66.1 all-gather.2
  114.4 76.5 all-gather.4
where the time goes:
time: 291 us; the launch traced here: 288 us
  waiting for transfers between devices  140 us (48%)
  local copies, waits for them, and re-layouts  61.6 us (21%)
  blocking collectives  31.1 us (11%)
  matrix products  24.2 us (8%)
  between operations  15.2 us (5%)
  starting transfers between devices  12.3 us (4%)
    all_gather x1, waiting for transfers between devices, shards(): lax.all_gather(merged, 'seq', axis=0, tiled=True)  74.4 us
    all_gather x1, waiting for transfers between devices, shards(): lax.all_gather(conv_weight, 'enc', axis=0, tiled=True)  52 us
    all_to_all x1, blocking collectives, shards(): lax.all_to_all(for_sending(head_block), 'seq', split_axis=0, concat_axis=...  31.1 us
    dynamic_update_slice x1, local copies, waits for them, and re-layouts, dilated_head(): lax.dynamic_update_slice_in_dim(placed, mixed_output.reshape(length // di...  25 us
    all_to_all x1, waiting for transfers between devices, shards(): lax.all_to_all(outgoing, 'seq', split_axis=0, concat_axis=0, tiled=True)  12.6 us
    all_to_all x1, starting transfers between devices, shards(): lax.all_to_all(outgoing, 'seq', split_axis=0, concat_axis=0, tiled=True)  12.3 us
    dot_general x1, matrix products, shards(): jnp.dot(columns, lax.all_gather(conv_weight, 'enc', axis=0, tiled=True),...  9.19 us
    unnamed x22, local copies, waits for them, and re-layouts  8.86 us
  transfers between devices with their start and end apart: 3, of which 3 were waited for; matrix products, arithmetic and copies ran while one was open for 6% of the time, Pallas kernels for 0%

commit v1 on v0

v1 whole, which is shorter than its diff:
```python
from functools import partial

import jax
import jax.numpy as jnp
from jax import lax
from jax.experimental import pallas as pl
from jax.experimental.pallas import tpu as pltpu
from jax.sharding import PartitionSpec as P

E = 768
HEADS = 16
WIDTH = E // HEADS
SEGMENT = 512
STEP_ROWS = 512


def attend(rate, offset, table, out_ref):
    length = table.shape[1]
    loc = out_ref.shape[2]
    spread = None
    if rate > 1:
        source = lax.broadcasted_iota(jnp.int32, (128, 128 * rate), 0)
        target = lax.broadcasted_iota(jnp.int32, (128, 128 * rate), 1)
        spread = (target == offset + rate * source).astype(jnp.float32).astype(jnp.bfloat16)
    lane = lax.broadcasted_iota(jnp.int32, (SEGMENT, 128), 1)

    def segment(index, carry):
        start = index * (SEGMENT * rate) + offset
        if rate == 1:
            start = pl.multiple_of(index * SEGMENT, SEGMENT)
            rows = pl.ds(start, SEGMENT)
        else:
            rows = pl.ds(start, SEGMENT, stride=rate)
        query_value = table[0, rows, :]
        keys = table[1, rows, :].astype(jnp.bfloat16)
        with_ones = jnp.where(lane == 112, 1.0, query_value).astype(jnp.bfloat16)
        query_value = query_value.astype(jnp.bfloat16)
        for part in range(SEGMENT // 256):
            queries = query_value[part * 256 : (part + 1) * 256]
            scores = lax.dot_general(
                keys, queries, (((1,), (1,)), ((), ())), preferred_element_type=jnp.float32
            )
            top = jnp.max(scores, axis=0, keepdims=True)
            raised = jnp.exp((scores - top) * WIDTH**-0.5).astype(jnp.bfloat16)
            mixed = lax.dot_general(
                with_ones, raised, (((0,), (0,)), ((), ())), preferred_element_type=jnp.float32
            )
            result = (mixed[64:112] / mixed[112:113]).astype(jnp.bfloat16)
            if rate == 1:
                out_ref[index * (SEGMENT // loc) + part] = result
            else:
                for half in range(2):
                    wide = jnp.dot(
                        result[:, half * 128 : (half + 1) * 128],
                        spread,
                        preferred_element_type=jnp.float32,
                    ).astype(jnp.bfloat16)
                    blocks = 128 * rate // loc
                    first = (index * 4 + part * 2 + half) * blocks
                    for block in range(blocks):
                        out_ref[first + block] = wide[:, block * loc : (block + 1) * loc]
        return carry

    lax.fori_loop(0, length // (SEGMENT * rate), segment, 0)


def head_kernel(places, choice, rows_ref, fresh_ref, weight_ref, out_ref, table, fresh):
    step = pl.program_id(0)
    made = jnp.dot(rows_ref[...], weight_ref[...], preferred_element_type=jnp.float32)
    made = made.astype(jnp.bfloat16).astype(jnp.float32)
    block = pl.ds(pl.multiple_of(step * STEP_ROWS, STEP_ROWS), STEP_ROWS)
    table[0, block, :] = made[:, :128]
    table[1, block, :] = made[:, 128:]

    @pl.when(step == pl.num_programs(0) - 1)
    def _():
        made_fresh = jnp.dot(fresh_ref[...], weight_ref[...], preferred_element_type=jnp.float32)
        made_fresh = made_fresh.astype(jnp.bfloat16).astype(jnp.float32)
        fresh[0] = made_fresh[:, :128]
        fresh[1] = made_fresh[:, 128:]

        def place(group, carry):
            for inner in range(8):
                tile = group * 8 + inner
                where = places[tile]
                for side in range(2):
                    table[side, pl.ds(where, 1), :] = fresh[side, pl.ds(tile, 1), :]
            return carry

        lax.fori_loop(0, fresh.shape[1] // 8, place, 0)
        for rate in (1, 2, 4, 8):
            pl.when(choice[0] == rate)(partial(attend, rate, choice[1], table, out_ref))


def head_attention(places, choice, rows, fresh, weight, seq_count):
    length = rows.shape[0]
    loc = length // seq_count
    return pl.pallas_call(
        head_kernel,
        out_shape=jax.ShapeDtypeStruct((seq_count, WIDTH, loc), jnp.bfloat16),
        grid_spec=pltpu.PrefetchScalarGridSpec(
            num_scalar_prefetch=2,
            grid=(length // STEP_ROWS,),
            in_specs=[
                pl.BlockSpec((STEP_ROWS, E), lambda i, *_: (i, 0)),
                pl.BlockSpec(fresh.shape, lambda i, *_: (0, 0)),
                pl.BlockSpec(weight.shape, lambda i, *_: (0, 0)),
            ],
            out_specs=pl.BlockSpec((seq_count, WIDTH, loc), lambda i, *_: (0, 0, 0)),
            scratch_shapes=[
                pltpu.VMEM((2, length, 128), jnp.float32),
                pltpu.VMEM((2, fresh.shape[0], 128), jnp.float32),
            ],
        ),
        compiler_params=pltpu.CompilerParams(
            dimension_semantics=("arbitrary",), vmem_limit_bytes=40 * 1024 * 1024
        ),
        cost_estimate=pl.CostEstimate(
            flops=2 * length * E * 256, bytes_accessed=rows.size * 2, transcendentals=length * SEGMENT
        ),
    )(places, choice, rows, fresh, weight)


def spread_to(shard, axis, count, groups=None):
    copies = jnp.broadcast_to(shard[None], (count,) + shard.shape)
    return lax.all_to_all(
        copies, axis, split_axis=0, concat_axis=0, tiled=True, axis_index_groups=groups
    )


def whole_weight(conv_weight):
    enc_count = lax.axis_size("enc")
    chips = enc_count // 2
    groups = [[2 * chip + core for chip in range(chips)] for core in range(2)]
    own = spread_to(conv_weight, "enc", chips, groups)
    other = lax.ppermute(own, "enc", [(e, e ^ 1) for e in range(enc_count)])
    first_core = lax.axis_index("enc") % 2 == 0
    even = jnp.where(first_core, own, other)
    odd = jnp.where(first_core, other, own)
    return jnp.stack([even, odd], axis=1).reshape(-1, conv_weight.shape[1])


def shards(
    tile_maps,
    conv_weight,
    norm_gain,
    norm_bias,
    tile_proj,
    positions,
    slide_cache,
    project_in,
    project_out,
    head_rates,
):
    tile_count = tile_maps.shape[1]
    side_len = tile_maps.shape[2]
    channels = tile_maps.shape[4]
    seq_count = lax.axis_size("seq")
    my_index = lax.axis_index("seq")

    with jax.named_scope("rows"):
        rows = lax.all_gather(slide_cache[0], "seq", axis=0, tiled=True)

    with jax.named_scope("encode"):
        images = tile_maps[0]
        padded = jnp.pad(images, ((0, 0), (1, 1), (1, 1), (0, 0)))
        columns = jnp.concatenate(
            [
                padded[:, row_shift : row_shift + side_len, col_shift : col_shift + side_len, :]
                for row_shift in range(3)
                for col_shift in range(3)
            ],
            axis=-1,
        )
        columns = columns.reshape(tile_count * side_len * side_len, 9 * channels)
        convolved = jnp.dot(columns, whole_weight(conv_weight), preferred_element_type=jnp.float32)
        activated = jnp.maximum(convolved * norm_gain + norm_bias, 0.0) + images.reshape(
            -1, channels
        ).astype(jnp.float32)
        pooled = jnp.mean(
            activated.reshape(tile_count, side_len * side_len, channels), axis=1
        ).astype(jnp.bfloat16)
        embedded = jnp.dot(pooled, tile_proj, preferred_element_type=jnp.float32).astype(
            jnp.bfloat16
        )

    with jax.named_scope("fresh"):
        fresh = spread_to(embedded, "seq", seq_count).reshape(-1, E)

    with jax.named_scope("head"):
        gap = jnp.zeros((E, 16), jnp.bfloat16)
        end = jnp.zeros((E, 80), jnp.bfloat16)
        queries, keys, values = jnp.split(project_in, 3, axis=1)
        weight = jnp.concatenate([queries, gap, values, gap, keys, end], axis=1)
        rate = head_rates[my_index]
        choice = jnp.stack([rate, my_index % rate]).astype(jnp.int32)
        head_out = head_attention(positions[0], choice, rows, fresh, weight, seq_count)

    with jax.named_scope("out"):
        gathered = lax.all_to_all(head_out, "seq", split_axis=0, concat_axis=0, tiled=True)
        gathered = gathered.reshape(E, -1)
        output = lax.dot_general(
            gathered, project_out, (((0,), (0,)), ((), ())), preferred_element_type=jnp.float32
        ).astype(jnp.bfloat16)
    return output[None]


def solution(mesh):
    in_specs = (
        P("enc", "seq", None, None, None),
        P("enc", None),
        P(),
        P(),
        P(),
        P("enc", None),
        P("enc", "seq", None),
        P(None, "seq"),
        P(),
        P(),
    )
    out_specs = P("enc", "seq", None)
    return jax.shard_map(shards, mesh=mesh, in_specs=in_specs, out_specs=out_specs, check_vma=False)
```

time: 291 us -> 169 us (0.58)
  waiting for transfers between devices: 140 us -> 30.7 us
  local copies, waits for them, and re-layouts: 61.6 us -> 18.5 us
  blocking collectives: 31.1 us -> 64.3 us
  matrix products: 24.2 us -> 6.7 us
  Pallas kernels: 0 us -> 12.3 us
  starting transfers between devices: 12.3 us -> 17.4 us
    all_gather x2 -> x1, waiting for transfers between devices: 126 us -> 6.02 us  [shards(): rows = lax.all_gather(slide_cache[0], 'seq', axis=0, tiled=True)]
    all_to_all x1 -> x2, blocking collectives: 31.1 us -> 64.3 us  [the longest x1 36.1 us: spread_to(): lax.all_to_all(copies, axis, split_axis=0, concat_axis=0, tiled=True, axi...]
    dynamic_update_slice x1 -> x0, local copies, waits for them, and re-layouts: 25 us -> none  [dilated_head(): lax.dynamic_update_slice_in_dim(placed, mixed_output.reshape(length // di...]
    dot_general x6 -> x3, matrix products: 20.7 us -> 6.7 us  [the longest x1 5.23 us: shards(): jnp.dot(columns, whole_weight(conv_weight), preferred_element_type=jnp.fl...]
    pallas_call x0 -> x1, Pallas kernels: none -> 12.3 us  [head_attention(): pl.pallas_call(head_kernel, out_shape=jax.ShapeDtypeStruct((seq_count, WI...]
    all_to_all x1, waiting for transfers between devices: 12.6 us -> 24 us  [spread_to(): lax.all_to_all(copies, axis, split_axis=0, concat_axis=0, tiled=True, axi...]
    dynamic_slice x4 -> x1, local copies, waits for them, and re-layouts: 7.79 us -> 0.62 us  [shards(): rate = head_rates[my_index]]
    another operation x4 -> x0, local copies, waits for them, and re-layouts: 5.42 us -> none
  transfers between devices with their start and end apart: 3 -> 3, of which waited for: 3 -> 2; matrix products, arithmetic and copies ran while one was open for 6% -> 11% of each run, Pallas kernels for 0% -> 0%
where the time goes in v1:
time: 169 us; the launch traced here: 168 us
  blocking collectives  64.3 us (38%)
  waiting for transfers between devices  30.7 us (18%)
  local copies, waits for them, and re-layouts  18.5 us (11%)
  starting transfers between devices  17.4 us (10%)
  between operations  15 us (9%)
  Pallas kernels  12.3 us (7%)
  matrix products  6.7 us (4%)
  other arithmetic  3.28 us (2%)
    all_to_all x1, blocking collectives, spread_to(): lax.all_to_all(copies, axis, split_axis=0, concat_axis=0, tiled=True, axi...  36.1 us
    all_to_all x1, blocking collectives, shards(): lax.all_to_all(head_out, 'seq', split_axis=0, concat_axis=0, tiled=True)  28.2 us
    all_to_all x1, waiting for transfers between devices, spread_to(): lax.all_to_all(copies, axis, split_axis=0, concat_axis=0, tiled=True, axi...  24 us
    all_to_all x1, starting transfers between devices, spread_to(): lax.all_to_all(copies, axis, split_axis=0, concat_axis=0, tiled=True, axi...  15.5 us
    pallas_call x1, Pallas kernels, head_attention(): pl.pallas_call(head_kernel, out_shape=jax.ShapeDtypeStruct((seq_count, WI...  12.3 us
    unnamed x37, local copies, waits for them, and re-layouts  10.6 us
    all_gather x1, waiting for transfers between devices, shards(): rows = lax.all_gather(slide_cache[0], 'seq', axis=0, tiled=True)  6.02 us
    dot_general x1, matrix products, shards(): jnp.dot(columns, whole_weight(conv_weight), preferred_element_type=jnp.fl...  5.23 us
  transfers between devices with their start and end apart: 3, of which 2 were waited for; matrix products, arithmetic and copies ran while one was open for 11% of the time, Pallas kernels for 0%

profile of v1, /device:TPU:6, one launch (start us, length us, event | category | flops | bytes accessed | tf_op | source)
XLA Modules:
  0.0 168.2 jit_solution(3651980850466481538)
XLA Ops:
  6.5 0.7 all-gather.3.cloned.1.call-update
  7.3 1.1 broadcast_in_dim.10
  8.4 36.1 %all_to_all.15 = bf16[16,144,512]{2,1,0:T(8,128)(2,1)S(1)} all-to-all(bf16[16,144,512]{2,1,0:T(8,128)(2,1)S(1)} %broadcast_in_dim.10), channel_id=1, replica_groups={{0,32,64,96,128,160,192,224,256,288,320,352,384,416,448,480},{16,48,80,..., dimensions={0} | all-to-all | bytes 4718592 | tf_op jit(solution)/shard_map/encode/all_to_all | solution.py:126
  44.5 1.9 %collective-permute-start = (bf16[16,144,512]{2,1,0:T(8,128)(2,1)S(1)}, bf16[16,144,512]{2,1,0:T(8,128)(2,1)}, u32[]{:S(2)}, u32[]{:S(2)}) collective-permute-start(bf16[16,144,512]{2,1,0:T(8,128)(2,1)S(1)} %all_to_all.15), channel_id=1, source_target_pairs={{0,16},{16,0},{32,48},{48,32},{64,80},{80,64},{96,112},{112,96},{1... | collective-permute-start | bytes 7077896 | tf_op jit(solution)/shard_map/encode/ppermute | solution.py:136
  46.4 4.7 %pad_slice_fusion = (bf16[16,8,8,512]{3,2,1,0:T(8,128)(2,1)S(1)}, bf16[16,8,8,512]{3,2,1,0:T(8,128)(2,1)S(1)}, bf16[16,8,8,512]{3,2,1,0:T(8,128)(2,1)S(1)}, bf16...) fusion(bf16[16,8,8,512]{3,2,1,0:T(8,128)(2,1)} %bitcast.36), kind=kLoop, calls=%fused_computation | loop fusion | bytes 9437184 | tf_op jit(solution)/shard_map/encode/slice | solution.py:169
  51.4 0.9 copy-done.3
  52.7 3.7 %copy-done.6 = bf16[1024,4608]{1,0:T(8,128)(2,1)} copy-done((bf16[1024,4608]{1,0:T(8,128)(2,1)}, bf16[1024,4608]{1,0:T(8,128)(2,1)S(1)}, u32[]{:S(2)}) %copy-start.6) | copy-done | bytes 9437208
  56.4 2.1 %select_bitcast_fusion.1 = (bf16[16,1,144,512]{3,2,1,0:T(8,128)(2,1)S(1)}, bf16[16,1,144,512]{3,2,1,0:T(8,128)(2,1)S(1)}) fusion(bf16[16,144,512]{2,1,0:T(8,128)(2,1)S(1)} %all_to_all.15, bf16[16,144,512]{2,1,0:T(8,128)(2,1)} %collective-permute-done, pred[]{:T(512)S(6)} %eq.10), kind=kLoop, calls=%fused_computation.10 | loop fusion | flops 2359296 | bytes 9437185 | tf_op jit(solution)/shard_map/encode/stack | solution.py:140
  58.6 0.4 pad_maximum_fusion
  59.0 0.3 slice-done
  59.4 1.4 slice-done.1
  60.7 0.4 slice-done.2
  61.2 5.2 %bitcast_reduce_fusion = f32[16,512]{1,0:T(8,128)S(1)} fusion(bf16[1024,512]{1,0:T(8,128)(2,1)S(1)} %bitcast.38, bf16[1024,4608]{1,0:T(8,128)(2,1)S(1)} %bitcast.49, bf16[4608,512]{1,0:T(8,128)(2,1)S(1)} %bitcast.35, f32[512]{0:T(512)S(1)} %copy-done.7, f32[512]{0:T(512)S(1)} %copy-done.8), kind=kOutput, calls=%fused_computation.11 | convolution fusion | flops 4834975744 | bytes 15241216 | tf_op jit(solution)/shard_map/encode/dot_general | solution.py:176
  66.7 0.8 broadcast_in_dim.11
  67.5 15.5 %all-to-all-start.1 = ((bf16[16,16,768]{2,1,0:T(8,128)(2,1)}), bf16[16,16,768]{2,1,0:T(8,128)(2,1)S(1)}, u32[]{:S(2)}, u32[]{:S(2)}) async-start(bf16[16,16,768]{2,1,0:T(8,128)(2,1)} %broadcast_in_dim.11), calls=%async_computation.1 | async-start | bytes 786432 | tf_op jit(solution)/shard_map/fresh/all_to_all | solution.py:126
  83.0 0.6 dynamic_slice.3
  85.5 0.5 concatenate.35.weight_ref
  86.1 0.7 pad_add_fusion.choice
  86.8 24.0 %all-to-all-done.1 = bf16[16,16,768]{2,1,0:T(8,128)(2,1)S(1)} async-done(((bf16[16,16,768]{2,1,0:T(8,128)(2,1)}), bf16[16,16,768]{2,1,0:T(8,128)(2,1)S(1)}, u32[]{:S(2)}, u32[]{:S(2)}) %all-to-all-start.1) | async-done | bytes 393248 | tf_op jit(solution)/shard_map/fresh/all_to_all | solution.py:126
  110.7 6.0 %all-gather.3.cloned.1.call-done = bf16[1,4096,768]{2,1,0:T(8,128)(2,1)} async-done(((bf16[1,256,768]{2,1,0:T(8,128)(2,1)}), bf16[1,4096,768]{2,1,0:T(8,128)(2,1)}) %all-gather.3.cloned.1.call-update) | async-done | bytes 6291472 | tf_op jit(solution)/shard_map/rows/all_gather | solution.py:162
  116.8 2.8 %copy-done.1 = bf16[1,4096,768]{2,1,0:T(8,128)(2,1)S(1)} copy-done((bf16[1,4096,768]{2,1,0:T(8,128)(2,1)S(1)}, bf16[1,4096,768]{2,1,0:T(8,128)(2,1)}, u32[]{:S(2)}) %copy-start.1) | copy-done | bytes 6291480
  119.6 12.3 %head.1 = bf16[16,48,256]{2,1,0:T(8,128)(2,1)S(1)} custom-call(s32[256]{0:T(256)S(1)} %bitcast.34, s32[2]{0:T(128)S(1)} %pad_add_fusion.choice, bf16[4096,768]{1,0:T(8,128)(2,1)S(1)} %bitcast.32, bf16[256,768]{1,0:T(8,128)(2,1)S(1)} %bitcast.33, bf16[768,256]{1,0:T(8,128)(2,1)S(1)} %concatenate.35.weight_ref), custom_call_target="tpu_custom_call" | custom-call | flops 1610612736 | bytes 6291456 | tf_op jit(solution)/shard_map/head/pallas_call | solution.py:98
  131.8 28.2 %all_to_all.16 = bf16[16,48,256]{2,1,0:T(8,128)(2,1)S(1)} all-to-all(bf16[16,48,256]{2,1,0:T(8,128)(2,1)S(1)} %head.1), channel_id=1, replica_groups=mesh['enc'=32,'seq'=16] {'seq'}, dimensions={0} | all-to-all | bytes 786432 | tf_op jit(solution)/shard_map/out/all_to_all | solution.py:200
  160.1 1.3 fusion
  (39 shorter events, 1.5 us)
Async XLA Ops:
  6.5 153.5 %copy-start = (bf16[768,768]{1,0:T(8,128)(2,1)S(1)}, bf16[768,768]{1,0:T(8,128)(2,1)}, u32[]{:S(2)}) copy-start(bf16[768,768]{1,0:T(8,128)(2,1)} %param.18) | copy-start | bytes 3538948
  6.5 110.2 %all-gather.3.cloned.1.call-start = ((), (), s32[]{:S(2)}) async-start(), calls=%async_computation.3 | async-start | bytes 6684672 | tf_op jit(solution)/shard_map/rows/all_gather | solution.py:162
  44.5 11.9 %collective-permute-start = (bf16[16,144,512]{2,1,0:T(8,128)(2,1)S(1)}, bf16[16,144,512]{2,1,0:T(8,128)(2,1)}, u32[]{:S(2)}, u32[]{:S(2)}) collective-permute-start(bf16[16,144,512]{2,1,0:T(8,128)(2,1)S(1)} %all_to_all.15), channel_id=1, source_target_pairs={{0,16},{16,0},{32,48},{48,32},{64,80},{80,64},{96,112},{112,96},{1... | collective-permute-start | bytes 7077896 | tf_op jit(solution)/shard_map/encode/ppermute | solution.py:136
  51.1 1.2 copy-start.3
  52.7 3.7 %copy-start.6 = (bf16[1024,4608]{1,0:T(8,128)(2,1)}, bf16[1024,4608]{1,0:T(8,128)(2,1)S(1)}, u32[]{:S(2)}) copy-start(bf16[1024,4608]{1,0:T(8,128)(2,1)S(1)} %constant_dynamic-update-slice_fusion) | copy-start | bytes 28311556
  56.4 3.0 %slice-start = ((s8[9437184]{0:T(1024)(128)(4,1)}), s8[4194304]{0:T(1024)(128)(4,1)S(1)}, s32[]{:S(2)}) async-start(s8[9437184]{0:T(1024)(128)(4,1)} %bitcast.48), calls=%async_computation.4 | async-start | bytes 8388608
  56.4 4.3 %slice-start.1 = ((s8[9437184]{0:T(1024)(128)(4,1)}), s8[4194304]{0:T(1024)(128)(4,1)S(1)}, s32[]{:S(2)}) async-start(s8[9437184]{0:T(1024)(128)(4,1)} %bitcast.48), calls=%async_computation.5 | async-start | bytes 8388608
  58.6 2.6 %slice-start.2 = ((s8[9437184]{0:T(1024)(128)(4,1)}), s8[1048576]{0:T(1024)(128)(4,1)S(1)}, s32[]{:S(2)}) async-start(s8[9437184]{0:T(1024)(128)(4,1)} %bitcast.48), calls=%async_computation.6 | async-start | bytes 2097152
  58.6 2.6 %copy-start.7 = (f32[512]{0:T(512)S(1)}, f32[512]{0:T(512)}, u32[]{:S(2)}) copy-start(f32[512]{0:T(512)} %param.13) | copy-start | bytes 6148
  58.6 2.6 %copy-start.8 = (f32[512]{0:T(512)S(1)}, f32[512]{0:T(512)}, u32[]{:S(2)}) copy-start(f32[512]{0:T(512)} %param.12) | copy-start | bytes 6148
  61.2 5.3 %copy-start.4 = (bf16[512,768]{1,0:T(8,128)(2,1)S(1)}, bf16[512,768]{1,0:T(8,128)(2,1)}, u32[]{:S(2)}) copy-start(bf16[512,768]{1,0:T(8,128)(2,1)} %param.14) | copy-start | bytes 2359300
  61.2 21.8 %copy-start.9 = (s32[16]{0:T(128)S(1)}, s32[16]{0:T(128)}, u32[]{:S(2)}) copy-start(s32[16]{0:T(128)} %param.19) | copy-start | bytes 196
  61.2 23.7 %copy-start.5 = (bf16[768,144]{0,1:T(8,128)(2,1)S(1)}, bf16[768,144]{0,1:T(8,128)(2,1)}, u32[]{:S(2)}) copy-start(bf16[768,144]{0,1:T(8,128)(2,1)} %param.17) | copy-start | bytes 663556
  66.4 50.3 %copy-start.2 = (s32[1,256]{1,0:T(1,128)S(1)}, s32[1,256]{1,0:T(1,128)}, u32[]{:S(2)}) copy-start(s32[1,256]{1,0:T(1,128)} %param.15) | copy-start | bytes 3076
  67.5 43.3 %all-to-all-start.1 = ((bf16[16,16,768]{2,1,0:T(8,128)(2,1)}), bf16[16,16,768]{2,1,0:T(8,128)(2,1)S(1)}, u32[]{:S(2)}, u32[]{:S(2)}) async-start(bf16[16,16,768]{2,1,0:T(8,128)(2,1)} %broadcast_in_dim.11), calls=%async_computation.1 | async-start | bytes 786432 | tf_op jit(solution)/shard_map/fresh/all_to_all | solution.py:126
  116.8 2.8 %copy-start.1 = (bf16[1,4096,768]{2,1,0:T(8,128)(2,1)S(1)}, bf16[1,4096,768]{2,1,0:T(8,128)(2,1)}, u32[]{:S(2)}) copy-start(bf16[1,4096,768]{2,1,0:T(8,128)(2,1)} %all-gather.3.cloned.1.call-done) | copy-start | bytes 18874372
Sparse Core Ops, SparseCore 0:
  9.4 107.2 all-gather.2

commit v2 on v1

--- a/solution.py
+++ b/solution.py
@@ -113,7 +113,7 @@
             ],
         ),
         compiler_params=pltpu.CompilerParams(
-            dimension_semantics=("arbitrary",), vmem_limit_bytes=40 * 1024 * 1024
+            dimension_semantics=("arbitrary",), vmem_limit_bytes=58 * 1024 * 1024
         ),
         cost_estimate=pl.CostEstimate(
             flops=2 * length * E * 256, bytes_accessed=rows.size * 2, transcendentals=length * SEGMENT
@@ -128,16 +128,17 @@
     )
 
 
-def whole_weight(conv_weight):
+def whole_weight(conv_weight, ready):
     enc_count = lax.axis_size("enc")
     chips = enc_count // 2
     groups = [[2 * chip + core for chip in range(chips)] for core in range(2)]
     own = spread_to(conv_weight, "enc", chips, groups)
+    own, ready = lax.optimization_barrier((own, ready))
     other = lax.ppermute(own, "enc", [(e, e ^ 1) for e in range(enc_count)])
     first_core = lax.axis_index("enc") % 2 == 0
     even = jnp.where(first_core, own, other)
     odd = jnp.where(first_core, other, own)
-    return jnp.stack([even, odd], axis=1).reshape(-1, conv_weight.shape[1])
+    return jnp.stack([even, odd], axis=1).reshape(-1, conv_weight.shape[1]), ready
 
 
 def shards(
@@ -173,7 +174,8 @@
             axis=-1,
         )
         columns = columns.reshape(tile_count * side_len * side_len, 9 * channels)
-        convolved = jnp.dot(columns, whole_weight(conv_weight), preferred_element_type=jnp.float32)
+        weight, columns = whole_weight(conv_weight, columns)
+        convolved = jnp.dot(columns, weight, preferred_element_type=jnp.float32)
         activated = jnp.maximum(convolved * norm_gain + norm_bias, 0.0) + images.reshape(
             -1, channels
         ).astype(jnp.float32)
@@ -185,7 +187,7 @@
         )
 
     with jax.named_scope("fresh"):
-        fresh = spread_to(embedded, "seq", seq_count).reshape(-1, E)
+        fresh = lax.all_gather(embedded, "seq", axis=0, tiled=True)
 
     with jax.named_scope("head"):
         gap = jnp.zeros((E, 16), jnp.bfloat16)

time: 169 us -> 169 us (level)
  the two profiles are of different devices: /device:TPU:6 before, /device:TPU:32 now
where the time goes in v2:
time: 169 us
  blocking collectives  72 us (43%)
  local copies, waits for them, and re-layouts  29.6 us (18%)
  waiting for transfers between devices  19.1 us (11%)
  between operations  14.8 us (9%)
  Pallas kernels  11.2 us (7%)
  matrix products  9.38 us (6%)
  starting transfers between devices  8.95 us (5%)
  other arithmetic  3.62 us (2%)
    all_gather x1, blocking collectives, shards(): fresh = lax.all_gather(embedded, 'seq', axis=0, tiled=True)  38.7 us
    all_to_all x1, blocking collectives, shards(): lax.all_to_all(head_out, 'seq', split_axis=0, concat_axis=0, tiled=True)  33.3 us
    all_to_all x1, waiting for transfers between devices, spread_to(): lax.all_to_all(copies, axis, split_axis=0, concat_axis=0, tiled=True, axi...  18.4 us
    unnamed x25, local copies, waits for them, and re-layouts  14.7 us
    pallas_call x1, Pallas kernels, head_attention(): pl.pallas_call(head_kernel, out_shape=jax.ShapeDtypeStruct((seq_count, WI...  11.2 us
    dot_general x1, matrix products, shards(): convolved = jnp.dot(columns, weight, preferred_element_type=jnp.float32)  7.91 us
    all_to_all x1, starting transfers between devices, spread_to(): lax.all_to_all(copies, axis, split_axis=0, concat_axis=0, tiled=True, axi...  7.03 us
    slice x1, local copies, waits for them, and re-layouts, shards(): padded[:, row_shift:row_shift + side_len, col_shift:col_shift + side_len, :]  5.35 us
  transfers between devices with their start and end apart: 3, of which 1 were waited for; matrix products, arithmetic and copies ran while one was open for 24% of the time, Pallas kernels for 0%

profile of v2, /device:TPU:32, one launch (start us, length us, event | category | flops | bytes accessed | tf_op | source)
XLA Modules:
  0.0 168.7 jit_solution(16979493382491925778)
XLA Ops:
  7.3 2.5 %broadcast_in_dim.8 = bf16[16,144,512]{2,1,0:T(8,128)(2,1)} broadcast(bf16[144,512]{1,0:T(8,128)(2,1)} %param.11), dimensions={1,2} | broadcast | bytes 2506752 | tf_op jit(solution)/shard_map/encode/broadcast_in_dim | solution.py:125
  9.8 7.0 %all-to-all-start = ((bf16[16,144,512]{2,1,0:T(8,128)(2,1)}), bf16[16,144,512]{2,1,0:T(8,128)(2,1)S(1)}, u32[]{:S(2)}, u32[]{:S(2)}) async-start(bf16[16,144,512]{2,1,0:T(8,128)(2,1)} %broadcast_in_dim.8), calls=%async_computation | async-start | bytes 4718592 | tf_op jit(solution)/shard_map/encode/all_to_all | solution.py:126
  16.8 5.3 %pad_slice_fusion = (bf16[16,8,8,512]{3,2,1,0:T(8,128)(2,1)S(1)}, bf16[16,8,8,512]{3,2,1,0:T(8,128)(2,1)S(1)}, bf16[16,8,8,512]{3,2,1,0:T(8,128)(2,1)S(1)}, bf16...) fusion(bf16[16,8,8,512]{3,2,1,0:T(8,128)(2,1)} %bitcast.33), kind=kLoop, calls=%fused_computation | loop fusion | bytes 9437184 | tf_op jit(solution)/shard_map/encode/slice | solution.py:170
  22.2 1.1 constant_dynamic-update-slice_fusion.8
  23.3 1.1 constant_dynamic-update-slice_fusion.7
  24.4 1.1 constant_dynamic-update-slice_fusion.6
  25.5 1.1 constant_dynamic-update-slice_fusion.5
  26.6 1.2 constant_dynamic-update-slice_fusion.4
  28.9 1.1 constant_dynamic-update-slice_fusion.2
  31.0 1.1 constant_dynamic-update-slice_fusion
  32.1 18.4 %all-to-all-done = bf16[16,144,512]{2,1,0:T(8,128)(2,1)S(1)} async-done(((bf16[16,144,512]{2,1,0:T(8,128)(2,1)}), bf16[16,144,512]{2,1,0:T(8,128)(2,1)S(1)}, u32[]{:S(2)}, u32[]{:S(2)}) %all-to-all-start) | async-done | bytes 2359328 | tf_op jit(solution)/shard_map/encode/all_to_all | solution.py:126
  50.5 1.9 %collective-permute-start = (bf16[16,144,512]{2,1,0:T(8,128)(2,1)S(1)}, bf16[16,144,512]{2,1,0:T(8,128)(2,1)}, u32[]{:S(2)}, u32[]{:S(2)}) collective-permute-start(bf16[16,144,512]{2,1,0:T(8,128)(2,1)S(1)} %all-to-all-done), channel_id=1, source_target_pairs={{0,16},{16,0},{32,48},{48,32},{64,80},{80,64},{96,112},{112,96},{1... | collective-permute-start | bytes 7077896 | tf_op jit(solution)/shard_map/encode/ppermute | solution.py:137
  54.3 1.6 fusion.3
  56.0 1.7 %copy.18 = bf16[768,48]{1,0:T(8,128)(2,1)} copy(bf16[768,48]{0,1:T(8,128)(2,1)} %get-tuple-element.21) | data formatting | bytes 147456
  57.7 1.7 copy.19
  59.4 1.7 %copy.20 = bf16[768,48]{1,0:T(8,128)(2,1)} copy(bf16[768,48]{0,1:T(8,128)(2,1)} %get-tuple-element.19) | data formatting | bytes 147456
  62.5 2.3 %concatenate.35.weight_ref = bf16[768,256]{1,0:T(8,128)(2,1)} concatenate(bf16[768,48]{1,0:T(8,128)(2,1)} %copy.18, bf16[768,16]{1,0:T(8,128)(2,1)} %broadcast_in_dim.18, bf16[768,48]{1,0:T(8,128)(2,1)} %copy.19, bf16[768,16]{1,0:T(8,128)(2,1)} %broadcast_in_dim.18, bf16[768,48]{1,0:T(8,128)(2,1)} %copy.20, bf16[768,80]{1,0:T(8,128)(2,1)} %broadcast_in_dim.19), dimensions={1} | concatenate | bytes 786432 | tf_op jit(solution)/shard_map/head/concatenate | solution.py:196
  64.7 1.2 pad_add_fusion.choice
  65.9 2.0 %select_bitcast_fusion.1 = (bf16[16,1,144,512]{3,2,1,0:T(8,128)(2,1)S(1)}, bf16[16,1,144,512]{3,2,1,0:T(8,128)(2,1)S(1)}) fusion(bf16[16,144,512]{2,1,0:T(8,128)(2,1)S(1)} %all-to-all-done, bf16[16,144,512]{2,1,0:T(8,128)(2,1)} %collective-permute-done, pred[]{:T(512)S(6)} %eq.10), kind=kLoop, calls=%fused_computation.10 | loop fusion | flops 2359296 | bytes 9437185 | tf_op jit(solution)/shard_map/encode/stack | solution.py:141
  69.2 7.9 %bitcast_reduce_fusion = f32[16,512]{1,0:T(8,128)S(1)} fusion(bf16[1024,512]{1,0:T(8,128)(2,1)S(1)} %bitcast.35, bf16[1024,4608]{1,0:T(8,128)(2,1)} %constant_dynamic-update-slice_fusion, bf16[4608,512]{1,0:T(8,128)(2,1)S(1)} %bitcast.32, f32[512]{0:T(512)S(1)} %copy-done.4, f32[512]{0:T(512)S(1)} %copy-done.5), kind=kOutput, calls=%fused_computation.11 | convolution fusion | flops 4834975744 | bytes 15241216 | tf_op jit(solution)/shard_map/encode/dot_general | solution.py:178
  77.3 38.7 %all_gather.7.fresh_ref = bf16[256,768]{1,0:T(8,128)(2,1)} all-gather(bf16[16,768]{1,0:T(8,128)(2,1)S(1)} %convolution_convert_fusion.1), channel_id=1, replica_groups=mesh['enc'=32,'seq'=16] {'seq'}, dimensions={0}, use_global_device_ids=true | all-gather | bytes 417792 | tf_op jit(solution)/shard_map/fresh/all_gather | solution.py:190
  116.0 11.2 %head.1 = bf16[16,48,256]{2,1,0:T(8,128)(2,1)} custom-call(s32[256]{0:T(256)} %bitcast.45, s32[2]{0:T(128)} %pad_add_fusion.choice, bf16[4096,768]{1,0:T(8,128)(2,1)} %bitcast.31, bf16[256,768]{1,0:T(8,128)(2,1)} %all_gather.7.fresh_ref, bf16[768,256]{1,0:T(8,128)(2,1)} %concatenate.35.weight_ref), custom_call_target="tpu_custom_call" | custom-call | flops 1610612736 | bytes 6291456 | tf_op jit(solution)/shard_map/head/pallas_call | solution.py:98
  127.3 33.3 %all_to_all.10 = bf16[16,48,256]{2,1,0:T(8,128)(2,1)S(1)} all-to-all(bf16[16,48,256]{2,1,0:T(8,128)(2,1)} %head.1), channel_id=1, replica_groups=mesh['enc'=32,'seq'=16] {'seq'}, dimensions={0} | all-to-all | bytes 786432 | tf_op jit(solution)/shard_map/out/all_to_all | solution.py:202
  160.6 1.3 fusion
  (25 shorter events, 6.3 us)
Async XLA Ops:
  6.5 154.0 %copy-start = (bf16[768,768]{1,0:T(8,128)(2,1)S(1)}, bf16[768,768]{1,0:T(8,128)(2,1)}, u32[]{:S(2)}) copy-start(bf16[768,768]{1,0:T(8,128)(2,1)} %param.18) | copy-start | bytes 3538948
  6.5 109.5 %all-gather.3.cloned.1.call-start = ((), (), s32[]{:S(2)}) async-start(), calls=%async_computation.2 | async-start | bytes 6684672 | tf_op jit(solution)/shard_map/rows/all_gather | solution.py:163
  9.8 40.7 %all-to-all-start = ((bf16[16,144,512]{2,1,0:T(8,128)(2,1)}), bf16[16,144,512]{2,1,0:T(8,128)(2,1)S(1)}, u32[]{:S(2)}, u32[]{:S(2)}) async-start(bf16[16,144,512]{2,1,0:T(8,128)(2,1)} %broadcast_in_dim.8), calls=%async_computation | async-start | bytes 4718592 | tf_op jit(solution)/shard_map/encode/all_to_all | solution.py:126
  22.2 4.4 %copy-start.1 = (bf16[1,16,8,8,512]{4,3,2,1,0:T(8,128)(2,1)S(1)}, bf16[1,16,8,8,512]{4,3,2,1,0:T(8,128)(2,1)}, u32[]{:S(2)}) copy-start(bf16[1,16,8,8,512]{4,3,2,1,0:T(8,128)(2,1)} %param.10) | copy-start | bytes 3145732
  27.8 24.6 %copy-start.6 = (s32[16]{0:T(128)S(1)}, s32[16]{0:T(128)}, u32[]{:S(2)}) copy-start(s32[16]{0:T(128)} %param.19) | copy-start | bytes 196
  50.5 15.4 %collective-permute-start = (bf16[16,144,512]{2,1,0:T(8,128)(2,1)S(1)}, bf16[16,144,512]{2,1,0:T(8,128)(2,1)}, u32[]{:S(2)}, u32[]{:S(2)}) collective-permute-start(bf16[16,144,512]{2,1,0:T(8,128)(2,1)S(1)} %all-to-all-done), channel_id=1, source_target_pairs={{0,16},{16,0},{32,48},{48,32},{64,80},{80,64},{96,112},{112,96},{1... | collective-permute-start | bytes 7077896 | tf_op jit(solution)/shard_map/encode/ppermute | solution.py:137
  67.9 1.2 copy-start.2
  67.9 1.2 copy-start.4
  67.9 1.2 copy-start.5
  69.2 7.9 %copy-start.3 = (bf16[512,768]{1,0:T(8,128)(2,1)S(1)}, bf16[512,768]{1,0:T(8,128)(2,1)}, u32[]{:S(2)}) copy-start(bf16[512,768]{1,0:T(8,128)(2,1)} %param.14) | copy-start | bytes 2359300
Sparse Core Ops, SparseCore 0:
  9.4 91.5 all-gather.2

commit v3 on v2

--- a/solution.py
+++ b/solution.py
@@ -113,7 +113,7 @@
             ],
         ),
         compiler_params=pltpu.CompilerParams(
-            dimension_semantics=("arbitrary",), vmem_limit_bytes=58 * 1024 * 1024
+            dimension_semantics=("arbitrary",), vmem_limit_bytes=24 * 1024 * 1024
         ),
         cost_estimate=pl.CostEstimate(
             flops=2 * length * E * 256, bytes_accessed=rows.size * 2, transcendentals=length * SEGMENT
@@ -162,6 +162,14 @@
     with jax.named_scope("rows"):
         rows = lax.all_gather(slide_cache[0], "seq", axis=0, tiled=True)
 
+    with jax.named_scope("choice"):
+        gap = jnp.zeros((E, 16), jnp.bfloat16)
+        end = jnp.zeros((E, 80), jnp.bfloat16)
+        queries, keys, values = jnp.split(project_in, 3, axis=1)
+        head_weight = jnp.concatenate([queries, gap, values, gap, keys, end], axis=1)
+        rate = head_rates[my_index]
+        choice = jnp.stack([rate, my_index % rate]).astype(jnp.int32)
+
     with jax.named_scope("encode"):
         images = tile_maps[0]
         padded = jnp.pad(images, ((0, 0), (1, 1), (1, 1), (0, 0)))
@@ -174,7 +182,9 @@
             axis=-1,
         )
         columns = columns.reshape(tile_count * side_len * side_len, 9 * channels)
-        weight, columns = whole_weight(conv_weight, columns)
+        weight, (columns, head_weight, choice) = whole_weight(
+            conv_weight, (columns, head_weight, choice)
+        )
         convolved = jnp.dot(columns, weight, preferred_element_type=jnp.float32)
         activated = jnp.maximum(convolved * norm_gain + norm_bias, 0.0) + images.reshape(
             -1, channels
@@ -190,13 +200,7 @@
         fresh = lax.all_gather(embedded, "seq", axis=0, tiled=True)
 
     with jax.named_scope("head"):
-        gap = jnp.zeros((E, 16), jnp.bfloat16)
-        end = jnp.zeros((E, 80), jnp.bfloat16)
-        queries, keys, values = jnp.split(project_in, 3, axis=1)
-        weight = jnp.concatenate([queries, gap, values, gap, keys, end], axis=1)
-        rate = head_rates[my_index]
-        choice = jnp.stack([rate, my_index % rate]).astype(jnp.int32)
-        head_out = head_attention(positions[0], choice, rows, fresh, weight, seq_count)
+        head_out = head_attention(positions[0], choice, rows, fresh, head_weight, seq_count)
 
     with jax.named_scope("out"):
         gathered = lax.all_to_all(head_out, "seq", split_axis=0, concat_axis=0, tiled=True)

time: 169 us -> 157 us (0.929)
  the two profiles are of different devices: /device:TPU:32 before, /device:TPU:6 now
where the time goes in v3:
time: 157 us; the launch traced here: 156 us
  blocking collectives  69.3 us (44%)
  local copies, waits for them, and re-layouts  20.4 us (13%)
  waiting for transfers between devices  16.7 us (11%)
  between operations  14.8 us (9%)
  starting transfers between devices  12 us (8%)
  Pallas kernels  9.56 us (6%)
  matrix products  9.36 us (6%)
  other arithmetic  3.85 us (2%)
    all_gather x1, blocking collectives, shards(): fresh = lax.all_gather(embedded, 'seq', axis=0, tiled=True)  40.4 us
    all_to_all x1, blocking collectives, shards(): lax.all_to_all(head_out, 'seq', split_axis=0, concat_axis=0, tiled=True)  28.8 us
    unnamed x29, local copies, waits for them, and re-layouts  13 us
    all_to_all x1, waiting for transfers between devices, spread_to(): lax.all_to_all(copies, axis, split_axis=0, concat_axis=0, tiled=True, axi...  11.1 us
    all_to_all x1, starting transfers between devices, spread_to(): lax.all_to_all(copies, axis, split_axis=0, concat_axis=0, tiled=True, axi...  10.1 us
    pallas_call x1, Pallas kernels, head_attention(): pl.pallas_call(head_kernel, out_shape=jax.ShapeDtypeStruct((seq_count, WI...  9.56 us
    dot_general x1, matrix products, shards(): convolved = jnp.dot(columns, weight, preferred_element_type=jnp.float32)  7.9 us
    ppermute x1, waiting for transfers between devices, whole_weight(): other = lax.ppermute(own, 'enc', [(e, e ^ 1) for e in range(enc_count)])  4.83 us
  transfers between devices with their start and end apart: 3, of which 2 were waited for; matrix products, arithmetic and copies ran while one was open for 19% of the time, Pallas kernels for 0%

profile of v3, /device:TPU:6, one launch (start us, length us, event | category | flops | bytes accessed | tf_op | source)
XLA Modules:
  0.0 155.9 jit_solution(15981336940997492379)
XLA Ops:
  7.3 2.6 %broadcast_in_dim.8 = bf16[16,144,512]{2,1,0:T(8,128)(2,1)} broadcast(bf16[144,512]{1,0:T(8,128)(2,1)} %param.11), dimensions={1,2} | broadcast | bytes 2506752 | tf_op jit(solution)/shard_map/encode/broadcast_in_dim | solution.py:125
  9.9 10.1 %all-to-all-start = ((bf16[16,144,512]{2,1,0:T(8,128)(2,1)}), bf16[16,144,512]{2,1,0:T(8,128)(2,1)}, u32[]{:S(2)}, u32[]{:S(2)}) async-start(bf16[16,144,512]{2,1,0:T(8,128)(2,1)} %broadcast_in_dim.8), calls=%async_computation | async-start | bytes 4718592 | tf_op jit(solution)/shard_map/encode/all_to_all | solution.py:126
  22.3 0.8 copy.20
  23.2 1.4 concatenate.35.weight_ref
  25.3 1.6 %pad_slice_fusion = (bf16[16,8,8,512]{3,2,1,0:T(8,128)(2,1)S(1)}, bf16[16,8,8,512]{3,2,1,0:T(8,128)(2,1)S(1)}, bf16[16,8,8,512]{3,2,1,0:T(8,128)(2,1)S(1)}, bf16...) fusion(bf16[16,8,8,512]{3,2,1,0:T(8,128)(2,1)S(1)} %bitcast.34), kind=kLoop, calls=%fused_computation | loop fusion | bytes 9437184 | tf_op jit(solution)/shard_map/encode/slice | solution.py:178
  26.9 1.2 constant_dynamic-update-slice_fusion.8
  28.1 1.1 constant_dynamic-update-slice_fusion.7
  29.1 1.1 constant_dynamic-update-slice_fusion.6
  30.2 1.1 constant_dynamic-update-slice_fusion.5
  31.3 1.1 constant_dynamic-update-slice_fusion.4
  32.4 1.1 constant_dynamic-update-slice_fusion.3
  33.5 1.1 constant_dynamic-update-slice_fusion.2
  34.5 1.1 constant_dynamic-update-slice_fusion.1
  35.7 1.1 constant_dynamic-update-slice_fusion
  36.8 11.1 %all-to-all-done = bf16[16,144,512]{2,1,0:T(8,128)(2,1)} async-done(((bf16[16,144,512]{2,1,0:T(8,128)(2,1)}), bf16[16,144,512]{2,1,0:T(8,128)(2,1)}, u32[]{:S(2)}, u32[]{:S(2)}) %all-to-all-start) | async-done | bytes 2359328 | tf_op jit(solution)/shard_map/encode/all_to_all | solution.py:126
  47.9 1.9 %collective-permute-start = (bf16[16,144,512]{2,1,0:T(8,128)(2,1)}, bf16[16,144,512]{2,1,0:T(8,128)(2,1)}, u32[]{:S(2)}, u32[]{:S(2)}) collective-permute-start(bf16[16,144,512]{2,1,0:T(8,128)(2,1)} %all-to-all-done), channel_id=1, source_target_pairs={{0,16},{16,0},{32,48},{48,32},{64,80},{80,64},{96,112},{112,96},{1... | collective-permute-start | bytes 7077896 | tf_op jit(solution)/shard_map/encode/ppermute | solution.py:137
  49.8 4.8 %collective-permute-done = bf16[16,144,512]{2,1,0:T(8,128)(2,1)} collective-permute-done((bf16[16,144,512]{2,1,0:T(8,128)(2,1)}, bf16[16,144,512]{2,1,0:T(8,128)(2,1)}, u32[]{:S(2)}, u32[]{:S(2)}) %collective-permute-start) | collective-permute-done | bytes 2359328 | tf_op jit(solution)/shard_map/encode/ppermute | solution.py:137
  54.6 2.7 %select_bitcast_fusion.1 = (bf16[16,1,144,512]{3,2,1,0:T(8,128)(2,1)S(1)}, bf16[16,1,144,512]{3,2,1,0:T(8,128)(2,1)S(1)}) fusion(bf16[16,144,512]{2,1,0:T(8,128)(2,1)} %all-to-all-done, bf16[16,144,512]{2,1,0:T(8,128)(2,1)} %collective-permute-done, pred[]{:T(512)S(6)} %eq.10), kind=kLoop, calls=%fused_computation.10 | loop fusion | flops 2359296 | bytes 9437185 | tf_op jit(solution)/shard_map/encode/stack | solution.py:141
  58.1 7.9 %bitcast_reduce_fusion = f32[16,512]{1,0:T(8,128)S(1)} fusion(bf16[1024,512]{1,0:T(8,128)(2,1)S(1)} %bitcast.36, bf16[1024,4608]{1,0:T(8,128)(2,1)} %constant_dynamic-update-slice_fusion, bf16[4608,512]{1,0:T(8,128)(2,1)S(1)} %bitcast.33, f32[512]{0:T(512)S(1)} %copy-done.6, f32[512]{0:T(512)S(1)} %copy-done.7), kind=kOutput, calls=%fused_computation.11 | convolution fusion | flops 4834975744 | bytes 15241216 | tf_op jit(solution)/shard_map/encode/dot_general | solution.py:188
  66.2 40.4 %all_gather.7.fresh_ref = bf16[256,768]{1,0:T(8,128)(2,1)S(1)} all-gather(bf16[16,768]{1,0:T(8,128)(2,1)S(1)} %convolution_convert_fusion.1), channel_id=1, replica_groups=mesh['enc'=32,'seq'=16] {'seq'}, dimensions={0}, use_global_device_ids=true | all-gather | bytes 417792 | tf_op jit(solution)/shard_map/fresh/all_gather | solution.py:200
  106.7 2.8 %copy-done.1 = bf16[1,4096,768]{2,1,0:T(8,128)(2,1)S(1)} copy-done((bf16[1,4096,768]{2,1,0:T(8,128)(2,1)S(1)}, bf16[1,4096,768]{2,1,0:T(8,128)(2,1)}, u32[]{:S(2)}) %copy-start.1) | copy-done | bytes 6291480
  109.4 9.6 %head.1 = bf16[16,48,256]{2,1,0:T(8,128)(2,1)S(1)} custom-call(s32[256]{0:T(256)S(1)} %bitcast.32, s32[2]{0:T(128)S(1)} %pad_add_fusion.choice, bf16[4096,768]{1,0:T(8,128)(2,1)S(1)} %bitcast.31, bf16[256,768]{1,0:T(8,128)(2,1)S(1)} %all_gather.7.fresh_ref, bf16[768,256]{1,0:T(8,128)(2,1)S(1)} %concatenate.35.weight_ref), custom_call_target="tpu_custom_call" | custom-call | flops 1610612736 | bytes 6291456 | tf_op jit(solution)/shard_map/head/pallas_call | solution.py:98
  119.0 28.8 %all_to_all.10 = bf16[16,48,256]{2,1,0:T(8,128)(2,1)S(1)} all-to-all(bf16[16,48,256]{2,1,0:T(8,128)(2,1)S(1)} %head.1), channel_id=1, replica_groups=mesh['enc'=32,'seq'=16] {'seq'}, dimensions={0} | all-to-all | bytes 786432 | tf_op jit(solution)/shard_map/out/all_to_all | solution.py:206
  147.8 1.3 fusion
  (29 shorter events, 3.4 us)
Async XLA Ops:
  6.5 141.3 %copy-start = (bf16[768,768]{1,0:T(8,128)(2,1)S(1)}, bf16[768,768]{1,0:T(8,128)(2,1)}, u32[]{:S(2)}) copy-start(bf16[768,768]{1,0:T(8,128)(2,1)} %param.18) | copy-start | bytes 3538948
  6.5 13.5 %copy-start.8 = (s32[16]{0:T(128)S(1)}, s32[16]{0:T(128)}, u32[]{:S(2)}) copy-start(s32[16]{0:T(128)} %param.19) | copy-start | bytes 196
  6.5 15.4 %copy-start.5 = (bf16[768,144]{0,1:T(8,128)(2,1)S(1)}, bf16[768,144]{0,1:T(8,128)(2,1)}, u32[]{:S(2)}) copy-start(bf16[768,144]{0,1:T(8,128)(2,1)} %param.17) | copy-start | bytes 663556
  6.5 100.1 %all-gather.3.cloned.1.call-start = ((), (), s32[]{:S(2)}) async-start(), calls=%async_computation.2 | async-start | bytes 6684672 | tf_op jit(solution)/shard_map/rows/all_gather | solution.py:163
  7.3 18.0 %copy-start.3 = (bf16[1,16,8,8,512]{4,3,2,1,0:T(8,128)(2,1)S(1)}, bf16[1,16,8,8,512]{4,3,2,1,0:T(8,128)(2,1)}, u32[]{:S(2)}) copy-start(bf16[1,16,8,8,512]{4,3,2,1,0:T(8,128)(2,1)} %param.10) | copy-start | bytes 3145732
  9.9 38.0 %all-to-all-start = ((bf16[16,144,512]{2,1,0:T(8,128)(2,1)}), bf16[16,144,512]{2,1,0:T(8,128)(2,1)}, u32[]{:S(2)}, u32[]{:S(2)}) async-start(bf16[16,144,512]{2,1,0:T(8,128)(2,1)} %broadcast_in_dim.8), calls=%async_computation | async-start | bytes 4718592 | tf_op jit(solution)/shard_map/encode/all_to_all | solution.py:126
  47.9 6.8 %collective-permute-start = (bf16[16,144,512]{2,1,0:T(8,128)(2,1)}, bf16[16,144,512]{2,1,0:T(8,128)(2,1)}, u32[]{:S(2)}, u32[]{:S(2)}) collective-permute-start(bf16[16,144,512]{2,1,0:T(8,128)(2,1)} %all-to-all-done), channel_id=1, source_target_pairs={{0,16},{16,0},{32,48},{48,32},{64,80},{80,64},{96,112},{112,96},{1... | collective-permute-start | bytes 7077896 | tf_op jit(solution)/shard_map/encode/ppermute | solution.py:137
  57.4 0.7 copy-start.6
  57.4 0.7 copy-start.7
  58.1 7.9 %copy-start.4 = (bf16[512,768]{1,0:T(8,128)(2,1)S(1)}, bf16[512,768]{1,0:T(8,128)(2,1)}, u32[]{:S(2)}) copy-start(bf16[512,768]{1,0:T(8,128)(2,1)} %param.14) | copy-start | bytes 2359300
  58.1 48.6 %copy-start.2 = (s32[1,256]{1,0:T(1,128)S(1)}, s32[1,256]{1,0:T(1,128)}, u32[]{:S(2)}) copy-start(s32[1,256]{1,0:T(1,128)} %param.15) | copy-start | bytes 3076
  106.7 2.8 %copy-start.1 = (bf16[1,4096,768]{2,1,0:T(8,128)(2,1)S(1)}, bf16[1,4096,768]{2,1,0:T(8,128)(2,1)}, u32[]{:S(2)}) copy-start(bf16[1,4096,768]{2,1,0:T(8,128)(2,1)} %all-gather.3.cloned.1.call-done) | copy-start | bytes 18874372
Sparse Core Ops, SparseCore 0:
  9.4 93.8 all-gather.2

commit v4 on v3

--- a/solution.py
+++ b/solution.py
@@ -1,3 +1,4 @@
+import math
 from functools import partial
 
 import jax
@@ -12,6 +13,7 @@
 WIDTH = E // HEADS
 SEGMENT = 512
 STEP_ROWS = 512
+SCALE = WIDTH**-0.5 * math.log2(math.e)
 
 
 def attend(rate, offset, table, out_ref):
@@ -41,7 +43,7 @@
                 keys, queries, (((1,), (1,)), ((), ())), preferred_element_type=jnp.float32
             )
             top = jnp.max(scores, axis=0, keepdims=True)
-            raised = jnp.exp((scores - top) * WIDTH**-0.5).astype(jnp.bfloat16)
+            raised = jnp.exp2((scores - top) * SCALE).astype(jnp.bfloat16)
             mixed = lax.dot_general(
                 with_ones, raised, (((0,), (0,)), ((), ())), preferred_element_type=jnp.float32
             )
@@ -61,66 +63,120 @@
                         out_ref[first + block] = wide[:, block * loc : (block + 1) * loc]
         return carry
 
-    lax.fori_loop(0, length // (SEGMENT * rate), segment, 0)
-
-
-def head_kernel(places, choice, rows_ref, fresh_ref, weight_ref, out_ref, table, fresh):
-    step = pl.program_id(0)
-    made = jnp.dot(rows_ref[...], weight_ref[...], preferred_element_type=jnp.float32)
-    made = made.astype(jnp.bfloat16).astype(jnp.float32)
-    block = pl.ds(pl.multiple_of(step * STEP_ROWS, STEP_ROWS), STEP_ROWS)
-    table[0, block, :] = made[:, :128]
-    table[1, block, :] = made[:, 128:]
-
-    @pl.when(step == pl.num_programs(0) - 1)
-    def _():
-        made_fresh = jnp.dot(fresh_ref[...], weight_ref[...], preferred_element_type=jnp.float32)
-        made_fresh = made_fresh.astype(jnp.bfloat16).astype(jnp.float32)
-        fresh[0] = made_fresh[:, :128]
-        fresh[1] = made_fresh[:, 128:]
-
-        def place(group, carry):
-            for inner in range(8):
-                tile = group * 8 + inner
-                where = places[tile]
-                for side in range(2):
-                    table[side, pl.ds(where, 1), :] = fresh[side, pl.ds(tile, 1), :]
-            return carry
-
-        lax.fori_loop(0, fresh.shape[1] // 8, place, 0)
-        for rate in (1, 2, 4, 8):
-            pl.when(choice[0] == rate)(partial(attend, rate, choice[1], table, out_ref))
+    lax.fori_loop(0, length // (SEGMENT * rate), segment, 0, unroll=2 if rate < 8 else 1)
+
+
+def head_kernel(
+    places, choice, rows_ref, fresh_ref, weight_ref, out_ref, table, fresh, held, arrived
+):
+    chunks = held.shape[0]
+
+    def arrival(chunk):
+        first = pl.multiple_of(chunk * STEP_ROWS, STEP_ROWS)
+        return pltpu.make_async_copy(
+            rows_ref.at[pl.ds(first, STEP_ROWS)], held.at[chunk], arrived.at[chunk]
+        )
+
+    for chunk in range(chunks):
+        arrival(chunk).start()
+    made_fresh = jnp.dot(fresh_ref[...], weight_ref[...], preferred_element_type=jnp.float32)
+    made_fresh = made_fresh.astype(jnp.bfloat16).astype(jnp.float32)
+    fresh[0] = made_fresh[:, :128]
+    fresh[1] = made_fresh[:, 128:]
+
+    def project(chunk, carry):
+        arrival(chunk).wait()
+        made = jnp.dot(held[chunk], weight_ref[...], preferred_element_type=jnp.float32)
+        made = made.astype(jnp.bfloat16).astype(jnp.float32)
+        block = pl.ds(pl.multiple_of(chunk * STEP_ROWS, STEP_ROWS), STEP_ROWS)
+        table[0, block, :] = made[:, :128]
+        table[1, block, :] = made[:, 128:]
+        return carry
+
+    lax.fori_loop(0, chunks, project, 0)
+
+    def place(group, carry):
+        for inner in range(8):
+            tile = group * 8 + inner
+            where = places[tile]
+            for side in range(2):
+                table[side, pl.ds(where, 1), :] = fresh[side, pl.ds(tile, 1), :]
+        return carry
+
+    lax.fori_loop(0, fresh.shape[1] // 8, place, 0)
+    for rate in (1, 2, 4, 8):
+        pl.when(choice[0] == rate)(partial(attend, rate, choice[1], table, out_ref))
 
 
 def head_attention(places, choice, rows, fresh, weight, seq_count):
     length = rows.shape[0]
     loc = length // seq_count
+    chunks = length // STEP_ROWS
     return pl.pallas_call(
         head_kernel,
         out_shape=jax.ShapeDtypeStruct((seq_count, WIDTH, loc), jnp.bfloat16),
-        grid_spec=pltpu.PrefetchScalarGridSpec(
-            num_scalar_prefetch=2,
-            grid=(length // STEP_ROWS,),
-            in_specs=[
-                pl.BlockSpec((STEP_ROWS, E), lambda i, *_: (i, 0)),
-                pl.BlockSpec(fresh.shape, lambda i, *_: (0, 0)),
-                pl.BlockSpec(weight.shape, lambda i, *_: (0, 0)),
-            ],
-            out_specs=pl.BlockSpec((seq_count, WIDTH, loc), lambda i, *_: (0, 0, 0)),
-            scratch_shapes=[
-                pltpu.VMEM((2, length, 128), jnp.float32),
-                pltpu.VMEM((2, fresh.shape[0], 128), jnp.float32),
-            ],
-        ),
-        compiler_params=pltpu.CompilerParams(
-            dimension_semantics=("arbitrary",), vmem_limit_bytes=24 * 1024 * 1024
-        ),
+        in_specs=[
+            pl.BlockSpec(memory_space=pltpu.SMEM),
+            pl.BlockSpec(memory_space=pltpu.SMEM),
+            pl.BlockSpec(memory_space=pltpu.HBM),
+            pl.BlockSpec(memory_space=pltpu.VMEM),
+            pl.BlockSpec(memory_space=pltpu.VMEM),
+        ],
+        out_specs=pl.BlockSpec(memory_space=pltpu.VMEM),
+        scratch_shapes=[
+            pltpu.VMEM((2, length, 128), jnp.float32),
+            pltpu.VMEM((2, fresh.shape[0], 128), jnp.float32),
+            pltpu.VMEM((chunks, STEP_ROWS, E), jnp.bfloat16),
+            pltpu.SemaphoreType.DMA((chunks,)),
+        ],
+        compiler_params=pltpu.CompilerParams(vmem_limit_bytes=24 * 1024 * 1024),
         cost_estimate=pl.CostEstimate(
             flops=2 * length * E * 256, bytes_accessed=rows.size * 2, transcendentals=length * SEGMENT
         ),
     )(places, choice, rows, fresh, weight)
 
 
+def regroup_kernel(shard, core, columns_ref, own_ref, other_ref):
+    columns = columns_ref[...]
+    count = columns.shape[1] // shard
+    even, odd = (
+        jnp.concatenate(
+            [columns[:, j * shard : (j + 1) * shard] for j in range(first, count, 2)], axis=1
+        )
+        for first in range(2)
+    )
+
+    @pl.when(core[0] == 0)
+    def _():
+        own_ref[...] = even
+        other_ref[...] = odd
+
+    @pl.when(core[0] == 1)
+    def _():
+        own_ref[...] = odd
+        other_ref[...] = even
+
+
+def regroup(core, columns, shard):
+    rows, depth = columns.shape
+    half = jax.ShapeDtypeStruct((rows, depth // 2), columns.dtype)
+    block = 128
+    return pl.pallas_call(
+        partial(regroup_kernel, shard),
+        out_shape=(half, half),
+        grid_spec=pltpu.PrefetchScalarGridSpec(
+            num_scalar_prefetch=1,
+            grid=(rows // block,),
+            in_specs=[pl.BlockSpec((block, depth), lambda i, *_: (i, 0))],
+            out_specs=[pl.BlockSpec((block, depth // 2), lambda i, *_: (i, 0))] * 2,
+        ),
+        compiler_params=pltpu.CompilerParams(vmem_limit_bytes=24 * 1024 * 1024),
+        cost_estimate=pl.CostEstimate(
+            flops=0, bytes_accessed=columns.size * 4, transcendentals=0
+        ),
+    )(core, columns)
+
+
 def spread_to(shard, axis, count, groups=None):
     copies = jnp.broadcast_to(shard[None], (count,) + shard.shape)
     return lax.all_to_all(
@@ -128,17 +184,25 @@
     )
 
 
-def whole_weight(conv_weight, ready):
+def convolve(conv_weight, columns, ready):
     enc_count = lax.axis_size("enc")
     chips = enc_count // 2
+    shard, channels = conv_weight.shape
     groups = [[2 * chip + core for chip in range(chips)] for core in range(2)]
     own = spread_to(conv_weight, "enc", chips, groups)
-    own, ready = lax.optimization_barrier((own, ready))
+    core = (lax.axis_index("enc") % 2).astype(jnp.int32).reshape(1)
+    own_columns, other_columns = regroup(core, columns, shard)
+    own, own_columns, other_columns, ready = lax.optimization_barrier(
+        (own, own_columns, other_columns, ready)
+    )
     other = lax.ppermute(own, "enc", [(e, e ^ 1) for e in range(enc_count)])
-    first_core = lax.axis_index("enc") % 2 == 0
-    even = jnp.where(first_core, own, other)
-    odd = jnp.where(first_core, other, own)
-    return jnp.stack([even, odd], axis=1).reshape(-1, conv_weight.shape[1]), ready
+    first = jnp.dot(
+        own_columns, own.reshape(-1, channels), preferred_element_type=jnp.float32
+    )
+    second = jnp.dot(
+        other_columns, other.reshape(-1, channels), preferred_element_type=jnp.float32
+    )
+    return first + second, ready
 
 
 def shards(
@@ -182,10 +246,7 @@
             axis=-1,
         )
         columns = columns.reshape(tile_count * side_len * side_len, 9 * channels)
-        weight, (columns, head_weight, choice) = whole_weight(
-            conv_weight, (columns, head_weight, choice)
-        )
-        convolved = jnp.dot(columns, weight, preferred_element_type=jnp.float32)
+        convolved, (head_weight, choice) = convolve(conv_weight, columns, (head_weight, choice))
         activated = jnp.maximum(convolved * norm_gain + norm_bias, 0.0) + images.reshape(
             -1, channels
         ).astype(jnp.float32)

time: 157 us -> 158 us (level)
  local copies, waits for them, and re-layouts: 20.4 us -> 15.2 us
  blocking collectives: 69.3 us -> 73.8 us
  Pallas kernels: 9.56 us -> 13.9 us
  other arithmetic: 3.85 us -> 0.68 us
  matrix products: 9.36 us -> 12 us
  waiting for transfers between devices: 16.7 us -> 14.9 us
    ppermute x1, waiting for transfers between devices: 4.83 us -> 0.01 us  [convolve(): other = lax.ppermute(own, 'enc', [(e, e ^ 1) for e in range(enc_count)])]
    pallas_call x0 -> x1, Pallas kernels: none -> 4.28 us  [regroup(): pl.pallas_call(partial(regroup_kernel, shard), out_shape=(half, half), gr...]
    unnamed x29 -> x33, local copies, waits for them, and re-layouts: 13 us -> 8.96 us
    all_to_all x1, blocking collectives: 28.8 us -> 32.8 us  [shards(): lax.all_to_all(head_out, 'seq', split_axis=0, concat_axis=0, tiled=True)]
    another operation x2 -> x0, other arithmetic: 3.16 us -> none  [whole_weight(): jnp.stack([even, odd], axis=1).reshape(-1, conv_weight.shape[1])]
    dot_general x1 -> x2, matrix products: 7.9 us -> 10.6 us  [the longest x1 5.35 us: convolve(): jnp.dot(other_columns, other.reshape(-1, channels), preferred_element_typ...]
    all_gather x1, waiting for transfers between devices: 0.01 us -> 2.59 us  [shards(): rows = lax.all_gather(slide_cache[0], 'seq', axis=0, tiled=True)]
  transfers between devices with their start and end apart: 3 -> 3, of which waited for: 2 -> 2; matrix products, arithmetic and copies ran while one was open for 19% -> 12% of each run, Pallas kernels for 0% -> 3%
where the time goes in v4:
time: 158 us
  blocking collectives  73.8 us (47%)
  local copies, waits for them, and re-layouts  15.2 us (10%)
  waiting for transfers between devices  14.9 us (9%)
  between operations  14.9 us (9%)
  Pallas kernels  13.9 us (9%)
  starting transfers between devices  12.1 us (8%)
  matrix products  12 us (8%)
    all_gather x1, blocking collectives, shards(): fresh = lax.all_gather(embedded, 'seq', axis=0, tiled=True)  41 us
    all_to_all x1, blocking collectives, shards(): lax.all_to_all(head_out, 'seq', split_axis=0, concat_axis=0, tiled=True)  32.8 us
    all_to_all x1, waiting for transfers between devices, spread_to(): lax.all_to_all(copies, axis, split_axis=0, concat_axis=0, tiled=True, axi...  11.6 us
    all_to_all x1, starting transfers between devices, spread_to(): lax.all_to_all(copies, axis, split_axis=0, concat_axis=0, tiled=True, axi...  10.1 us
    pallas_call x1, Pallas kernels, head_attention(): pl.pallas_call(head_kernel, out_shape=jax.ShapeDtypeStruct((seq_count, WI...  9.6 us
    unnamed x33, local copies, waits for them, and re-layouts  8.96 us
    dot_general x1, matrix products, convolve(): jnp.dot(other_columns, other.reshape(-1, channels), preferred_element_typ...  5.35 us
    dot_general x1, matrix products, convolve(): jnp.dot(own_columns, own.reshape(-1, channels), preferred_element_type=jn...  5.2 us
  transfers between devices with their start and end apart: 3, of which 2 were waited for; matrix products, arithmetic and copies ran while one was open for 12% of the time, Pallas kernels for 3%

profile of v4, /device:TPU:6, one launch (start us, length us, event | category | flops | bytes accessed | tf_op | source)
XLA Modules:
  0.0 157.5 jit_solution(7768601203035258700)
XLA Ops:
  6.6 0.7 all-gather.3.cloned.1.call-update
  7.3 2.5 %broadcast_in_dim.8 = bf16[16,144,512]{2,1,0:T(8,128)(2,1)} broadcast(bf16[144,512]{1,0:T(8,128)(2,1)} %param.11), dimensions={1,2} | broadcast | bytes 2506752 | tf_op jit(solution)/shard_map/encode/broadcast_in_dim | solution.py:181
  9.8 10.1 %all-to-all-start = ((bf16[16,144,512]{2,1,0:T(8,128)(2,1)}), bf16[16,144,512]{2,1,0:T(8,128)(2,1)}, u32[]{:S(2)}, u32[]{:S(2)}) async-start(bf16[16,144,512]{2,1,0:T(8,128)(2,1)} %broadcast_in_dim.8), calls=%async_computation | async-start | bytes 4718592 | tf_op jit(solution)/shard_map/encode/all_to_all | solution.py:182
  20.0 0.6 dynamic_slice.3
  21.8 0.2 copy.14
  22.0 0.2 copy.15
  22.2 0.8 copy.16
  23.0 1.6 %pad_slice_fusion = (bf16[16,8,8,512]{3,2,1,0:T(8,128)(2,1)S(1)}, bf16[16,8,8,512]{3,2,1,0:T(8,128)(2,1)S(1)}, bf16[16,8,8,512]{3,2,1,0:T(8,128)(2,1)S(1)}, bf16...) fusion(bf16[16,8,8,512]{3,2,1,0:T(8,128)(2,1)S(1)} %bitcast.31), kind=kLoop, calls=%fused_computation | loop fusion | bytes 9437184 | tf_op jit(solution)/shard_map/encode/slice | solution.py:242
  25.3 4.3 %encode.1 = (bf16[1024,2304]{1,0:T(8,128)(2,1)S(1)}, bf16[1024,2304]{1,0:T(8,128)(2,1)S(1)}) custom-call(s32[1]{0:T(128)} %bitcast.1.core, bf16[1024,4608]{1,0:T(8,128)(2,1)S(1)} %constant_dynamic-update-slice_fusion.columns_ref), custom_call_target="tpu_custom_call" | custom-call | bytes 18874368 | tf_op jit(solution)/shard_map/encode/pallas_call | solution.py:164
  29.6 2.2 %copy-done.3 = bf16[1024,2304]{1,0:T(8,128)(2,1)} copy-done((bf16[1024,2304]{1,0:T(8,128)(2,1)}, bf16[1024,2304]{1,0:T(8,128)(2,1)S(1)}, u32[]{:S(2)}) %copy-start.3) | copy-done | bytes 4718616
  31.9 2.2 %copy-done.4 = bf16[1024,2304]{1,0:T(8,128)(2,1)} copy-done((bf16[1024,2304]{1,0:T(8,128)(2,1)}, bf16[1024,2304]{1,0:T(8,128)(2,1)S(1)}, u32[]{:S(2)}) %copy-start.4) | copy-done | bytes 4718616
  34.1 1.4 concatenate.35.weight_ref
  35.5 0.7 pad_add_fusion.choice
  36.2 11.6 %all-to-all-done = bf16[16,144,512]{2,1,0:T(8,128)(2,1)} async-done(((bf16[16,144,512]{2,1,0:T(8,128)(2,1)}), bf16[16,144,512]{2,1,0:T(8,128)(2,1)}, u32[]{:S(2)}, u32[]{:S(2)}) %all-to-all-start) | async-done | bytes 2359328 | tf_op jit(solution)/shard_map/encode/all_to_all | solution.py:182
  47.8 1.9 %collective-permute-start = (bf16[16,144,512]{2,1,0:T(8,128)(2,1)}, bf16[16,144,512]{2,1,0:T(8,128)(2,1)S(1)}, u32[]{:S(2)}, u32[]{:S(2)}) collective-permute-start(bf16[16,144,512]{2,1,0:T(8,128)(2,1)} %all-to-all-done), channel_id=1, source_target_pairs={{0,16},{16,0},{32,48},{48,32},{64,80},{80,64},{96,112},{112,96},{1... | collective-permute-start | bytes 7077896 | tf_op jit(solution)/shard_map/encode/ppermute | solution.py:198
  49.7 5.2 %fusion.4 = f32[1024,512]{1,0:T(8,128)S(1)} fusion(bf16[1024,2304]{1,0:T(8,128)(2,1)} %copy-done.4, bf16[2304,512]{1,0:T(8,128)(2,1)} %bitcast.15), kind=kOutput, calls=%fused_computation.27 | convolution fusion | flops 2415919104 | bytes 9175040 | tf_op jit(solution)/shard_map/encode/dot_general | solution.py:199
  55.0 5.4 %bitcast_reduce_fusion = f32[16,512]{1,0:T(8,128)S(1)} fusion(bf16[1024,512]{1,0:T(8,128)(2,1)S(1)} %bitcast.33, f32[1024,512]{1,0:T(8,128)S(1)} %fusion.4, bf16[1024,2304]{1,0:T(8,128)(2,1)} %copy-done.3, bf16[2304,512]{1,0:T(8,128)(2,1)S(1)} %bitcast.43, f32[512]{0:T(512)S(1)} %copy-done.8, f32[512]{0:T(512)S(1)} %copy-done.9), kind=kOutput, calls=%fused_computation.8 | convolution fusion | flops 2419580928 | bytes 10260480 | tf_op jit(solution)/shard_map/encode/dot_general | solution.py:202
  60.4 0.2 convolution_convert_fusion.1
  60.6 41.0 %all_gather.7.fresh_ref = bf16[256,768]{1,0:T(8,128)(2,1)S(1)} all-gather(bf16[16,768]{1,0:T(8,128)(2,1)S(1)} %convolution_convert_fusion.1), channel_id=1, replica_groups=mesh['enc'=32,'seq'=16] {'seq'}, dimensions={0}, use_global_device_ids=true | all-gather | bytes 417792 | tf_op jit(solution)/shard_map/fresh/all_gather | solution.py:261
  101.6 2.6 %all-gather.3.cloned.1.call-done = bf16[1,4096,768]{2,1,0:T(8,128)(2,1)} async-done(((bf16[1,256,768]{2,1,0:T(8,128)(2,1)}), bf16[1,4096,768]{2,1,0:T(8,128)(2,1)}) %all-gather.3.cloned.1.call-update) | async-done | bytes 6291472 | tf_op jit(solution)/shard_map/rows/all_gather | solution.py:227
  104.2 2.8 %copy-done.1 = bf16[1,4096,768]{2,1,0:T(8,128)(2,1)S(1)} copy-done((bf16[1,4096,768]{2,1,0:T(8,128)(2,1)S(1)}, bf16[1,4096,768]{2,1,0:T(8,128)(2,1)}, u32[]{:S(2)}) %copy-start.1) | copy-done | bytes 6291480
  107.0 9.6 %head.1 = bf16[16,48,256]{2,1,0:T(8,128)(2,1)S(1)} custom-call(s32[256]{0:T(256)S(1)} %bitcast.30, s32[2]{0:T(128)S(1)} %pad_add_fusion.choice, bf16[4096,768]{1,0:T(8,128)(2,1)S(1)} %bitcast.29, bf16[256,768]{1,0:T(8,128)(2,1)S(1)} %all_gather.7.fresh_ref, bf16[768,256]{1,0:T(8,128)(2,1)S(1)} %concatenate.35.weight_ref), custom_call_target="tpu_custom_call" | custom-call | flops 1610612736 | bytes 6291456 | tf_op jit(solution)/shard_map/head/pallas_call | solution.py:115
  116.6 32.8 %all_to_all.10 = bf16[16,48,256]{2,1,0:T(8,128)(2,1)S(1)} all-to-all(bf16[16,48,256]{2,1,0:T(8,128)(2,1)S(1)} %head.1), channel_id=1, replica_groups=mesh['enc'=32,'seq'=16] {'seq'}, dimensions={0} | all-to-all | bytes 786432 | tf_op jit(solution)/shard_map/out/all_to_all | solution.py:267
  149.4 1.3 fusion
  (33 shorter events, 0.8 us)
Async XLA Ops:
  6.5 142.9 %copy-start = (bf16[768,768]{1,0:T(8,128)(2,1)S(1)}, bf16[768,768]{1,0:T(8,128)(2,1)}, u32[]{:S(2)}) copy-start(bf16[768,768]{1,0:T(8,128)(2,1)} %param.18) | copy-start | bytes 3538948
  6.5 13.4 %copy-start.10 = (s32[16]{0:T(128)S(1)}, s32[16]{0:T(128)}, u32[]{:S(2)}) copy-start(s32[16]{0:T(128)} %param.19) | copy-start | bytes 196
  6.5 15.3 %copy-start.7 = (bf16[768,144]{0,1:T(8,128)(2,1)S(1)}, bf16[768,144]{0,1:T(8,128)(2,1)}, u32[]{:S(2)}) copy-start(bf16[768,144]{0,1:T(8,128)(2,1)} %param.17) | copy-start | bytes 663556
  6.5 16.5 %copy-start.5 = (bf16[1,16,8,8,512]{4,3,2,1,0:T(8,128)(2,1)S(1)}, bf16[1,16,8,8,512]{4,3,2,1,0:T(8,128)(2,1)}, u32[]{:S(2)}) copy-start(bf16[1,16,8,8,512]{4,3,2,1,0:T(8,128)(2,1)} %param.10) | copy-start | bytes 3145732
  6.5 97.6 %all-gather.3.cloned.1.call-start = ((), (), s32[]{:S(2)}) async-start(), calls=%async_computation.2 | async-start | bytes 6684672 | tf_op jit(solution)/shard_map/rows/all_gather | solution.py:227
  9.8 38.0 %all-to-all-start = ((bf16[16,144,512]{2,1,0:T(8,128)(2,1)}), bf16[16,144,512]{2,1,0:T(8,128)(2,1)}, u32[]{:S(2)}, u32[]{:S(2)}) async-start(bf16[16,144,512]{2,1,0:T(8,128)(2,1)} %broadcast_in_dim.8), calls=%async_computation | async-start | bytes 4718592 | tf_op jit(solution)/shard_map/encode/all_to_all | solution.py:182
  29.6 2.2 %copy-start.3 = (bf16[1024,2304]{1,0:T(8,128)(2,1)}, bf16[1024,2304]{1,0:T(8,128)(2,1)S(1)}, u32[]{:S(2)}) copy-start(bf16[1024,2304]{1,0:T(8,128)(2,1)S(1)} %get-tuple-element.17) | copy-start | bytes 14155780
  31.9 2.2 %copy-start.4 = (bf16[1024,2304]{1,0:T(8,128)(2,1)}, bf16[1024,2304]{1,0:T(8,128)(2,1)S(1)}, u32[]{:S(2)}) copy-start(bf16[1024,2304]{1,0:T(8,128)(2,1)S(1)} %get-tuple-element.15) | copy-start | bytes 14155780
  47.8 7.2 %collective-permute-start = (bf16[16,144,512]{2,1,0:T(8,128)(2,1)}, bf16[16,144,512]{2,1,0:T(8,128)(2,1)S(1)}, u32[]{:S(2)}, u32[]{:S(2)}) collective-permute-start(bf16[16,144,512]{2,1,0:T(8,128)(2,1)} %all-to-all-done), channel_id=1, source_target_pairs={{0,16},{16,0},{32,48},{48,32},{64,80},{80,64},{96,112},{112,96},{1... | collective-permute-start | bytes 7077896 | tf_op jit(solution)/shard_map/encode/ppermute | solution.py:198
  49.7 5.2 %copy-start.8 = (f32[512]{0:T(512)S(1)}, f32[512]{0:T(512)}, u32[]{:S(2)}) copy-start(f32[512]{0:T(512)} %param.13) | copy-start | bytes 6148
  49.7 5.2 %copy-start.9 = (f32[512]{0:T(512)S(1)}, f32[512]{0:T(512)}, u32[]{:S(2)}) copy-start(f32[512]{0:T(512)} %param.12) | copy-start | bytes 6148
  55.0 5.4 %copy-start.6 = (bf16[512,768]{1,0:T(8,128)(2,1)S(1)}, bf16[512,768]{1,0:T(8,128)(2,1)}, u32[]{:S(2)}) copy-start(bf16[512,768]{1,0:T(8,128)(2,1)} %param.14) | copy-start | bytes 2359300
  55.0 49.2 %copy-start.2 = (s32[1,256]{1,0:T(1,128)S(1)}, s32[1,256]{1,0:T(1,128)}, u32[]{:S(2)}) copy-start(s32[1,256]{1,0:T(1,128)} %param.15) | copy-start | bytes 3076
  104.2 2.8 %copy-start.1 = (bf16[1,4096,768]{2,1,0:T(8,128)(2,1)S(1)}, bf16[1,4096,768]{2,1,0:T(8,128)(2,1)}, u32[]{:S(2)}) copy-start(bf16[1,4096,768]{2,1,0:T(8,128)(2,1)} %all-gather.3.cloned.1.call-done) | copy-start | bytes 18874372
Sparse Core Ops, SparseCore 0:
  9.5 94.6 all-gather.2

commit v5 on v4

--- a/solution.py
+++ b/solution.py
@@ -12,7 +12,7 @@
 HEADS = 16
 WIDTH = E // HEADS
 SEGMENT = 512
-STEP_ROWS = 512
+STEP_ROWS = 1024
 SCALE = WIDTH**-0.5 * math.log2(math.e)
 
 
@@ -25,45 +25,68 @@
         target = lax.broadcasted_iota(jnp.int32, (128, 128 * rate), 1)
         spread = (target == offset + rate * source).astype(jnp.float32).astype(jnp.bfloat16)
     lane = lax.broadcasted_iota(jnp.int32, (SEGMENT, 128), 1)
-
-    def segment(index, carry):
+    def load(index):
         start = index * (SEGMENT * rate) + offset
         if rate == 1:
-            start = pl.multiple_of(index * SEGMENT, SEGMENT)
-            rows = pl.ds(start, SEGMENT)
+            rows = pl.ds(pl.multiple_of(index * SEGMENT, SEGMENT), SEGMENT)
         else:
             rows = pl.ds(start, SEGMENT, stride=rate)
         query_value = table[0, rows, :]
         keys = table[1, rows, :].astype(jnp.bfloat16)
         with_ones = jnp.where(lane == 112, 1.0, query_value).astype(jnp.bfloat16)
-        query_value = query_value.astype(jnp.bfloat16)
-        for part in range(SEGMENT // 256):
-            queries = query_value[part * 256 : (part + 1) * 256]
-            scores = lax.dot_general(
-                keys, queries, (((1,), (1,)), ((), ())), preferred_element_type=jnp.float32
-            )
-            top = jnp.max(scores, axis=0, keepdims=True)
-            raised = jnp.exp2((scores - top) * SCALE).astype(jnp.bfloat16)
-            mixed = lax.dot_general(
-                with_ones, raised, (((0,), (0,)), ((), ())), preferred_element_type=jnp.float32
-            )
-            result = (mixed[64:112] / mixed[112:113]).astype(jnp.bfloat16)
-            if rate == 1:
-                out_ref[index * (SEGMENT // loc) + part] = result
-            else:
-                for half in range(2):
-                    wide = jnp.dot(
-                        result[:, half * 128 : (half + 1) * 128],
-                        spread,
-                        preferred_element_type=jnp.float32,
-                    ).astype(jnp.bfloat16)
-                    blocks = 128 * rate // loc
-                    first = (index * 4 + part * 2 + half) * blocks
-                    for block in range(blocks):
-                        out_ref[first + block] = wide[:, block * loc : (block + 1) * loc]
+        return query_value.astype(jnp.bfloat16), keys, with_ones
+
+    def score(loaded, part):
+        queries, keys, _ = loaded
+        return lax.dot_general(
+            keys,
+            queries[part * 512 : (part + 1) * 512],
+            (((1,), (1,)), ((), ())),
+            preferred_element_type=jnp.float32,
+        )
+
+    def finish(index, part, loaded, scores):
+        top = jnp.max(scores, axis=0, keepdims=True)
+        raised = jnp.exp2((scores - top) * SCALE).astype(jnp.bfloat16)
+        mixed = lax.dot_general(
+            loaded[2], raised, (((0,), (0,)), ((), ())), preferred_element_type=jnp.float32
+        )
+        result = (mixed[64:112] / mixed[112:113]).astype(jnp.bfloat16)
+        if rate == 1:
+            for block in range(512 // loc):
+                out_ref[index * (SEGMENT // loc) + part * (512 // loc) + block] = result[
+                    :, block * loc : (block + 1) * loc
+                ]
+            return
+        blocks = 128 * rate // loc
+        for piece in range(512 // 128):
+            wide = jnp.dot(
+                result[:, piece * 128 : (piece + 1) * 128],
+                spread,
+                preferred_element_type=jnp.float32,
+            ).astype(jnp.bfloat16)
+            first = (index * 4 + part * (512 // 128) + piece) * blocks
+            for block in range(blocks):
+                out_ref[first + block] = wide[:, block * loc : (block + 1) * loc]
+
+    segments = length // (SEGMENT * rate)
+    together = min(segments, 4)
+
+    def group(step, carry):
+        work = []
+        for inner in range(together):
+            index = step * together + inner
+            loaded = load(index)
+            work += [(index, part, loaded) for part in range(SEGMENT // 512)]
+        ahead = [score(loaded, part) for _, part, loaded in work[:1]]
+        for number, (index, part, loaded) in enumerate(work):
+            if number + 1 < len(work):
+                _, next_part, next_loaded = work[number + 1]
+                ahead.append(score(next_loaded, next_part))
+            finish(index, part, loaded, ahead[number])
         return carry
 
-    lax.fori_loop(0, length // (SEGMENT * rate), segment, 0, unroll=2 if rate < 8 else 1)
+    lax.fori_loop(0, segments // together, group, 0)
 
 
 def head_kernel(
@@ -129,9 +152,9 @@
             pltpu.VMEM((chunks, STEP_ROWS, E), jnp.bfloat16),
             pltpu.SemaphoreType.DMA((chunks,)),
         ],
-        compiler_params=pltpu.CompilerParams(vmem_limit_bytes=24 * 1024 * 1024),
+        compiler_params=pltpu.CompilerParams(vmem_limit_bytes=48 * 1024 * 1024),
         cost_estimate=pl.CostEstimate(
-            flops=2 * length * E * 256, bytes_accessed=rows.size * 2, transcendentals=length * SEGMENT
+            flops=2 * length * E * 256, bytes_accessed=0, transcendentals=0
         ),
     )(places, choice, rows, fresh, weight)
 

time: 158 us -> 152 us (0.962)
  local copies, waits for them, and re-layouts: 15.2 us -> 12.4 us
  Pallas kernels: 13.9 us -> 11.4 us
    unnamed x33 -> x31, local copies, waits for them, and re-layouts: 8.96 us -> 6.15 us
    pallas_call x1, Pallas kernels: 9.6 us -> 7.14 us  [head_attention(): pl.pallas_call(head_kernel, out_shape=jax.ShapeDtypeStruct((seq_count, WI...]
  transfers between devices with their start and end apart: 3 -> 3, of which waited for: 2 -> 2; matrix products, arithmetic and copies ran while one was open for 12% -> 13% of each run, Pallas kernels for 3% -> 3%
where the time goes in v5:
time: 152 us; the launch traced here: 151 us
  blocking collectives  72.7 us (48%)
  waiting for transfers between devices  14.9 us (10%)
  between operations  14.9 us (10%)
  local copies, waits for them, and re-layouts  12.4 us (8%)
  starting transfers between devices  12.1 us (8%)
  matrix products  12 us (8%)
  Pallas kernels  11.4 us (8%)
    all_gather x1, blocking collectives, shards(): fresh = lax.all_gather(embedded, 'seq', axis=0, tiled=True)  41 us
    all_to_all x1, blocking collectives, shards(): lax.all_to_all(head_out, 'seq', split_axis=0, concat_axis=0, tiled=True)  31.7 us
    all_to_all x1, waiting for transfers between devices, spread_to(): lax.all_to_all(copies, axis, split_axis=0, concat_axis=0, tiled=True, axi...  11.6 us
    all_to_all x1, starting transfers between devices, spread_to(): lax.all_to_all(copies, axis, split_axis=0, concat_axis=0, tiled=True, axi...  10.1 us
    pallas_call x1, Pallas kernels, head_attention(): pl.pallas_call(head_kernel, out_shape=jax.ShapeDtypeStruct((seq_count, WI...  7.14 us
    unnamed x31, local copies, waits for them, and re-layouts  6.15 us
    dot_general x1, matrix products, convolve(): jnp.dot(other_columns, other.reshape(-1, channels), preferred_element_typ...  5.35 us
    dot_general x1, matrix products, convolve(): jnp.dot(own_columns, own.reshape(-1, channels), preferred_element_type=jn...  5.2 us
  transfers between devices with their start and end apart: 3, of which 2 were waited for; matrix products, arithmetic and copies ran while one was open for 13% of the time, Pallas kernels for 3%

profile of v5, /device:TPU:6, one launch (start us, length us, event | category | flops | bytes accessed | tf_op | source)
XLA Modules:
  0.0 151.2 jit_solution(2666362303613122793)
XLA Ops:
  6.6 0.7 all-gather.3.cloned.1.call-update
  7.3 2.5 %broadcast_in_dim.8 = bf16[16,144,512]{2,1,0:T(8,128)(2,1)} broadcast(bf16[144,512]{1,0:T(8,128)(2,1)} %param.11), dimensions={1,2} | broadcast | bytes 2506752 | tf_op jit(solution)/shard_map/encode/broadcast_in_dim | solution.py:204
  9.8 10.1 %all-to-all-start = ((bf16[16,144,512]{2,1,0:T(8,128)(2,1)}), bf16[16,144,512]{2,1,0:T(8,128)(2,1)}, u32[]{:S(2)}, u32[]{:S(2)}) async-start(bf16[16,144,512]{2,1,0:T(8,128)(2,1)} %broadcast_in_dim.8), calls=%async_computation | async-start | bytes 4718592 | tf_op jit(solution)/shard_map/encode/all_to_all | solution.py:205
  19.9 0.6 dynamic_slice.3
  21.9 0.2 copy.14
  22.1 0.2 copy.15
  22.2 0.8 copy.16
  23.1 1.6 %pad_slice_fusion = (bf16[16,8,8,512]{3,2,1,0:T(8,128)(2,1)S(1)}, bf16[16,8,8,512]{3,2,1,0:T(8,128)(2,1)S(1)}, bf16[16,8,8,512]{3,2,1,0:T(8,128)(2,1)S(1)}, bf16...) fusion(bf16[16,8,8,512]{3,2,1,0:T(8,128)(2,1)S(1)} %bitcast.31), kind=kLoop, calls=%fused_computation | loop fusion | bytes 9437184 | tf_op jit(solution)/shard_map/encode/slice | solution.py:265
  24.8 0.1 constant_dynamic-update-slice_fusion.7
  25.4 4.3 %encode.1 = (bf16[1024,2304]{1,0:T(8,128)(2,1)S(1)}, bf16[1024,2304]{1,0:T(8,128)(2,1)S(1)}) custom-call(s32[1]{0:T(128)} %bitcast.1.core, bf16[1024,4608]{1,0:T(8,128)(2,1)S(1)} %constant_dynamic-update-slice_fusion.columns_ref), custom_call_target="tpu_custom_call" | custom-call | bytes 18874368 | tf_op jit(solution)/shard_map/encode/pallas_call | solution.py:187
  29.7 2.2 %copy-done.2 = bf16[1024,2304]{1,0:T(8,128)(2,1)} copy-done((bf16[1024,2304]{1,0:T(8,128)(2,1)}, bf16[1024,2304]{1,0:T(8,128)(2,1)S(1)}, u32[]{:S(2)}) %copy-start.2) | copy-done | bytes 4718616
  31.9 2.2 %copy-done.3 = bf16[1024,2304]{1,0:T(8,128)(2,1)} copy-done((bf16[1024,2304]{1,0:T(8,128)(2,1)}, bf16[1024,2304]{1,0:T(8,128)(2,1)S(1)}, u32[]{:S(2)}) %copy-start.3) | copy-done | bytes 4718616
  34.1 1.4 concatenate.35.weight_ref
  35.5 0.7 pad_add_fusion.choice
  36.2 11.6 %all-to-all-done = bf16[16,144,512]{2,1,0:T(8,128)(2,1)} async-done(((bf16[16,144,512]{2,1,0:T(8,128)(2,1)}), bf16[16,144,512]{2,1,0:T(8,128)(2,1)}, u32[]{:S(2)}, u32[]{:S(2)}) %all-to-all-start) | async-done | bytes 2359328 | tf_op jit(solution)/shard_map/encode/all_to_all | solution.py:205
  47.8 1.9 %collective-permute-start = (bf16[16,144,512]{2,1,0:T(8,128)(2,1)}, bf16[16,144,512]{2,1,0:T(8,128)(2,1)S(1)}, u32[]{:S(2)}, u32[]{:S(2)}) collective-permute-start(bf16[16,144,512]{2,1,0:T(8,128)(2,1)} %all-to-all-done), channel_id=1, source_target_pairs={{0,16},{16,0},{32,48},{48,32},{64,80},{80,64},{96,112},{112,96},{1... | collective-permute-start | bytes 7077896 | tf_op jit(solution)/shard_map/encode/ppermute | solution.py:221
  49.7 5.2 %fusion.4 = f32[1024,512]{1,0:T(8,128)S(1)} fusion(bf16[1024,2304]{1,0:T(8,128)(2,1)} %copy-done.3, bf16[2304,512]{1,0:T(8,128)(2,1)} %bitcast.15), kind=kOutput, calls=%fused_computation.27 | convolution fusion | flops 2415919104 | bytes 9175040 | tf_op jit(solution)/shard_map/encode/dot_general | solution.py:222
  55.0 5.4 %bitcast_reduce_fusion = f32[16,512]{1,0:T(8,128)S(1)} fusion(bf16[1024,512]{1,0:T(8,128)(2,1)S(1)} %bitcast.33, f32[1024,512]{1,0:T(8,128)S(1)} %fusion.4, bf16[1024,2304]{1,0:T(8,128)(2,1)} %copy-done.2, bf16[2304,512]{1,0:T(8,128)(2,1)S(1)} %bitcast.43, f32[512]{0:T(512)S(1)} %copy-done.7, f32[512]{0:T(512)S(1)} %copy-done.8), kind=kOutput, calls=%fused_computation.8 | convolution fusion | flops 2419580928 | bytes 10260480 | tf_op jit(solution)/shard_map/encode/dot_general | solution.py:225
  60.4 0.2 convolution_convert_fusion.1
  60.6 41.0 %all_gather.7.fresh_ref = bf16[256,768]{1,0:T(8,128)(2,1)S(1)} all-gather(bf16[16,768]{1,0:T(8,128)(2,1)S(1)} %convolution_convert_fusion.1), channel_id=1, replica_groups=mesh['enc'=32,'seq'=16] {'seq'}, dimensions={0}, use_global_device_ids=true | all-gather | bytes 417792 | tf_op jit(solution)/shard_map/fresh/all_gather | solution.py:284
  101.6 2.6 %all-gather.3.cloned.1.call-done = bf16[1,4096,768]{2,1,0:T(8,128)(2,1)} async-done(((bf16[1,256,768]{2,1,0:T(8,128)(2,1)}), bf16[1,4096,768]{2,1,0:T(8,128)(2,1)}) %all-gather.3.cloned.1.call-update) | async-done | bytes 6291472 | tf_op jit(solution)/shard_map/rows/all_gather | solution.py:250
  104.2 7.1 %head.1 = bf16[16,48,256]{2,1,0:T(8,128)(2,1)S(1)} custom-call(s32[256]{0:T(256)S(1)} %bitcast.29, s32[2]{0:T(128)S(1)} %pad_add_fusion.choice, bf16[4096,768]{1,0:T(8,128)(2,1)} %bitcast.30, bf16[256,768]{1,0:T(8,128)(2,1)S(1)} %all_gather.7.fresh_ref, bf16[768,256]{1,0:T(8,128)(2,1)S(1)} %concatenate.35.weight_ref), custom_call_target="tpu_custom_call" | custom-call | flops 1610612736 | tf_op jit(solution)/shard_map/head/pallas_call | solution.py:138
  111.3 31.7 %all_to_all.10 = bf16[16,48,256]{2,1,0:T(8,128)(2,1)S(1)} all-to-all(bf16[16,48,256]{2,1,0:T(8,128)(2,1)S(1)} %head.1), channel_id=1, replica_groups=mesh['enc'=32,'seq'=16] {'seq'}, dimensions={0} | all-to-all | bytes 786432 | tf_op jit(solution)/shard_map/out/all_to_all | solution.py:290
  143.1 1.3 fusion
  (31 shorter events, 0.7 us)
Async XLA Ops:
  6.5 136.6 %copy-start = (bf16[768,768]{1,0:T(8,128)(2,1)S(1)}, bf16[768,768]{1,0:T(8,128)(2,1)}, u32[]{:S(2)}) copy-start(bf16[768,768]{1,0:T(8,128)(2,1)} %param.18) | copy-start | bytes 3538948
  6.5 13.4 %copy-start.9 = (s32[16]{0:T(128)S(1)}, s32[16]{0:T(128)}, u32[]{:S(2)}) copy-start(s32[16]{0:T(128)} %param.19) | copy-start | bytes 196
  6.5 15.3 %copy-start.6 = (bf16[768,144]{0,1:T(8,128)(2,1)S(1)}, bf16[768,144]{0,1:T(8,128)(2,1)}, u32[]{:S(2)}) copy-start(bf16[768,144]{0,1:T(8,128)(2,1)} %param.17) | copy-start | bytes 663556
  6.5 16.5 %copy-start.4 = (bf16[1,16,8,8,512]{4,3,2,1,0:T(8,128)(2,1)S(1)}, bf16[1,16,8,8,512]{4,3,2,1,0:T(8,128)(2,1)}, u32[]{:S(2)}) copy-start(bf16[1,16,8,8,512]{4,3,2,1,0:T(8,128)(2,1)} %param.10) | copy-start | bytes 3145732
  6.5 97.6 %all-gather.3.cloned.1.call-start = ((), (), s32[]{:S(2)}) async-start(), calls=%async_computation.2 | async-start | bytes 6684672 | tf_op jit(solution)/shard_map/rows/all_gather | solution.py:250
  9.8 38.0 %all-to-all-start = ((bf16[16,144,512]{2,1,0:T(8,128)(2,1)}), bf16[16,144,512]{2,1,0:T(8,128)(2,1)}, u32[]{:S(2)}, u32[]{:S(2)}) async-start(bf16[16,144,512]{2,1,0:T(8,128)(2,1)} %broadcast_in_dim.8), calls=%async_computation | async-start | bytes 4718592 | tf_op jit(solution)/shard_map/encode/all_to_all | solution.py:205
  29.7 2.2 %copy-start.2 = (bf16[1024,2304]{1,0:T(8,128)(2,1)}, bf16[1024,2304]{1,0:T(8,128)(2,1)S(1)}, u32[]{:S(2)}) copy-start(bf16[1024,2304]{1,0:T(8,128)(2,1)S(1)} %get-tuple-element.17) | copy-start | bytes 14155780
  31.9 2.2 %copy-start.3 = (bf16[1024,2304]{1,0:T(8,128)(2,1)}, bf16[1024,2304]{1,0:T(8,128)(2,1)S(1)}, u32[]{:S(2)}) copy-start(bf16[1024,2304]{1,0:T(8,128)(2,1)S(1)} %get-tuple-element.15) | copy-start | bytes 14155780
  47.8 7.2 %collective-permute-start = (bf16[16,144,512]{2,1,0:T(8,128)(2,1)}, bf16[16,144,512]{2,1,0:T(8,128)(2,1)S(1)}, u32[]{:S(2)}, u32[]{:S(2)}) collective-permute-start(bf16[16,144,512]{2,1,0:T(8,128)(2,1)} %all-to-all-done), channel_id=1, source_target_pairs={{0,16},{16,0},{32,48},{48,32},{64,80},{80,64},{96,112},{112,96},{1... | collective-permute-start | bytes 7077896 | tf_op jit(solution)/shard_map/encode/ppermute | solution.py:221
  49.7 5.2 %copy-start.7 = (f32[512]{0:T(512)S(1)}, f32[512]{0:T(512)}, u32[]{:S(2)}) copy-start(f32[512]{0:T(512)} %param.13) | copy-start | bytes 6148
  49.7 5.2 %copy-start.8 = (f32[512]{0:T(512)S(1)}, f32[512]{0:T(512)}, u32[]{:S(2)}) copy-start(f32[512]{0:T(512)} %param.12) | copy-start | bytes 6148
  55.0 5.4 %copy-start.5 = (bf16[512,768]{1,0:T(8,128)(2,1)S(1)}, bf16[512,768]{1,0:T(8,128)(2,1)}, u32[]{:S(2)}) copy-start(bf16[512,768]{1,0:T(8,128)(2,1)} %param.14) | copy-start | bytes 2359300
  55.0 49.2 %copy-start.1 = (s32[1,256]{1,0:T(1,128)S(1)}, s32[1,256]{1,0:T(1,128)}, u32[]{:S(2)}) copy-start(s32[1,256]{1,0:T(1,128)} %param.15) | copy-start | bytes 3076
Sparse Core Ops, SparseCore 0:
  9.5 94.6 all-gather.2

commit v6 on v5

--- a/solution.py
+++ b/solution.py
@@ -12,7 +12,8 @@
 HEADS = 16
 WIDTH = E // HEADS
 SEGMENT = 512
-STEP_ROWS = 1024
+STEP_BLOCKS = 4
+TAIL = 16
 SCALE = WIDTH**-0.5 * math.log2(math.e)
 
 
@@ -90,28 +91,44 @@
 
 
 def head_kernel(
-    places, choice, rows_ref, fresh_ref, weight_ref, out_ref, table, fresh, held, arrived
+    places, choice, rows_ref, tail_ref, weight_ref, out_ref, table, fresh, held, arrived
 ):
-    chunks = held.shape[0]
-
-    def arrival(chunk):
-        first = pl.multiple_of(chunk * STEP_ROWS, STEP_ROWS)
-        return pltpu.make_async_copy(
-            rows_ref.at[pl.ds(first, STEP_ROWS)], held.at[chunk], arrived.at[chunk]
+    kept = rows_ref.shape[1]
+    tiles = fresh.shape[1] // held.shape[0]
+    loc = held.shape[1]
+    step_rows = STEP_BLOCKS * loc
+    chunks = held.shape[0] // STEP_BLOCKS
+
+    def arrivals(chunk):
+        blocks = pl.ds(chunk * STEP_BLOCKS, STEP_BLOCKS)
+        return (
+            pltpu.make_async_copy(
+                rows_ref.at[blocks], held.at[blocks, pl.ds(0, kept)], arrived.at[chunk, 0]
+            ),
+            pltpu.make_async_copy(
+                tail_ref.at[blocks, pl.ds(tiles, loc - kept)],
+                held.at[blocks, pl.ds(kept, loc - kept)],
+                arrived.at[chunk, 1],
+            ),
         )
 
     for chunk in range(chunks):
-        arrival(chunk).start()
-    made_fresh = jnp.dot(fresh_ref[...], weight_ref[...], preferred_element_type=jnp.float32)
+        for copy in arrivals(chunk):
+            copy.start()
+    made_fresh = jnp.dot(
+        tail_ref[:, :tiles, :].reshape(-1, E), weight_ref[...], preferred_element_type=jnp.float32
+    )
     made_fresh = made_fresh.astype(jnp.bfloat16).astype(jnp.float32)
     fresh[0] = made_fresh[:, :128]
     fresh[1] = made_fresh[:, 128:]
 
     def project(chunk, carry):
-        arrival(chunk).wait()
-        made = jnp.dot(held[chunk], weight_ref[...], preferred_element_type=jnp.float32)
+        for copy in arrivals(chunk):
+            copy.wait()
+        rows = held[pl.ds(chunk * STEP_BLOCKS, STEP_BLOCKS)].reshape(step_rows, E)
+        made = jnp.dot(rows, weight_ref[...], preferred_element_type=jnp.float32)
         made = made.astype(jnp.bfloat16).astype(jnp.float32)
-        block = pl.ds(pl.multiple_of(chunk * STEP_ROWS, STEP_ROWS), STEP_ROWS)
+        block = pl.ds(pl.multiple_of(chunk * step_rows, step_rows), step_rows)
         table[0, block, :] = made[:, :128]
         table[1, block, :] = made[:, 128:]
         return carry
@@ -131,13 +148,13 @@
         pl.when(choice[0] == rate)(partial(attend, rate, choice[1], table, out_ref))
 
 
-def head_attention(places, choice, rows, fresh, weight, seq_count):
-    length = rows.shape[0]
-    loc = length // seq_count
-    chunks = length // STEP_ROWS
+def head_attention(places, choice, rows, tail, weight, loc):
+    blocks = rows.shape[0]
+    length = blocks * loc
+    new_rows = blocks * (tail.shape[1] - (loc - rows.shape[1]))
     return pl.pallas_call(
         head_kernel,
-        out_shape=jax.ShapeDtypeStruct((seq_count, WIDTH, loc), jnp.bfloat16),
+        out_shape=jax.ShapeDtypeStruct((blocks, WIDTH, loc), jnp.bfloat16),
         in_specs=[
             pl.BlockSpec(memory_space=pltpu.SMEM),
             pl.BlockSpec(memory_space=pltpu.SMEM),
@@ -148,15 +165,15 @@
         out_specs=pl.BlockSpec(memory_space=pltpu.VMEM),
         scratch_shapes=[
             pltpu.VMEM((2, length, 128), jnp.float32),
-            pltpu.VMEM((2, fresh.shape[0], 128), jnp.float32),
-            pltpu.VMEM((chunks, STEP_ROWS, E), jnp.bfloat16),
-            pltpu.SemaphoreType.DMA((chunks,)),
+            pltpu.VMEM((2, new_rows, 128), jnp.float32),
+            pltpu.VMEM((blocks, loc, E), jnp.bfloat16),
+            pltpu.SemaphoreType.DMA((blocks // STEP_BLOCKS, 2)),
         ],
         compiler_params=pltpu.CompilerParams(vmem_limit_bytes=48 * 1024 * 1024),
         cost_estimate=pl.CostEstimate(
             flops=2 * length * E * 256, bytes_accessed=0, transcendentals=0
         ),
-    )(places, choice, rows, fresh, weight)
+    )(places, choice, rows, tail, weight)
 
 
 def regroup_kernel(shard, core, columns_ref, own_ref, other_ref):
@@ -243,11 +260,11 @@
     tile_count = tile_maps.shape[1]
     side_len = tile_maps.shape[2]
     channels = tile_maps.shape[4]
-    seq_count = lax.axis_size("seq")
     my_index = lax.axis_index("seq")
 
     with jax.named_scope("rows"):
-        rows = lax.all_gather(slide_cache[0], "seq", axis=0, tiled=True)
+        loc = slide_cache.shape[1]
+        rows = lax.all_gather(slide_cache[0, : loc - TAIL], "seq", axis=0, tiled=False)
 
     with jax.named_scope("choice"):
         gap = jnp.zeros((E, 16), jnp.bfloat16)
@@ -281,10 +298,11 @@
         )
 
     with jax.named_scope("fresh"):
-        fresh = lax.all_gather(embedded, "seq", axis=0, tiled=True)
+        tail = jnp.concatenate([embedded, slide_cache[0, loc - TAIL :]], axis=0)
+        tail = lax.all_gather(tail, "seq", axis=0, tiled=False)
 
     with jax.named_scope("head"):
-        head_out = head_attention(positions[0], choice, rows, fresh, head_weight, seq_count)
+        head_out = head_attention(positions[0], choice, rows, tail, head_weight, loc)
 
     with jax.named_scope("out"):
         gathered = lax.all_to_all(head_out, "seq", split_axis=0, concat_axis=0, tiled=True)

time: 152 us -> 154 us (1.013)
  waiting for transfers between devices: 14.9 us -> 11.6 us
  local copies, waits for them, and re-layouts: 12.4 us -> 15.1 us
  blocking collectives: 72.7 us -> 75.3 us
    all_gather x1, blocking collectives: 41 us -> 45.2 us  [shards(): tail = lax.all_gather(tail, 'seq', axis=0, tiled=False)]
    all_gather x1, waiting for transfers between devices: 2.59 us -> 0.01 us  [shards(): lax.all_gather(slide_cache[0, :loc - TAIL], 'seq', axis=0, tiled=False)]
    slice x0 -> x1, local copies, waits for them, and re-layouts: none -> 1.9 us  [shards(): slide_cache[0, :loc - TAIL]]
    all_to_all x1, blocking collectives: 31.7 us -> 30.1 us  [shards(): lax.all_to_all(head_out, 'seq', split_axis=0, concat_axis=0, tiled=True)]
  transfers between devices with their start and end apart: 3 -> 3, of which waited for: 2 -> 1; matrix products, arithmetic and copies ran while one was open for 13% -> 13% of each run, Pallas kernels for 3% -> 3%
where the time goes in v6:
time: 154 us; the launch traced here: 153 us
  blocking collectives  75.3 us (49%)
  local copies, waits for them, and re-layouts  15.1 us (10%)
  between operations  14.9 us (10%)
  starting transfers between devices  12.1 us (8%)
  matrix products  12 us (8%)
  waiting for transfers between devices  11.6 us (8%)
  Pallas kernels  11.3 us (7%)
    all_gather x1, blocking collectives, shards(): tail = lax.all_gather(tail, 'seq', axis=0, tiled=False)  45.2 us
    all_to_all x1, blocking collectives, shards(): lax.all_to_all(head_out, 'seq', split_axis=0, concat_axis=0, tiled=True)  30.1 us
    all_to_all x1, waiting for transfers between devices, spread_to(): lax.all_to_all(copies, axis, split_axis=0, concat_axis=0, tiled=True, axi...  11.6 us
    all_to_all x1, starting transfers between devices, spread_to(): lax.all_to_all(copies, axis, split_axis=0, concat_axis=0, tiled=True, axi...  10.1 us
    pallas_call x1, Pallas kernels, head_attention(): pl.pallas_call(head_kernel, out_shape=jax.ShapeDtypeStruct((blocks, WIDTH...  7.07 us
    unnamed x31, local copies, waits for them, and re-layouts  6.17 us
    dot_general x1, matrix products, convolve(): jnp.dot(other_columns, other.reshape(-1, channels), preferred_element_typ...  5.34 us
    dot_general x1, matrix products, convolve(): jnp.dot(own_columns, own.reshape(-1, channels), preferred_element_type=jn...  5.21 us
  transfers between devices with their start and end apart: 3, of which 1 were waited for; matrix products, arithmetic and copies ran while one was open for 13% of the time, Pallas kernels for 3%

profile of v6, /device:TPU:6, one launch (start us, length us, event | category | flops | bytes accessed | tf_op | source)
XLA Modules:
  0.0 153.0 jit_solution(15085853561380671078)
XLA Ops:
  6.6 1.9 %slice.39 = bf16[1,240,768]{2,1,0:T(8,128)(2,1)} slice(bf16[1,256,768]{2,1,0:T(8,128)(2,1)} %param.16), slice={[0:1], [0:240], [0:768]} | slice | bytes 737280 | tf_op jit(solution)/shard_map/rows/slice | solution.py:267
  8.5 2.5 %broadcast_in_dim.8 = bf16[16,144,512]{2,1,0:T(8,128)(2,1)} broadcast(bf16[144,512]{1,0:T(8,128)(2,1)} %param.11), dimensions={1,2} | broadcast | bytes 2506752 | tf_op jit(solution)/shard_map/encode/broadcast_in_dim | solution.py:221
  11.0 10.1 %all-to-all-start = ((bf16[16,144,512]{2,1,0:T(8,128)(2,1)}), bf16[16,144,512]{2,1,0:T(8,128)(2,1)}, u32[]{:S(2)}, u32[]{:S(2)}) async-start(bf16[16,144,512]{2,1,0:T(8,128)(2,1)} %broadcast_in_dim.8), calls=%async_computation | async-start | bytes 4718592 | tf_op jit(solution)/shard_map/encode/all_to_all | solution.py:222
  21.2 0.6 dynamic_slice.3
  23.1 0.2 copy.17
  23.3 0.2 copy.18
  23.5 0.8 copy.19
  24.3 1.6 %pad_slice_fusion = (bf16[16,8,8,512]{3,2,1,0:T(8,128)(2,1)S(1)}, bf16[16,8,8,512]{3,2,1,0:T(8,128)(2,1)S(1)}, bf16[16,8,8,512]{3,2,1,0:T(8,128)(2,1)S(1)}, bf16...) fusion(bf16[16,8,8,512]{3,2,1,0:T(8,128)(2,1)S(1)} %bitcast.33), kind=kLoop, calls=%fused_computation | loop fusion | bytes 9437184 | tf_op jit(solution)/shard_map/encode/slice | solution.py:282
  26.0 0.1 constant_dynamic-update-slice_fusion.7
  26.6 4.3 %encode.1 = (bf16[1024,2304]{1,0:T(8,128)(2,1)S(1)}, bf16[1024,2304]{1,0:T(8,128)(2,1)S(1)}) custom-call(s32[1]{0:T(128)} %bitcast.1.core, bf16[1024,4608]{1,0:T(8,128)(2,1)S(1)} %constant_dynamic-update-slice_fusion.columns_ref), custom_call_target="tpu_custom_call" | custom-call | bytes 18874368 | tf_op jit(solution)/shard_map/encode/pallas_call | solution.py:204
  30.9 2.2 %copy-done.2 = bf16[1024,2304]{1,0:T(8,128)(2,1)} copy-done((bf16[1024,2304]{1,0:T(8,128)(2,1)}, bf16[1024,2304]{1,0:T(8,128)(2,1)S(1)}, u32[]{:S(2)}) %copy-start.2) | copy-done | bytes 4718616
  33.1 2.2 %copy-done.3 = bf16[1024,2304]{1,0:T(8,128)(2,1)} copy-done((bf16[1024,2304]{1,0:T(8,128)(2,1)}, bf16[1024,2304]{1,0:T(8,128)(2,1)S(1)}, u32[]{:S(2)}) %copy-start.3) | copy-done | bytes 4718616
  35.4 1.4 concatenate.38.weight_ref
  36.8 0.7 pad_add_fusion.choice
  37.4 11.6 %all-to-all-done = bf16[16,144,512]{2,1,0:T(8,128)(2,1)} async-done(((bf16[16,144,512]{2,1,0:T(8,128)(2,1)}), bf16[16,144,512]{2,1,0:T(8,128)(2,1)}, u32[]{:S(2)}, u32[]{:S(2)}) %all-to-all-start) | async-done | bytes 2359328 | tf_op jit(solution)/shard_map/encode/all_to_all | solution.py:222
  49.0 1.9 %collective-permute-start = (bf16[16,144,512]{2,1,0:T(8,128)(2,1)}, bf16[16,144,512]{2,1,0:T(8,128)(2,1)S(1)}, u32[]{:S(2)}, u32[]{:S(2)}) collective-permute-start(bf16[16,144,512]{2,1,0:T(8,128)(2,1)} %all-to-all-done), channel_id=1, source_target_pairs={{0,16},{16,0},{32,48},{48,32},{64,80},{80,64},{96,112},{112,96},{1... | collective-permute-start | bytes 7077896 | tf_op jit(solution)/shard_map/encode/ppermute | solution.py:238
  50.9 0.7 slice_bitcast_fusion
  51.7 5.2 %fusion.4 = f32[1024,512]{1,0:T(8,128)S(1)} fusion(bf16[1024,2304]{1,0:T(8,128)(2,1)} %copy-done.3, bf16[2304,512]{1,0:T(8,128)(2,1)} %bitcast.14), kind=kOutput, calls=%fused_computation.29 | convolution fusion | flops 2415919104 | bytes 9175040 | tf_op jit(solution)/shard_map/encode/dot_general | solution.py:239
  57.0 5.3 %bitcast_reduce_fusion = f32[16,512]{1,0:T(8,128)S(1)} fusion(bf16[1024,512]{1,0:T(8,128)(2,1)S(1)} %bitcast.35, f32[1024,512]{1,0:T(8,128)S(1)} %fusion.4, bf16[1024,2304]{1,0:T(8,128)(2,1)} %copy-done.2, bf16[2304,512]{1,0:T(8,128)(2,1)S(1)} %bitcast.45, f32[512]{0:T(512)S(1)} %copy-done.7, f32[512]{0:T(512)S(1)} %copy-done.8), kind=kOutput, calls=%fused_computation.8 | convolution fusion | flops 2419580928 | bytes 10260480 | tf_op jit(solution)/shard_map/encode/dot_general | solution.py:242
  62.3 0.2 convolution_convert_fusion.1
  62.5 45.2 %all-gather = bf16[512,768]{1,0:T(8,128)(2,1)S(1)} all-gather(bf16[32,768]{1,0:T(8,128)(2,1)S(1)} %pad_maximum_fusion), channel_id=2, replica_groups=mesh['enc'=32,'seq'=16] {'seq'}, dimensions={0}, use_global_device_ids=true | all-gather | bytes 835584 | tf_op jit(solution)/shard_map/fresh/all_gather | solution.py:302
  107.8 7.1 %head.1 = bf16[16,48,256]{2,1,0:T(8,128)(2,1)S(1)} custom-call(s32[256]{0:T(256)S(1)} %bitcast.32, s32[2]{0:T(128)S(1)} %pad_add_fusion.choice, bf16[16,240,768]{2,1,0:T(8,128)(2,1)} %all-gather.3.cloned.1.call-done.rows_ref, bf16[16,32,768]{2,1,0:T(8,128)(2,1)S(1)} %bitcast.31, bf16[768,256]{1,0:T(8,128)(2,1)S(1)} %concatenate.38.weight_ref), custom_call_target="tpu_custom_call" | custom-call | flops 1610612736 | tf_op jit(solution)/shard_map/head/pallas_call | solution.py:155
  114.9 30.1 %all_to_all.10 = bf16[16,48,256]{2,1,0:T(8,128)(2,1)S(1)} all-to-all(bf16[16,48,256]{2,1,0:T(8,128)(2,1)S(1)} %head.1), channel_id=1, replica_groups=mesh['enc'=32,'seq'=16] {'seq'}, dimensions={0} | all-to-all | bytes 786432 | tf_op jit(solution)/shard_map/out/all_to_all | solution.py:308
  144.9 1.3 fusion
  (34 shorter events, 0.7 us)
Async XLA Ops:
  6.5 138.4 %copy-start = (bf16[768,768]{1,0:T(8,128)(2,1)S(1)}, bf16[768,768]{1,0:T(8,128)(2,1)}, u32[]{:S(2)}) copy-start(bf16[768,768]{1,0:T(8,128)(2,1)} %param.18) | copy-start | bytes 3538948
  6.5 14.6 %copy-start.9 = (s32[16]{0:T(128)S(1)}, s32[16]{0:T(128)}, u32[]{:S(2)}) copy-start(s32[16]{0:T(128)} %param.19) | copy-start | bytes 196
  6.5 16.5 %copy-start.6 = (bf16[768,144]{0,1:T(8,128)(2,1)S(1)}, bf16[768,144]{0,1:T(8,128)(2,1)}, u32[]{:S(2)}) copy-start(bf16[768,144]{0,1:T(8,128)(2,1)} %param.17) | copy-start | bytes 663556
  6.5 17.7 %copy-start.4 = (bf16[1,16,8,8,512]{4,3,2,1,0:T(8,128)(2,1)S(1)}, bf16[1,16,8,8,512]{4,3,2,1,0:T(8,128)(2,1)}, u32[]{:S(2)}) copy-start(bf16[1,16,8,8,512]{4,3,2,1,0:T(8,128)(2,1)} %param.10) | copy-start | bytes 3145732
  6.5 101.2 %all-gather.3.cloned.1.call-start = ((), (), s32[]{:S(2)}) async-start(), calls=%async_computation.2 | async-start | bytes 6266880 | tf_op jit(solution)/shard_map/rows/all_gather | solution.py:267
  11.0 38.0 %all-to-all-start = ((bf16[16,144,512]{2,1,0:T(8,128)(2,1)}), bf16[16,144,512]{2,1,0:T(8,128)(2,1)}, u32[]{:S(2)}, u32[]{:S(2)}) async-start(bf16[16,144,512]{2,1,0:T(8,128)(2,1)} %broadcast_in_dim.8), calls=%async_computation | async-start | bytes 4718592 | tf_op jit(solution)/shard_map/encode/all_to_all | solution.py:222
  30.9 2.2 %copy-start.2 = (bf16[1024,2304]{1,0:T(8,128)(2,1)}, bf16[1024,2304]{1,0:T(8,128)(2,1)S(1)}, u32[]{:S(2)}) copy-start(bf16[1024,2304]{1,0:T(8,128)(2,1)S(1)} %get-tuple-element.17) | copy-start | bytes 14155780
  33.1 2.2 %copy-start.3 = (bf16[1024,2304]{1,0:T(8,128)(2,1)}, bf16[1024,2304]{1,0:T(8,128)(2,1)S(1)}, u32[]{:S(2)}) copy-start(bf16[1024,2304]{1,0:T(8,128)(2,1)S(1)} %get-tuple-element.15) | copy-start | bytes 14155780
  49.0 7.9 %collective-permute-start = (bf16[16,144,512]{2,1,0:T(8,128)(2,1)}, bf16[16,144,512]{2,1,0:T(8,128)(2,1)S(1)}, u32[]{:S(2)}, u32[]{:S(2)}) collective-permute-start(bf16[16,144,512]{2,1,0:T(8,128)(2,1)} %all-to-all-done), channel_id=1, source_target_pairs={{0,16},{16,0},{32,48},{48,32},{64,80},{80,64},{96,112},{112,96},{1... | collective-permute-start | bytes 7077896 | tf_op jit(solution)/shard_map/encode/ppermute | solution.py:238
  51.7 5.2 %copy-start.7 = (f32[512]{0:T(512)S(1)}, f32[512]{0:T(512)}, u32[]{:S(2)}) copy-start(f32[512]{0:T(512)} %param.13) | copy-start | bytes 6148
  51.7 5.2 %copy-start.8 = (f32[512]{0:T(512)S(1)}, f32[512]{0:T(512)}, u32[]{:S(2)}) copy-start(f32[512]{0:T(512)} %param.12) | copy-start | bytes 6148
  56.9 5.4 %copy-start.5 = (bf16[512,768]{1,0:T(8,128)(2,1)S(1)}, bf16[512,768]{1,0:T(8,128)(2,1)}, u32[]{:S(2)}) copy-start(bf16[512,768]{1,0:T(8,128)(2,1)} %param.14) | copy-start | bytes 2359300
  57.0 50.8 %copy-start.1 = (s32[1,256]{1,0:T(1,128)S(1)}, s32[1,256]{1,0:T(1,128)}, u32[]{:S(2)}) copy-start(s32[1,256]{1,0:T(1,128)} %param.15) | copy-start | bytes 3076
Sparse Core Ops, SparseCore 0:
  9.5 94.5 all-gather.2

commit v7 on v5

--- a/solution.py
+++ b/solution.py
@@ -276,12 +276,9 @@
         pooled = jnp.mean(
             activated.reshape(tile_count, side_len * side_len, channels), axis=1
         ).astype(jnp.bfloat16)
-        embedded = jnp.dot(pooled, tile_proj, preferred_element_type=jnp.float32).astype(
-            jnp.bfloat16
-        )
-
     with jax.named_scope("fresh"):
-        fresh = lax.all_gather(embedded, "seq", axis=0, tiled=True)
+        pooled = lax.all_gather(pooled, "seq", axis=0, tiled=True)
+        fresh = jnp.dot(pooled, tile_proj, preferred_element_type=jnp.float32).astype(jnp.bfloat16)
 
     with jax.named_scope("head"):
         head_out = head_attention(positions[0], choice, rows, fresh, head_weight, seq_count)

time: 152 us -> 149 us (0.980)
  blocking collectives: 72.7 us -> 69.1 us
    all_gather x1, blocking collectives: 41 us -> 38.6 us  [shards(): pooled = lax.all_gather(pooled, 'seq', axis=0, tiled=True)]
where the time goes in v7:
time: 149 us
  blocking collectives  69.1 us (46%)
  waiting for transfers between devices  15.9 us (11%)
  between operations  14.9 us (10%)
  local copies, waits for them, and re-layouts  12.4 us (8%)
  matrix products  12.2 us (8%)
  starting transfers between devices  12.1 us (8%)
  Pallas kernels  11.4 us (8%)
    all_gather x1, blocking collectives, shards(): pooled = lax.all_gather(pooled, 'seq', axis=0, tiled=True)  38.6 us
    all_to_all x1, blocking collectives, shards(): lax.all_to_all(head_out, 'seq', split_axis=0, concat_axis=0, tiled=True)  30.5 us
    all_to_all x1, waiting for transfers between devices, spread_to(): lax.all_to_all(copies, axis, split_axis=0, concat_axis=0, tiled=True, axi...  11.6 us
    all_to_all x1, starting transfers between devices, spread_to(): lax.all_to_all(copies, axis, split_axis=0, concat_axis=0, tiled=True, axi...  10.1 us
    pallas_call x1, Pallas kernels, head_attention(): pl.pallas_call(head_kernel, out_shape=jax.ShapeDtypeStruct((seq_count, WI...  7.14 us
    unnamed x31, local copies, waits for them, and re-layouts  6.15 us
    dot_general x1, matrix products, convolve(): jnp.dot(other_columns, other.reshape(-1, channels), preferred_element_typ...  5.36 us
    dot_general x1, matrix products, convolve(): jnp.dot(own_columns, own.reshape(-1, channels), preferred_element_type=jn...  5.2 us
  transfers between devices with their start and end apart: 3, of which 2 were waited for; matrix products, arithmetic and copies ran while one was open for 13% of the time, Pallas kernels for 3%

profile of v7, /device:TPU:6, one launch (start us, length us, event | category | flops | bytes accessed | tf_op | source)
XLA Modules:
  0.0 148.8 jit_solution(16010794357206202640)
XLA Ops:
  6.6 0.7 all-gather.3.cloned.1.call-update
  7.3 2.5 %broadcast_in_dim.8 = bf16[16,144,512]{2,1,0:T(8,128)(2,1)} broadcast(bf16[144,512]{1,0:T(8,128)(2,1)} %param.11), dimensions={1,2} | broadcast | bytes 2506752 | tf_op jit(solution)/shard_map/encode/broadcast_in_dim | solution.py:204
  9.8 10.1 %all-to-all-start = ((bf16[16,144,512]{2,1,0:T(8,128)(2,1)}), bf16[16,144,512]{2,1,0:T(8,128)(2,1)}, u32[]{:S(2)}, u32[]{:S(2)}) async-start(bf16[16,144,512]{2,1,0:T(8,128)(2,1)} %broadcast_in_dim.8), calls=%async_computation | async-start | bytes 4718592 | tf_op jit(solution)/shard_map/encode/all_to_all | solution.py:205
  19.9 0.6 dynamic_slice.3
  21.9 0.2 copy.14
  22.1 0.2 copy.15
  22.2 0.8 copy.16
  23.1 1.6 %pad_slice_fusion = (bf16[16,8,8,512]{3,2,1,0:T(8,128)(2,1)S(1)}, bf16[16,8,8,512]{3,2,1,0:T(8,128)(2,1)S(1)}, bf16[16,8,8,512]{3,2,1,0:T(8,128)(2,1)S(1)}, bf16...) fusion(bf16[16,8,8,512]{3,2,1,0:T(8,128)(2,1)S(1)} %bitcast.32), kind=kLoop, calls=%fused_computation | loop fusion | bytes 9437184 | tf_op jit(solution)/shard_map/encode/slice | solution.py:265
  24.8 0.1 constant_dynamic-update-slice_fusion.7
  25.4 4.3 %encode.1 = (bf16[1024,2304]{1,0:T(8,128)(2,1)S(1)}, bf16[1024,2304]{1,0:T(8,128)(2,1)S(1)}) custom-call(s32[1]{0:T(128)} %bitcast.1.core, bf16[1024,4608]{1,0:T(8,128)(2,1)S(1)} %constant_dynamic-update-slice_fusion.columns_ref), custom_call_target="tpu_custom_call" | custom-call | bytes 18874368 | tf_op jit(solution)/shard_map/encode/pallas_call | solution.py:187
  29.7 2.2 %copy-done.2 = bf16[1024,2304]{1,0:T(8,128)(2,1)} copy-done((bf16[1024,2304]{1,0:T(8,128)(2,1)}, bf16[1024,2304]{1,0:T(8,128)(2,1)S(1)}, u32[]{:S(2)}) %copy-start.2) | copy-done | bytes 4718616
  31.9 2.2 %copy-done.3 = bf16[1024,2304]{1,0:T(8,128)(2,1)} copy-done((bf16[1024,2304]{1,0:T(8,128)(2,1)}, bf16[1024,2304]{1,0:T(8,128)(2,1)S(1)}, u32[]{:S(2)}) %copy-start.3) | copy-done | bytes 4718616
  34.1 1.4 concatenate.35.weight_ref
  35.5 0.7 pad_add_fusion.choice
  36.2 11.6 %all-to-all-done = bf16[16,144,512]{2,1,0:T(8,128)(2,1)} async-done(((bf16[16,144,512]{2,1,0:T(8,128)(2,1)}), bf16[16,144,512]{2,1,0:T(8,128)(2,1)}, u32[]{:S(2)}, u32[]{:S(2)}) %all-to-all-start) | async-done | bytes 2359328 | tf_op jit(solution)/shard_map/encode/all_to_all | solution.py:205
  47.8 1.9 %collective-permute-start = (bf16[16,144,512]{2,1,0:T(8,128)(2,1)}, bf16[16,144,512]{2,1,0:T(8,128)(2,1)S(1)}, u32[]{:S(2)}, u32[]{:S(2)}) collective-permute-start(bf16[16,144,512]{2,1,0:T(8,128)(2,1)} %all-to-all-done), channel_id=1, source_target_pairs={{0,16},{16,0},{32,48},{48,32},{64,80},{80,64},{96,112},{112,96},{1... | collective-permute-start | bytes 7077896 | tf_op jit(solution)/shard_map/encode/ppermute | solution.py:221
  49.7 5.2 %fusion.2 = f32[1024,512]{1,0:T(8,128)S(1)} fusion(bf16[1024,2304]{1,0:T(8,128)(2,1)} %copy-done.3, bf16[2304,512]{1,0:T(8,128)(2,1)} %bitcast.15), kind=kOutput, calls=%fused_computation.25 | convolution fusion | flops 2415919104 | bytes 9175040 | tf_op jit(solution)/shard_map/encode/dot_general | solution.py:222
  55.0 5.4 %bitcast_reduce_fusion = f32[16,512]{1,0:T(8,128)S(1)} fusion(bf16[1024,512]{1,0:T(8,128)(2,1)S(1)} %bitcast.34, f32[1024,512]{1,0:T(8,128)S(1)} %fusion.2, bf16[1024,2304]{1,0:T(8,128)(2,1)} %copy-done.2, bf16[2304,512]{1,0:T(8,128)(2,1)S(1)} %bitcast.44, f32[512]{0:T(512)S(1)} %copy-done.7, f32[512]{0:T(512)S(1)} %copy-done.8), kind=kOutput, calls=%fused_computation.8 | convolution fusion | flops 2419580928 | bytes 10260480 | tf_op jit(solution)/shard_map/encode/dot_general | solution.py:225
  60.4 38.6 %all_gather.7 = bf16[256,512]{1,0:T(8,128)(2,1)S(1)} all-gather(bf16[16,512]{1,0:T(8,128)(2,1)S(1)} %multiply_convert_fusion), channel_id=1, replica_groups=mesh['enc'=32,'seq'=16] {'seq'}, dimensions={0}, use_global_device_ids=true | all-gather | bytes 278528 | tf_op jit(solution)/shard_map/fresh/all_gather | solution.py:280
  99.0 0.4 convolution_convert_fusion.1.fresh_ref
  99.4 3.7 %all-gather.3.cloned.1.call-done = bf16[1,4096,768]{2,1,0:T(8,128)(2,1)} async-done(((bf16[1,256,768]{2,1,0:T(8,128)(2,1)}), bf16[1,4096,768]{2,1,0:T(8,128)(2,1)}) %all-gather.3.cloned.1.call-update) | async-done | bytes 6291472 | tf_op jit(solution)/shard_map/rows/all_gather | solution.py:250
  103.0 7.1 %head.1 = bf16[16,48,256]{2,1,0:T(8,128)(2,1)S(1)} custom-call(s32[256]{0:T(256)S(1)} %bitcast.30, s32[2]{0:T(128)S(1)} %pad_add_fusion.choice, bf16[4096,768]{1,0:T(8,128)(2,1)} %bitcast.31, bf16[256,768]{1,0:T(8,128)(2,1)S(1)} %convolution_convert_fusion.1.fresh_ref, bf16[768,256]{1,0:T(8,128)(2,1)S(1)} %concatenate.35.weight_ref), custom_call_target="tpu_custom_call" | custom-call | flops 1610612736 | tf_op jit(solution)/shard_map/head/pallas_call | solution.py:138
  110.2 30.5 %all_to_all.10 = bf16[16,48,256]{2,1,0:T(8,128)(2,1)S(1)} all-to-all(bf16[16,48,256]{2,1,0:T(8,128)(2,1)S(1)} %head.1), channel_id=1, replica_groups=mesh['enc'=32,'seq'=16] {'seq'}, dimensions={0} | all-to-all | bytes 786432 | tf_op jit(solution)/shard_map/out/all_to_all | solution.py:287
  140.7 1.3 fusion
  (32 shorter events, 0.7 us)
Async XLA Ops:
  6.5 134.2 %copy-start = (bf16[768,768]{1,0:T(8,128)(2,1)S(1)}, bf16[768,768]{1,0:T(8,128)(2,1)}, u32[]{:S(2)}) copy-start(bf16[768,768]{1,0:T(8,128)(2,1)} %param.18) | copy-start | bytes 3538948
  6.5 13.4 %copy-start.9 = (s32[16]{0:T(128)S(1)}, s32[16]{0:T(128)}, u32[]{:S(2)}) copy-start(s32[16]{0:T(128)} %param.19) | copy-start | bytes 196
  6.5 15.3 %copy-start.6 = (bf16[768,144]{0,1:T(8,128)(2,1)S(1)}, bf16[768,144]{0,1:T(8,128)(2,1)}, u32[]{:S(2)}) copy-start(bf16[768,144]{0,1:T(8,128)(2,1)} %param.17) | copy-start | bytes 663556
  6.5 16.5 %copy-start.4 = (bf16[1,16,8,8,512]{4,3,2,1,0:T(8,128)(2,1)S(1)}, bf16[1,16,8,8,512]{4,3,2,1,0:T(8,128)(2,1)}, u32[]{:S(2)}) copy-start(bf16[1,16,8,8,512]{4,3,2,1,0:T(8,128)(2,1)} %param.10) | copy-start | bytes 3145732
  6.5 96.5 %all-gather.3.cloned.1.call-start = ((), (), s32[]{:S(2)}) async-start(), calls=%async_computation.2 | async-start | bytes 6684672 | tf_op jit(solution)/shard_map/rows/all_gather | solution.py:250
  9.8 38.0 %all-to-all-start = ((bf16[16,144,512]{2,1,0:T(8,128)(2,1)}), bf16[16,144,512]{2,1,0:T(8,128)(2,1)}, u32[]{:S(2)}, u32[]{:S(2)}) async-start(bf16[16,144,512]{2,1,0:T(8,128)(2,1)} %broadcast_in_dim.8), calls=%async_computation | async-start | bytes 4718592 | tf_op jit(solution)/shard_map/encode/all_to_all | solution.py:205
  29.7 2.2 %copy-start.2 = (bf16[1024,2304]{1,0:T(8,128)(2,1)}, bf16[1024,2304]{1,0:T(8,128)(2,1)S(1)}, u32[]{:S(2)}) copy-start(bf16[1024,2304]{1,0:T(8,128)(2,1)S(1)} %get-tuple-element.17) | copy-start | bytes 14155780
  31.9 2.2 %copy-start.3 = (bf16[1024,2304]{1,0:T(8,128)(2,1)}, bf16[1024,2304]{1,0:T(8,128)(2,1)S(1)}, u32[]{:S(2)}) copy-start(bf16[1024,2304]{1,0:T(8,128)(2,1)S(1)} %get-tuple-element.15) | copy-start | bytes 14155780
  47.8 7.2 %collective-permute-start = (bf16[16,144,512]{2,1,0:T(8,128)(2,1)}, bf16[16,144,512]{2,1,0:T(8,128)(2,1)S(1)}, u32[]{:S(2)}, u32[]{:S(2)}) collective-permute-start(bf16[16,144,512]{2,1,0:T(8,128)(2,1)} %all-to-all-done), channel_id=1, source_target_pairs={{0,16},{16,0},{32,48},{48,32},{64,80},{80,64},{96,112},{112,96},{1... | collective-permute-start | bytes 7077896 | tf_op jit(solution)/shard_map/encode/ppermute | solution.py:221
  49.7 5.2 %copy-start.7 = (f32[512]{0:T(512)S(1)}, f32[512]{0:T(512)}, u32[]{:S(2)}) copy-start(f32[512]{0:T(512)} %param.13) | copy-start | bytes 6148
  49.7 5.2 %copy-start.8 = (f32[512]{0:T(512)S(1)}, f32[512]{0:T(512)}, u32[]{:S(2)}) copy-start(f32[512]{0:T(512)} %param.12) | copy-start | bytes 6148
  55.0 44.0 %copy-start.5 = (bf16[512,768]{1,0:T(8,128)(2,1)S(1)}, bf16[512,768]{1,0:T(8,128)(2,1)}, u32[]{:S(2)}) copy-start(bf16[512,768]{1,0:T(8,128)(2,1)} %param.14) | copy-start | bytes 2359300
  55.0 48.0 %copy-start.1 = (s32[1,256]{1,0:T(1,128)S(1)}, s32[1,256]{1,0:T(1,128)}, u32[]{:S(2)}) copy-start(s32[1,256]{1,0:T(1,128)} %param.15) | copy-start | bytes 3076
Sparse Core Ops, SparseCore 0:
  9.5 93.5 all-gather.2

commit v8 on v7

--- a/solution.py
+++ b/solution.py
@@ -40,7 +40,7 @@
         queries, keys, _ = loaded
         return lax.dot_general(
             keys,
-            queries[part * 512 : (part + 1) * 512],
+            queries[part * 256 : (part + 1) * 256],
             (((1,), (1,)), ((), ())),
             preferred_element_type=jnp.float32,
         )
@@ -53,35 +53,35 @@
         )
         result = (mixed[64:112] / mixed[112:113]).astype(jnp.bfloat16)
         if rate == 1:
-            for block in range(512 // loc):
-                out_ref[index * (SEGMENT // loc) + part * (512 // loc) + block] = result[
+            for block in range(256 // loc):
+                out_ref[index * (SEGMENT // loc) + part * (256 // loc) + block] = result[
                     :, block * loc : (block + 1) * loc
                 ]
             return
         blocks = 128 * rate // loc
-        for piece in range(512 // 128):
+        for piece in range(256 // 128):
             wide = jnp.dot(
                 result[:, piece * 128 : (piece + 1) * 128],
                 spread,
                 preferred_element_type=jnp.float32,
             ).astype(jnp.bfloat16)
-            first = (index * 4 + part * (512 // 128) + piece) * blocks
+            first = (index * 4 + part * (256 // 128) + piece) * blocks
             for block in range(blocks):
                 out_ref[first + block] = wide[:, block * loc : (block + 1) * loc]
 
     segments = length // (SEGMENT * rate)
-    together = min(segments, 4)
+    together = min(segments, 8)
 
     def group(step, carry):
         work = []
         for inner in range(together):
             index = step * together + inner
             loaded = load(index)
-            work += [(index, part, loaded) for part in range(SEGMENT // 512)]
-        ahead = [score(loaded, part) for _, part, loaded in work[:1]]
+            work += [(index, part, loaded) for part in range(SEGMENT // 256)]
+        ahead = [score(loaded, part) for _, part, loaded in work[:3]]
         for number, (index, part, loaded) in enumerate(work):
-            if number + 1 < len(work):
-                _, next_part, next_loaded = work[number + 1]
+            if number + 3 < len(work):
+                _, next_part, next_loaded = work[number + 3]
                 ahead.append(score(next_loaded, next_part))
             finish(index, part, loaded, ahead[number])
         return carry

time: 149 us -> 150 us (level)
  blocking collectives: 69.1 us -> 70.9 us
    all_to_all x1, blocking collectives: 30.5 us -> 32.4 us  [shards(): lax.all_to_all(head_out, 'seq', split_axis=0, concat_axis=0, tiled=True)]
where the time goes in v8:
time: 150 us
  blocking collectives  70.9 us (47%)
  waiting for transfers between devices  16.1 us (11%)
  between operations  14.9 us (10%)
  local copies, waits for them, and re-layouts  12.4 us (8%)
  matrix products  12.2 us (8%)
  starting transfers between devices  12.1 us (8%)
  Pallas kernels  10.4 us (7%)
    all_gather x1, blocking collectives, shards(): pooled = lax.all_gather(pooled, 'seq', axis=0, tiled=True)  38.5 us
    all_to_all x1, blocking collectives, shards(): lax.all_to_all(head_out, 'seq', split_axis=0, concat_axis=0, tiled=True)  32.4 us
    all_to_all x1, waiting for transfers between devices, spread_to(): lax.all_to_all(copies, axis, split_axis=0, concat_axis=0, tiled=True, axi...  11.6 us
    all_to_all x1, starting transfers between devices, spread_to(): lax.all_to_all(copies, axis, split_axis=0, concat_axis=0, tiled=True, axi...  10.1 us
    unnamed x31, local copies, waits for them, and re-layouts  6.15 us
    pallas_call x1, Pallas kernels, head_attention(): pl.pallas_call(head_kernel, out_shape=jax.ShapeDtypeStruct((seq_count, WI...  6.13 us
    dot_general x1, matrix products, convolve(): jnp.dot(other_columns, other.reshape(-1, channels), preferred_element_typ...  5.36 us
    dot_general x1, matrix products, convolve(): jnp.dot(own_columns, own.reshape(-1, channels), preferred_element_type=jn...  5.2 us
  transfers between devices with their start and end apart: 3, of which 2 were waited for; matrix products, arithmetic and copies ran while one was open for 13% of the time, Pallas kernels for 3%

profile of v8, /device:TPU:6, one launch (start us, length us, event | category | flops | bytes accessed | tf_op | source)
XLA Modules:
  0.0 149.7 jit_solution(2973778319922062478)
XLA Ops:
  6.6 0.7 all-gather.3.cloned.1.call-update
  7.3 2.5 %broadcast_in_dim.8 = bf16[16,144,512]{2,1,0:T(8,128)(2,1)} broadcast(bf16[144,512]{1,0:T(8,128)(2,1)} %param.11), dimensions={1,2} | broadcast | bytes 2506752 | tf_op jit(solution)/shard_map/encode/broadcast_in_dim | solution.py:204
  9.8 10.1 %all-to-all-start = ((bf16[16,144,512]{2,1,0:T(8,128)(2,1)}), bf16[16,144,512]{2,1,0:T(8,128)(2,1)}, u32[]{:S(2)}, u32[]{:S(2)}) async-start(bf16[16,144,512]{2,1,0:T(8,128)(2,1)} %broadcast_in_dim.8), calls=%async_computation | async-start | bytes 4718592 | tf_op jit(solution)/shard_map/encode/all_to_all | solution.py:205
  19.9 0.6 dynamic_slice.3
  21.9 0.2 copy.14
  22.1 0.2 copy.15
  22.2 0.8 copy.16
  23.1 1.6 %pad_slice_fusion = (bf16[16,8,8,512]{3,2,1,0:T(8,128)(2,1)S(1)}, bf16[16,8,8,512]{3,2,1,0:T(8,128)(2,1)S(1)}, bf16[16,8,8,512]{3,2,1,0:T(8,128)(2,1)S(1)}, bf16...) fusion(bf16[16,8,8,512]{3,2,1,0:T(8,128)(2,1)S(1)} %bitcast.32), kind=kLoop, calls=%fused_computation | loop fusion | bytes 9437184 | tf_op jit(solution)/shard_map/encode/slice | solution.py:265
  24.8 0.1 constant_dynamic-update-slice_fusion.7
  25.4 4.3 %encode.1 = (bf16[1024,2304]{1,0:T(8,128)(2,1)S(1)}, bf16[1024,2304]{1,0:T(8,128)(2,1)S(1)}) custom-call(s32[1]{0:T(128)} %bitcast.1.core, bf16[1024,4608]{1,0:T(8,128)(2,1)S(1)} %constant_dynamic-update-slice_fusion.columns_ref), custom_call_target="tpu_custom_call" | custom-call | bytes 18874368 | tf_op jit(solution)/shard_map/encode/pallas_call | solution.py:187
  29.7 2.2 %copy-done.2 = bf16[1024,2304]{1,0:T(8,128)(2,1)} copy-done((bf16[1024,2304]{1,0:T(8,128)(2,1)}, bf16[1024,2304]{1,0:T(8,128)(2,1)S(1)}, u32[]{:S(2)}) %copy-start.2) | copy-done | bytes 4718616
  31.9 2.2 %copy-done.3 = bf16[1024,2304]{1,0:T(8,128)(2,1)} copy-done((bf16[1024,2304]{1,0:T(8,128)(2,1)}, bf16[1024,2304]{1,0:T(8,128)(2,1)S(1)}, u32[]{:S(2)}) %copy-start.3) | copy-done | bytes 4718616
  34.1 1.4 concatenate.35.weight_ref
  35.5 0.7 pad_add_fusion.choice
  36.2 11.6 %all-to-all-done = bf16[16,144,512]{2,1,0:T(8,128)(2,1)} async-done(((bf16[16,144,512]{2,1,0:T(8,128)(2,1)}), bf16[16,144,512]{2,1,0:T(8,128)(2,1)}, u32[]{:S(2)}, u32[]{:S(2)}) %all-to-all-start) | async-done | bytes 2359328 | tf_op jit(solution)/shard_map/encode/all_to_all | solution.py:205
  47.8 1.9 %collective-permute-start = (bf16[16,144,512]{2,1,0:T(8,128)(2,1)}, bf16[16,144,512]{2,1,0:T(8,128)(2,1)S(1)}, u32[]{:S(2)}, u32[]{:S(2)}) collective-permute-start(bf16[16,144,512]{2,1,0:T(8,128)(2,1)} %all-to-all-done), channel_id=1, source_target_pairs={{0,16},{16,0},{32,48},{48,32},{64,80},{80,64},{96,112},{112,96},{1... | collective-permute-start | bytes 7077896 | tf_op jit(solution)/shard_map/encode/ppermute | solution.py:221
  49.7 5.2 %fusion.2 = f32[1024,512]{1,0:T(8,128)S(1)} fusion(bf16[1024,2304]{1,0:T(8,128)(2,1)} %copy-done.3, bf16[2304,512]{1,0:T(8,128)(2,1)} %bitcast.15), kind=kOutput, calls=%fused_computation.25 | convolution fusion | flops 2415919104 | bytes 9175040 | tf_op jit(solution)/shard_map/encode/dot_general | solution.py:222
  55.0 5.4 %bitcast_reduce_fusion = f32[16,512]{1,0:T(8,128)S(1)} fusion(bf16[1024,512]{1,0:T(8,128)(2,1)S(1)} %bitcast.34, f32[1024,512]{1,0:T(8,128)S(1)} %fusion.2, bf16[1024,2304]{1,0:T(8,128)(2,1)} %copy-done.2, bf16[2304,512]{1,0:T(8,128)(2,1)S(1)} %bitcast.44, f32[512]{0:T(512)S(1)} %copy-done.7, f32[512]{0:T(512)S(1)} %copy-done.8), kind=kOutput, calls=%fused_computation.8 | convolution fusion | flops 2419580928 | bytes 10260480 | tf_op jit(solution)/shard_map/encode/dot_general | solution.py:225
  60.4 38.5 %all_gather.7 = bf16[256,512]{1,0:T(8,128)(2,1)S(1)} all-gather(bf16[16,512]{1,0:T(8,128)(2,1)S(1)} %multiply_convert_fusion), channel_id=1, replica_groups=mesh['enc'=32,'seq'=16] {'seq'}, dimensions={0}, use_global_device_ids=true | all-gather | bytes 278528 | tf_op jit(solution)/shard_map/fresh/all_gather | solution.py:280
  98.8 0.4 convolution_convert_fusion.1.fresh_ref
  99.2 3.8 %all-gather.3.cloned.1.call-done = bf16[1,4096,768]{2,1,0:T(8,128)(2,1)} async-done(((bf16[1,256,768]{2,1,0:T(8,128)(2,1)}), bf16[1,4096,768]{2,1,0:T(8,128)(2,1)}) %all-gather.3.cloned.1.call-update) | async-done | bytes 6291472 | tf_op jit(solution)/shard_map/rows/all_gather | solution.py:250
  103.0 6.1 %head.1 = bf16[16,48,256]{2,1,0:T(8,128)(2,1)S(1)} custom-call(s32[256]{0:T(256)S(1)} %bitcast.30, s32[2]{0:T(128)S(1)} %pad_add_fusion.choice, bf16[4096,768]{1,0:T(8,128)(2,1)} %bitcast.31, bf16[256,768]{1,0:T(8,128)(2,1)S(1)} %convolution_convert_fusion.1.fresh_ref, bf16[768,256]{1,0:T(8,128)(2,1)S(1)} %concatenate.35.weight_ref), custom_call_target="tpu_custom_call" | custom-call | flops 1610612736 | tf_op jit(solution)/shard_map/head/pallas_call | solution.py:138
  109.2 32.4 %all_to_all.10 = bf16[16,48,256]{2,1,0:T(8,128)(2,1)S(1)} all-to-all(bf16[16,48,256]{2,1,0:T(8,128)(2,1)S(1)} %head.1), channel_id=1, replica_groups=mesh['enc'=32,'seq'=16] {'seq'}, dimensions={0} | all-to-all | bytes 786432 | tf_op jit(solution)/shard_map/out/all_to_all | solution.py:287
  141.6 1.3 fusion
  (32 shorter events, 0.7 us)
Async XLA Ops:
  6.5 135.1 %copy-start = (bf16[768,768]{1,0:T(8,128)(2,1)S(1)}, bf16[768,768]{1,0:T(8,128)(2,1)}, u32[]{:S(2)}) copy-start(bf16[768,768]{1,0:T(8,128)(2,1)} %param.18) | copy-start | bytes 3538948
  6.5 13.4 %copy-start.9 = (s32[16]{0:T(128)S(1)}, s32[16]{0:T(128)}, u32[]{:S(2)}) copy-start(s32[16]{0:T(128)} %param.19) | copy-start | bytes 196
  6.5 15.3 %copy-start.6 = (bf16[768,144]{0,1:T(8,128)(2,1)S(1)}, bf16[768,144]{0,1:T(8,128)(2,1)}, u32[]{:S(2)}) copy-start(bf16[768,144]{0,1:T(8,128)(2,1)} %param.17) | copy-start | bytes 663556
  6.5 16.5 %copy-start.4 = (bf16[1,16,8,8,512]{4,3,2,1,0:T(8,128)(2,1)S(1)}, bf16[1,16,8,8,512]{4,3,2,1,0:T(8,128)(2,1)}, u32[]{:S(2)}) copy-start(bf16[1,16,8,8,512]{4,3,2,1,0:T(8,128)(2,1)} %param.10) | copy-start | bytes 3145732
  6.5 96.5 %all-gather.3.cloned.1.call-start = ((), (), s32[]{:S(2)}) async-start(), calls=%async_computation.2 | async-start | bytes 6684672 | tf_op jit(solution)/shard_map/rows/all_gather | solution.py:250
  9.8 38.0 %all-to-all-start = ((bf16[16,144,512]{2,1,0:T(8,128)(2,1)}), bf16[16,144,512]{2,1,0:T(8,128)(2,1)}, u32[]{:S(2)}, u32[]{:S(2)}) async-start(bf16[16,144,512]{2,1,0:T(8,128)(2,1)} %broadcast_in_dim.8), calls=%async_computation | async-start | bytes 4718592 | tf_op jit(solution)/shard_map/encode/all_to_all | solution.py:205
  29.7 2.2 %copy-start.2 = (bf16[1024,2304]{1,0:T(8,128)(2,1)}, bf16[1024,2304]{1,0:T(8,128)(2,1)S(1)}, u32[]{:S(2)}) copy-start(bf16[1024,2304]{1,0:T(8,128)(2,1)S(1)} %get-tuple-element.17) | copy-start | bytes 14155780
  31.9 2.2 %copy-start.3 = (bf16[1024,2304]{1,0:T(8,128)(2,1)}, bf16[1024,2304]{1,0:T(8,128)(2,1)S(1)}, u32[]{:S(2)}) copy-start(bf16[1024,2304]{1,0:T(8,128)(2,1)S(1)} %get-tuple-element.15) | copy-start | bytes 14155780
  47.8 7.2 %collective-permute-start = (bf16[16,144,512]{2,1,0:T(8,128)(2,1)}, bf16[16,144,512]{2,1,0:T(8,128)(2,1)S(1)}, u32[]{:S(2)}, u32[]{:S(2)}) collective-permute-start(bf16[16,144,512]{2,1,0:T(8,128)(2,1)} %all-to-all-done), channel_id=1, source_target_pairs={{0,16},{16,0},{32,48},{48,32},{64,80},{80,64},{96,112},{112,96},{1... | collective-permute-start | bytes 7077896 | tf_op jit(solution)/shard_map/encode/ppermute | solution.py:221
  49.7 5.2 %copy-start.7 = (f32[512]{0:T(512)S(1)}, f32[512]{0:T(512)}, u32[]{:S(2)}) copy-start(f32[512]{0:T(512)} %param.13) | copy-start | bytes 6148
  49.7 5.2 %copy-start.8 = (f32[512]{0:T(512)S(1)}, f32[512]{0:T(512)}, u32[]{:S(2)}) copy-start(f32[512]{0:T(512)} %param.12) | copy-start | bytes 6148
  55.0 43.9 %copy-start.5 = (bf16[512,768]{1,0:T(8,128)(2,1)S(1)}, bf16[512,768]{1,0:T(8,128)(2,1)}, u32[]{:S(2)}) copy-start(bf16[512,768]{1,0:T(8,128)(2,1)} %param.14) | copy-start | bytes 2359300
  55.0 48.0 %copy-start.1 = (s32[1,256]{1,0:T(1,128)S(1)}, s32[1,256]{1,0:T(1,128)}, u32[]{:S(2)}) copy-start(s32[1,256]{1,0:T(1,128)} %param.15) | copy-start | bytes 3076
Sparse Core Ops, SparseCore 0:
  9.5 93.5 all-gather.2

commit v9 on v8

--- a/solution.py
+++ b/solution.py
@@ -13,11 +13,12 @@
 WIDTH = E // HEADS
 SEGMENT = 512
 STEP_ROWS = 1024
+SPARE = 8
 SCALE = WIDTH**-0.5 * math.log2(math.e)
 
 
 def attend(rate, offset, table, out_ref):
-    length = table.shape[1]
+    length = table.shape[1] - SPARE
     loc = out_ref.shape[2]
     spread = None
     if rate > 1:
@@ -147,7 +148,7 @@
         ],
         out_specs=pl.BlockSpec(memory_space=pltpu.VMEM),
         scratch_shapes=[
-            pltpu.VMEM((2, length, 128), jnp.float32),
+            pltpu.VMEM((2, length + SPARE, 128), jnp.float32),
             pltpu.VMEM((2, fresh.shape[0], 128), jnp.float32),
             pltpu.VMEM((chunks, STEP_ROWS, E), jnp.bfloat16),
             pltpu.SemaphoreType.DMA((chunks,)),

time: 150 us -> 150 us (level)
  no operation moved by 1% of the time
where the time goes in v9:
time: 150 us
  blocking collectives  71 us (47%)
  waiting for transfers between devices  16.1 us (11%)
  between operations  14.9 us (10%)
  local copies, waits for them, and re-layouts  12.4 us (8%)
  matrix products  12.2 us (8%)
  starting transfers between devices  12.1 us (8%)
  Pallas kernels  10.6 us (7%)
    all_gather x1, blocking collectives, shards(): pooled = lax.all_gather(pooled, 'seq', axis=0, tiled=True)  38.5 us
    all_to_all x1, blocking collectives, shards(): lax.all_to_all(head_out, 'seq', split_axis=0, concat_axis=0, tiled=True)  32.5 us
    all_to_all x1, waiting for transfers between devices, spread_to(): lax.all_to_all(copies, axis, split_axis=0, concat_axis=0, tiled=True, axi...  11.6 us
    all_to_all x1, starting transfers between devices, spread_to(): lax.all_to_all(copies, axis, split_axis=0, concat_axis=0, tiled=True, axi...  10.1 us
    pallas_call x1, Pallas kernels, head_attention(): pl.pallas_call(head_kernel, out_shape=jax.ShapeDtypeStruct((seq_count, WI...  6.32 us
    unnamed x31, local copies, waits for them, and re-layouts  6.15 us
    dot_general x1, matrix products, convolve(): jnp.dot(other_columns, other.reshape(-1, channels), preferred_element_typ...  5.36 us
    dot_general x1, matrix products, convolve(): jnp.dot(own_columns, own.reshape(-1, channels), preferred_element_type=jn...  5.2 us
  transfers between devices with their start and end apart: 3, of which 2 were waited for; matrix products, arithmetic and copies ran while one was open for 13% of the time, Pallas kernels for 3%

profile of v9, /device:TPU:6, one launch (start us, length us, event | category | flops | bytes accessed | tf_op | source)
XLA Modules:
  0.0 150.0 jit_solution(962748803843257885)
XLA Ops:
  6.6 0.7 all-gather.3.cloned.1.call-update
  7.3 2.5 %broadcast_in_dim.8 = bf16[16,144,512]{2,1,0:T(8,128)(2,1)} broadcast(bf16[144,512]{1,0:T(8,128)(2,1)} %param.11), dimensions={1,2} | broadcast | bytes 2506752 | tf_op jit(solution)/shard_map/encode/broadcast_in_dim | solution.py:205
  9.8 10.1 %all-to-all-start = ((bf16[16,144,512]{2,1,0:T(8,128)(2,1)}), bf16[16,144,512]{2,1,0:T(8,128)(2,1)}, u32[]{:S(2)}, u32[]{:S(2)}) async-start(bf16[16,144,512]{2,1,0:T(8,128)(2,1)} %broadcast_in_dim.8), calls=%async_computation | async-start | bytes 4718592 | tf_op jit(solution)/shard_map/encode/all_to_all | solution.py:206
  19.9 0.6 dynamic_slice.3
  21.9 0.2 copy.14
  22.1 0.2 copy.15
  22.2 0.8 copy.16
  23.1 1.6 %pad_slice_fusion = (bf16[16,8,8,512]{3,2,1,0:T(8,128)(2,1)S(1)}, bf16[16,8,8,512]{3,2,1,0:T(8,128)(2,1)S(1)}, bf16[16,8,8,512]{3,2,1,0:T(8,128)(2,1)S(1)}, bf16...) fusion(bf16[16,8,8,512]{3,2,1,0:T(8,128)(2,1)S(1)} %bitcast.32), kind=kLoop, calls=%fused_computation | loop fusion | bytes 9437184 | tf_op jit(solution)/shard_map/encode/slice | solution.py:266
  24.8 0.1 constant_dynamic-update-slice_fusion.7
  25.4 4.3 %encode.1 = (bf16[1024,2304]{1,0:T(8,128)(2,1)S(1)}, bf16[1024,2304]{1,0:T(8,128)(2,1)S(1)}) custom-call(s32[1]{0:T(128)} %bitcast.1.core, bf16[1024,4608]{1,0:T(8,128)(2,1)S(1)} %constant_dynamic-update-slice_fusion.columns_ref), custom_call_target="tpu_custom_call" | custom-call | bytes 18874368 | tf_op jit(solution)/shard_map/encode/pallas_call | solution.py:188
  29.7 2.2 %copy-done.2 = bf16[1024,2304]{1,0:T(8,128)(2,1)} copy-done((bf16[1024,2304]{1,0:T(8,128)(2,1)}, bf16[1024,2304]{1,0:T(8,128)(2,1)S(1)}, u32[]{:S(2)}) %copy-start.2) | copy-done | bytes 4718616
  31.9 2.2 %copy-done.3 = bf16[1024,2304]{1,0:T(8,128)(2,1)} copy-done((bf16[1024,2304]{1,0:T(8,128)(2,1)}, bf16[1024,2304]{1,0:T(8,128)(2,1)S(1)}, u32[]{:S(2)}) %copy-start.3) | copy-done | bytes 4718616
  34.1 1.4 concatenate.35.weight_ref
  35.5 0.7 pad_add_fusion.choice
  36.2 11.6 %all-to-all-done = bf16[16,144,512]{2,1,0:T(8,128)(2,1)} async-done(((bf16[16,144,512]{2,1,0:T(8,128)(2,1)}), bf16[16,144,512]{2,1,0:T(8,128)(2,1)}, u32[]{:S(2)}, u32[]{:S(2)}) %all-to-all-start) | async-done | bytes 2359328 | tf_op jit(solution)/shard_map/encode/all_to_all | solution.py:206
  47.8 1.9 %collective-permute-start = (bf16[16,144,512]{2,1,0:T(8,128)(2,1)}, bf16[16,144,512]{2,1,0:T(8,128)(2,1)S(1)}, u32[]{:S(2)}, u32[]{:S(2)}) collective-permute-start(bf16[16,144,512]{2,1,0:T(8,128)(2,1)} %all-to-all-done), channel_id=1, source_target_pairs={{0,16},{16,0},{32,48},{48,32},{64,80},{80,64},{96,112},{112,96},{1... | collective-permute-start | bytes 7077896 | tf_op jit(solution)/shard_map/encode/ppermute | solution.py:222
  49.7 5.2 %fusion.2 = f32[1024,512]{1,0:T(8,128)S(1)} fusion(bf16[1024,2304]{1,0:T(8,128)(2,1)} %copy-done.3, bf16[2304,512]{1,0:T(8,128)(2,1)} %bitcast.15), kind=kOutput, calls=%fused_computation.25 | convolution fusion | flops 2415919104 | bytes 9175040 | tf_op jit(solution)/shard_map/encode/dot_general | solution.py:223
  55.0 5.4 %bitcast_reduce_fusion = f32[16,512]{1,0:T(8,128)S(1)} fusion(bf16[1024,512]{1,0:T(8,128)(2,1)S(1)} %bitcast.34, f32[1024,512]{1,0:T(8,128)S(1)} %fusion.2, bf16[1024,2304]{1,0:T(8,128)(2,1)} %copy-done.2, bf16[2304,512]{1,0:T(8,128)(2,1)S(1)} %bitcast.44, f32[512]{0:T(512)S(1)} %copy-done.7, f32[512]{0:T(512)S(1)} %copy-done.8), kind=kOutput, calls=%fused_computation.8 | convolution fusion | flops 2419580928 | bytes 10260480 | tf_op jit(solution)/shard_map/encode/dot_general | solution.py:226
  60.4 38.5 %all_gather.7 = bf16[256,512]{1,0:T(8,128)(2,1)S(1)} all-gather(bf16[16,512]{1,0:T(8,128)(2,1)S(1)} %multiply_convert_fusion), channel_id=1, replica_groups=mesh['enc'=32,'seq'=16] {'seq'}, dimensions={0}, use_global_device_ids=true | all-gather | bytes 278528 | tf_op jit(solution)/shard_map/fresh/all_gather | solution.py:281
  98.8 0.4 convolution_convert_fusion.1.fresh_ref
  99.2 3.8 %all-gather.3.cloned.1.call-done = bf16[1,4096,768]{2,1,0:T(8,128)(2,1)} async-done(((bf16[1,256,768]{2,1,0:T(8,128)(2,1)}), bf16[1,4096,768]{2,1,0:T(8,128)(2,1)}) %all-gather.3.cloned.1.call-update) | async-done | bytes 6291472 | tf_op jit(solution)/shard_map/rows/all_gather | solution.py:251
  103.0 6.3 %head.1 = bf16[16,48,256]{2,1,0:T(8,128)(2,1)S(1)} custom-call(s32[256]{0:T(256)S(1)} %bitcast.30, s32[2]{0:T(128)S(1)} %pad_add_fusion.choice, bf16[4096,768]{1,0:T(8,128)(2,1)} %bitcast.31, bf16[256,768]{1,0:T(8,128)(2,1)S(1)} %convolution_convert_fusion.1.fresh_ref, bf16[768,256]{1,0:T(8,128)(2,1)S(1)} %concatenate.35.weight_ref), custom_call_target="tpu_custom_call" | custom-call | flops 1610612736 | tf_op jit(solution)/shard_map/head/pallas_call | solution.py:139
  109.4 32.5 %all_to_all.10 = bf16[16,48,256]{2,1,0:T(8,128)(2,1)S(1)} all-to-all(bf16[16,48,256]{2,1,0:T(8,128)(2,1)S(1)} %head.1), channel_id=1, replica_groups=mesh['enc'=32,'seq'=16] {'seq'}, dimensions={0} | all-to-all | bytes 786432 | tf_op jit(solution)/shard_map/out/all_to_all | solution.py:288
  141.9 1.3 fusion
  (32 shorter events, 0.7 us)
Async XLA Ops:
  6.5 135.4 %copy-start = (bf16[768,768]{1,0:T(8,128)(2,1)S(1)}, bf16[768,768]{1,0:T(8,128)(2,1)}, u32[]{:S(2)}) copy-start(bf16[768,768]{1,0:T(8,128)(2,1)} %param.18) | copy-start | bytes 3538948
  6.5 13.4 %copy-start.9 = (s32[16]{0:T(128)S(1)}, s32[16]{0:T(128)}, u32[]{:S(2)}) copy-start(s32[16]{0:T(128)} %param.19) | copy-start | bytes 196
  6.5 15.3 %copy-start.6 = (bf16[768,144]{0,1:T(8,128)(2,1)S(1)}, bf16[768,144]{0,1:T(8,128)(2,1)}, u32[]{:S(2)}) copy-start(bf16[768,144]{0,1:T(8,128)(2,1)} %param.17) | copy-start | bytes 663556
  6.5 16.5 %copy-start.4 = (bf16[1,16,8,8,512]{4,3,2,1,0:T(8,128)(2,1)S(1)}, bf16[1,16,8,8,512]{4,3,2,1,0:T(8,128)(2,1)}, u32[]{:S(2)}) copy-start(bf16[1,16,8,8,512]{4,3,2,1,0:T(8,128)(2,1)} %param.10) | copy-start | bytes 3145732
  6.5 96.5 %all-gather.3.cloned.1.call-start = ((), (), s32[]{:S(2)}) async-start(), calls=%async_computation.2 | async-start | bytes 6684672 | tf_op jit(solution)/shard_map/rows/all_gather | solution.py:251
  9.8 38.0 %all-to-all-start = ((bf16[16,144,512]{2,1,0:T(8,128)(2,1)}), bf16[16,144,512]{2,1,0:T(8,128)(2,1)}, u32[]{:S(2)}, u32[]{:S(2)}) async-start(bf16[16,144,512]{2,1,0:T(8,128)(2,1)} %broadcast_in_dim.8), calls=%async_computation | async-start | bytes 4718592 | tf_op jit(solution)/shard_map/encode/all_to_all | solution.py:206
  29.7 2.2 %copy-start.2 = (bf16[1024,2304]{1,0:T(8,128)(2,1)}, bf16[1024,2304]{1,0:T(8,128)(2,1)S(1)}, u32[]{:S(2)}) copy-start(bf16[1024,2304]{1,0:T(8,128)(2,1)S(1)} %get-tuple-element.17) | copy-start | bytes 14155780
  31.9 2.2 %copy-start.3 = (bf16[1024,2304]{1,0:T(8,128)(2,1)}, bf16[1024,2304]{1,0:T(8,128)(2,1)S(1)}, u32[]{:S(2)}) copy-start(bf16[1024,2304]{1,0:T(8,128)(2,1)S(1)} %get-tuple-element.15) | copy-start | bytes 14155780
  47.8 7.2 %collective-permute-start = (bf16[16,144,512]{2,1,0:T(8,128)(2,1)}, bf16[16,144,512]{2,1,0:T(8,128)(2,1)S(1)}, u32[]{:S(2)}, u32[]{:S(2)}) collective-permute-start(bf16[16,144,512]{2,1,0:T(8,128)(2,1)} %all-to-all-done), channel_id=1, source_target_pairs={{0,16},{16,0},{32,48},{48,32},{64,80},{80,64},{96,112},{112,96},{1... | collective-permute-start | bytes 7077896 | tf_op jit(solution)/shard_map/encode/ppermute | solution.py:222
  49.7 5.2 %copy-start.7 = (f32[512]{0:T(512)S(1)}, f32[512]{0:T(512)}, u32[]{:S(2)}) copy-start(f32[512]{0:T(512)} %param.13) | copy-start | bytes 6148
  49.7 5.2 %copy-start.8 = (f32[512]{0:T(512)S(1)}, f32[512]{0:T(512)}, u32[]{:S(2)}) copy-start(f32[512]{0:T(512)} %param.12) | copy-start | bytes 6148
  55.0 43.9 %copy-start.5 = (bf16[512,768]{1,0:T(8,128)(2,1)S(1)}, bf16[512,768]{1,0:T(8,128)(2,1)}, u32[]{:S(2)}) copy-start(bf16[512,768]{1,0:T(8,128)(2,1)} %param.14) | copy-start | bytes 2359300
  55.0 48.0 %copy-start.1 = (s32[1,256]{1,0:T(1,128)S(1)}, s32[1,256]{1,0:T(1,128)}, u32[]{:S(2)}) copy-start(s32[1,256]{1,0:T(1,128)} %param.15) | copy-start | bytes 3076
Sparse Core Ops, SparseCore 0:
  9.5 93.5 all-gather.2

commit v10 on v9

--- a/solution.py
+++ b/solution.py
@@ -91,7 +91,7 @@
 
 
 def head_kernel(
-    places, choice, rows_ref, fresh_ref, weight_ref, out_ref, table, fresh, held, arrived
+    places, choice, rows_ref, fresh, weight_ref, out_ref, table, held, arrived
 ):
     chunks = held.shape[0]
 
@@ -103,10 +103,6 @@
 
     for chunk in range(chunks):
         arrival(chunk).start()
-    made_fresh = jnp.dot(fresh_ref[...], weight_ref[...], preferred_element_type=jnp.float32)
-    made_fresh = made_fresh.astype(jnp.bfloat16).astype(jnp.float32)
-    fresh[0] = made_fresh[:, :128]
-    fresh[1] = made_fresh[:, 128:]
 
     def project(chunk, carry):
         arrival(chunk).wait()
@@ -149,7 +145,6 @@
         out_specs=pl.BlockSpec(memory_space=pltpu.VMEM),
         scratch_shapes=[
             pltpu.VMEM((2, length + SPARE, 128), jnp.float32),
-            pltpu.VMEM((2, fresh.shape[0], 128), jnp.float32),
             pltpu.VMEM((chunks, STEP_ROWS, E), jnp.bfloat16),
             pltpu.SemaphoreType.DMA((chunks,)),
         ],
@@ -282,6 +277,9 @@
         fresh = jnp.dot(pooled, tile_proj, preferred_element_type=jnp.float32).astype(jnp.bfloat16)
 
     with jax.named_scope("head"):
+        made = jnp.dot(fresh, head_weight, preferred_element_type=jnp.float32)
+        made = made.astype(jnp.bfloat16).astype(jnp.float32)
+        fresh = jnp.stack([made[:, :128], made[:, 128:]])
         head_out = head_attention(positions[0], choice, rows, fresh, head_weight, seq_count)
 
     with jax.named_scope("out"):

time: 150 us -> 150 us (level)
  waiting for transfers between devices: 16.1 us -> 14.5 us
    all_gather x1, waiting for transfers between devices: 3.81 us -> 2.26 us  [shards(): rows = lax.all_gather(slide_cache[0], 'seq', axis=0, tiled=True)]
    unnamed x31 -> x29, local copies, waits for them, and re-layouts: 6.15 us -> 6.14 us
  transfers between devices with their start and end apart: 3 -> 3, of which waited for: 2 -> 2; matrix products, arithmetic and copies ran while one was open for 13% -> 14% of each run, Pallas kernels for 3% -> 3%
where the time goes in v10:
time: 150 us
  blocking collectives  71.2 us (47%)
  between operations  14.9 us (10%)
  waiting for transfers between devices  14.5 us (10%)
  matrix products  13.5 us (9%)
  local copies, waits for them, and re-layouts  12.4 us (8%)
  starting transfers between devices  12.1 us (8%)
  Pallas kernels  10.4 us (7%)
    all_gather x1, blocking collectives, shards(): pooled = lax.all_gather(pooled, 'seq', axis=0, tiled=True)  38.7 us
    all_to_all x1, blocking collectives, shards(): lax.all_to_all(head_out, 'seq', split_axis=0, concat_axis=0, tiled=True)  32.5 us
    all_to_all x1, waiting for transfers between devices, spread_to(): lax.all_to_all(copies, axis, split_axis=0, concat_axis=0, tiled=True, axi...  11.6 us
    all_to_all x1, starting transfers between devices, spread_to(): lax.all_to_all(copies, axis, split_axis=0, concat_axis=0, tiled=True, axi...  10.1 us
    unnamed x29, local copies, waits for them, and re-layouts  6.14 us
    pallas_call x1, Pallas kernels, head_attention(): pl.pallas_call(head_kernel, out_shape=jax.ShapeDtypeStruct((seq_count, WI...  6.14 us
    dot_general x1, matrix products, convolve(): jnp.dot(other_columns, other.reshape(-1, channels), preferred_element_typ...  5.28 us
    dot_general x1, matrix products, convolve(): jnp.dot(own_columns, own.reshape(-1, channels), preferred_element_type=jn...  5.2 us
  transfers between devices with their start and end apart: 3, of which 2 were waited for; matrix products, arithmetic and copies ran while one was open for 14% of the time, Pallas kernels for 3%

profile of v10, /device:TPU:6, one launch (start us, length us, event | category | flops | bytes accessed | tf_op | source)
XLA Modules:
  0.0 149.8 jit_solution(1435803029848637484)
XLA Ops:
  6.6 0.7 all-gather.3.cloned.1.call-update
  7.3 2.5 %broadcast_in_dim.8 = bf16[16,144,512]{2,1,0:T(8,128)(2,1)} broadcast(bf16[144,512]{1,0:T(8,128)(2,1)} %param.11), dimensions={1,2} | broadcast | bytes 2506752 | tf_op jit(solution)/shard_map/encode/broadcast_in_dim | solution.py:200
  9.8 10.1 %all-to-all-start = ((bf16[16,144,512]{2,1,0:T(8,128)(2,1)}), bf16[16,144,512]{2,1,0:T(8,128)(2,1)}, u32[]{:S(2)}, u32[]{:S(2)}) async-start(bf16[16,144,512]{2,1,0:T(8,128)(2,1)} %broadcast_in_dim.8), calls=%async_computation | async-start | bytes 4718592 | tf_op jit(solution)/shard_map/encode/all_to_all | solution.py:201
  19.9 0.6 dynamic_slice.3
  21.9 0.2 copy.14
  22.1 0.2 copy.15
  22.2 0.8 copy.16
  23.1 1.6 %pad_slice_fusion = (bf16[16,8,8,512]{3,2,1,0:T(8,128)(2,1)S(1)}, bf16[16,8,8,512]{3,2,1,0:T(8,128)(2,1)S(1)}, bf16[16,8,8,512]{3,2,1,0:T(8,128)(2,1)S(1)}, bf16...) fusion(bf16[16,8,8,512]{3,2,1,0:T(8,128)(2,1)S(1)} %bitcast.37), kind=kLoop, calls=%fused_computation | loop fusion | bytes 9437184 | tf_op jit(solution)/shard_map/encode/slice | solution.py:261
  24.8 0.1 constant_dynamic-update-slice_fusion.7
  25.4 4.3 %encode.1 = (bf16[1024,2304]{1,0:T(8,128)(2,1)S(1)}, bf16[1024,2304]{1,0:T(8,128)(2,1)S(1)}) custom-call(s32[1]{0:T(128)} %bitcast.1.core, bf16[1024,4608]{1,0:T(8,128)(2,1)S(1)} %constant_dynamic-update-slice_fusion.columns_ref), custom_call_target="tpu_custom_call" | custom-call | bytes 18874368 | tf_op jit(solution)/shard_map/encode/pallas_call | solution.py:183
  29.7 2.2 %copy-done.2 = bf16[1024,2304]{1,0:T(8,128)(2,1)} copy-done((bf16[1024,2304]{1,0:T(8,128)(2,1)}, bf16[1024,2304]{1,0:T(8,128)(2,1)S(1)}, u32[]{:S(2)}) %copy-start.2) | copy-done | bytes 4718616
  31.9 2.2 %copy-done.3 = bf16[1024,2304]{1,0:T(8,128)(2,1)} copy-done((bf16[1024,2304]{1,0:T(8,128)(2,1)}, bf16[1024,2304]{1,0:T(8,128)(2,1)S(1)}, u32[]{:S(2)}) %copy-start.3) | copy-done | bytes 4718616
  34.1 1.4 concatenate.35.weight_ref
  35.5 0.7 pad_add_fusion.choice
  36.2 11.6 %all-to-all-done = bf16[16,144,512]{2,1,0:T(8,128)(2,1)} async-done(((bf16[16,144,512]{2,1,0:T(8,128)(2,1)}), bf16[16,144,512]{2,1,0:T(8,128)(2,1)}, u32[]{:S(2)}, u32[]{:S(2)}) %all-to-all-start) | async-done | bytes 2359328 | tf_op jit(solution)/shard_map/encode/all_to_all | solution.py:201
  47.8 1.9 %collective-permute-start = (bf16[16,144,512]{2,1,0:T(8,128)(2,1)}, bf16[16,144,512]{2,1,0:T(8,128)(2,1)S(1)}, u32[]{:S(2)}, u32[]{:S(2)}) collective-permute-start(bf16[16,144,512]{2,1,0:T(8,128)(2,1)} %all-to-all-done), channel_id=1, source_target_pairs={{0,16},{16,0},{32,48},{48,32},{64,80},{80,64},{96,112},{112,96},{1... | collective-permute-start | bytes 7077896 | tf_op jit(solution)/shard_map/encode/ppermute | solution.py:217
  49.7 5.2 %fusion.5 = f32[1024,512]{1,0:T(8,128)S(1)} fusion(bf16[1024,2304]{1,0:T(8,128)(2,1)} %copy-done.3, bf16[2304,512]{1,0:T(8,128)(2,1)} %bitcast.15), kind=kOutput, calls=%fused_computation.31 | convolution fusion | flops 2415919104 | bytes 9175040 | tf_op jit(solution)/shard_map/encode/dot_general | solution.py:218
  55.0 5.3 %bitcast_reduce_fusion = f32[16,512]{1,0:T(8,128)S(1)} fusion(bf16[1024,512]{1,0:T(8,128)(2,1)S(1)} %bitcast.39, f32[1024,512]{1,0:T(8,128)S(1)} %fusion.5, bf16[1024,2304]{1,0:T(8,128)(2,1)} %copy-done.2, bf16[2304,512]{1,0:T(8,128)(2,1)S(1)} %bitcast.49, f32[512]{0:T(512)S(1)} %copy-done.6, f32[512]{0:T(512)S(1)} %copy-done.7), kind=kOutput, calls=%fused_computation.8 | convolution fusion | flops 2419580928 | bytes 10260480 | tf_op jit(solution)/shard_map/encode/dot_general | solution.py:221
  60.3 38.7 %all_gather.7 = bf16[256,512]{1,0:T(8,128)(2,1)S(1)} all-gather(bf16[16,512]{1,0:T(8,128)(2,1)S(1)} %multiply_convert_fusion), channel_id=1, replica_groups=mesh['enc'=32,'seq'=16] {'seq'}, dimensions={0}, use_global_device_ids=true | all-gather | bytes 278528 | tf_op jit(solution)/shard_map/fresh/all_gather | solution.py:276
  99.0 1.7 %fusion.3 = f32[256,256]{1,0:T(8,128)S(1)} fusion(bf16[768,256]{1,0:T(8,128)(2,1)S(1)} %concatenate.35.weight_ref, bf16[256,512]{1,0:T(8,128)(2,1)S(1)} %all_gather.7, bf16[512,768]{1,0:T(8,128)(2,1)} %param.14), kind=kOutput, calls=%fused_computation.15 | convolution fusion | flops 302317568 | bytes 1703936 | tf_op jit(solution)/shard_map/head/dot_general | solution.py:280
  100.8 2.3 %all-gather.3.cloned.1.call-done = bf16[1,4096,768]{2,1,0:T(8,128)(2,1)} async-done(((bf16[1,256,768]{2,1,0:T(8,128)(2,1)}), bf16[1,4096,768]{2,1,0:T(8,128)(2,1)}) %all-gather.3.cloned.1.call-update) | async-done | bytes 6291472 | tf_op jit(solution)/shard_map/rows/all_gather | solution.py:246
  103.1 6.1 %head.1 = bf16[16,48,256]{2,1,0:T(8,128)(2,1)S(1)} custom-call(s32[256]{0:T(256)S(1)} %bitcast.35, s32[2]{0:T(128)S(1)} %pad_add_fusion.choice, bf16[4096,768]{1,0:T(8,128)(2,1)} %bitcast.36, f32[2,256,128]{2,1,0:T(8,128)S(1)} %pad_maximum_fusion.fresh, bf16[768,256]{1,0:T(8,128)(2,1)S(1)} %concatenate.35.weight_ref), custom_call_target="tpu_custom_call" | custom-call | flops 1610612736 | tf_op jit(solution)/shard_map/head/pallas_call | solution.py:135
  109.2 32.5 %all_to_all.10 = bf16[16,48,256]{2,1,0:T(8,128)(2,1)S(1)} all-to-all(bf16[16,48,256]{2,1,0:T(8,128)(2,1)S(1)} %head.1), channel_id=1, replica_groups=mesh['enc'=32,'seq'=16] {'seq'}, dimensions={0} | all-to-all | bytes 786432 | tf_op jit(solution)/shard_map/out/all_to_all | solution.py:286
  141.7 1.3 fusion
  (32 shorter events, 0.8 us)
Async XLA Ops:
  6.5 135.2 %copy-start = (bf16[768,768]{1,0:T(8,128)(2,1)S(1)}, bf16[768,768]{1,0:T(8,128)(2,1)}, u32[]{:S(2)}) copy-start(bf16[768,768]{1,0:T(8,128)(2,1)} %param.18) | copy-start | bytes 3538948
  6.5 13.4 %copy-start.8 = (s32[16]{0:T(128)S(1)}, s32[16]{0:T(128)}, u32[]{:S(2)}) copy-start(s32[16]{0:T(128)} %param.19) | copy-start | bytes 196
  6.5 15.3 %copy-start.5 = (bf16[768,144]{0,1:T(8,128)(2,1)S(1)}, bf16[768,144]{0,1:T(8,128)(2,1)}, u32[]{:S(2)}) copy-start(bf16[768,144]{0,1:T(8,128)(2,1)} %param.17) | copy-start | bytes 663556
  6.5 16.5 %copy-start.4 = (bf16[1,16,8,8,512]{4,3,2,1,0:T(8,128)(2,1)S(1)}, bf16[1,16,8,8,512]{4,3,2,1,0:T(8,128)(2,1)}, u32[]{:S(2)}) copy-start(bf16[1,16,8,8,512]{4,3,2,1,0:T(8,128)(2,1)} %param.10) | copy-start | bytes 3145732
  6.5 96.5 %all-gather.3.cloned.1.call-start = ((), (), s32[]{:S(2)}) async-start(), calls=%async_computation.2 | async-start | bytes 6684672 | tf_op jit(solution)/shard_map/rows/all_gather | solution.py:246
  9.8 38.0 %all-to-all-start = ((bf16[16,144,512]{2,1,0:T(8,128)(2,1)}), bf16[16,144,512]{2,1,0:T(8,128)(2,1)}, u32[]{:S(2)}, u32[]{:S(2)}) async-start(bf16[16,144,512]{2,1,0:T(8,128)(2,1)} %broadcast_in_dim.8), calls=%async_computation | async-start | bytes 4718592 | tf_op jit(solution)/shard_map/encode/all_to_all | solution.py:201
  29.7 2.2 %copy-start.2 = (bf16[1024,2304]{1,0:T(8,128)(2,1)}, bf16[1024,2304]{1,0:T(8,128)(2,1)S(1)}, u32[]{:S(2)}) copy-start(bf16[1024,2304]{1,0:T(8,128)(2,1)S(1)} %get-tuple-element.17) | copy-start | bytes 14155780
  31.9 2.2 %copy-start.3 = (bf16[1024,2304]{1,0:T(8,128)(2,1)}, bf16[1024,2304]{1,0:T(8,128)(2,1)S(1)}, u32[]{:S(2)}) copy-start(bf16[1024,2304]{1,0:T(8,128)(2,1)S(1)} %get-tuple-element.15) | copy-start | bytes 14155780
  47.8 7.2 %collective-permute-start = (bf16[16,144,512]{2,1,0:T(8,128)(2,1)}, bf16[16,144,512]{2,1,0:T(8,128)(2,1)S(1)}, u32[]{:S(2)}, u32[]{:S(2)}) collective-permute-start(bf16[16,144,512]{2,1,0:T(8,128)(2,1)} %all-to-all-done), channel_id=1, source_target_pairs={{0,16},{16,0},{32,48},{48,32},{64,80},{80,64},{96,112},{112,96},{1... | collective-permute-start | bytes 7077896 | tf_op jit(solution)/shard_map/encode/ppermute | solution.py:217
  49.7 5.2 %copy-start.6 = (f32[512]{0:T(512)S(1)}, f32[512]{0:T(512)}, u32[]{:S(2)}) copy-start(f32[512]{0:T(512)} %param.13) | copy-start | bytes 6148
  49.7 5.2 %copy-start.7 = (f32[512]{0:T(512)S(1)}, f32[512]{0:T(512)}, u32[]{:S(2)}) copy-start(f32[512]{0:T(512)} %param.12) | copy-start | bytes 6148
  55.0 48.1 %copy-start.1 = (s32[1,256]{1,0:T(1,128)S(1)}, s32[1,256]{1,0:T(1,128)}, u32[]{:S(2)}) copy-start(s32[1,256]{1,0:T(1,128)} %param.15) | copy-start | bytes 3076
Sparse Core Ops, SparseCore 0:
  9.5 93.5 all-gather.2
